TPU v7x, 256 devices: a whole 4x4x8 slice. The times are simulated.
256 devices in a mesh: pat: 16 (over z, core), seq: 16 (over x, y).
Axes of the slice: x: 4, y: 4, z: 8, core: 2. Of those that a mesh axis runs over, the one named last changes fastest.
Arguments:
- query_matrix: bfloat16 [65536, 1024], P(('pat', 'seq')), parts along dimension 0, may hold values from -24 to 24
- key_rows: bfloat16 [65536, 1024], P(('pat', 'seq')), parts along dimension 0, may hold values from -24 to 24
- value_rows: bfloat16 [65536, 1024], P(('pat', 'seq')), parts along dimension 0, may hold values from -6 to 6
- output_gradient_rows: bfloat16 [65536, 1024], P(('pat', 'seq')), parts along dimension 0, may hold values from -6 to 6
- far_pick: int32 [256, 15], P(('pat', 'seq')), parts along dimension 0, may hold values from 0 to 1
- far_count: int32 [16], P('seq'), may hold values from 1 to 15, as said below
- global_ids: int32 [32], P('pat'), parts along dimension 0, may hold values from 0 to 31
Outputs:
- d_query: bfloat16 [65536, 1024], P(('pat', 'seq')), parts along dimension 0
- d_key: bfloat16 [65536, 1024], P(('pat', 'seq')), parts along dimension 0
- d_value: bfloat16 [65536, 1024], P(('pat', 'seq')), parts along dimension 0
There are 16 independent parts, one for each index of `pat`. A program takes and returns all parts, laid end to end along the dimension named above; an argument that names none is the same for every part. Nothing has to cross between parts.
Inputs may be any that keep to these rules, and one draw needn't show every extreme that they name: `far_count`: on exactly one shard the count is 15; every other shard uses at least one and at most the larger of 2 and a quarter of 15, rounded up.
All inputs are finite; a program needn't handle non-finite values.
Results may differ from a plain program's by a relative error of at most 0.015.
Values may be sent and summed in bfloat16 or wider, within the bound.
No kernel may reach another device: no remote copies, remote signals or barrier semaphores. Data moves between devices by JAX's collectives and lax.ppermute only.
A program may use at most 128 MiB of HBM per device.

v0:
```python
import jax
import jax.numpy as jnp
from jax import lax
from jax.sharding import PartitionSpec as P

HEADS = 8
HD = 128
BLK = 128
GLOB = 2


def extended_2(array, sides, width):
    for axis, dim in sides:
        size, length = (lax.axis_size(axis), array.shape[dim])
        up = [(i, (i + 1) % size) for i in range(size - 1)]
        down = [(j, i) for i, j in up]
        last = lax.slice_in_dim(array, length - width, length, axis=dim)
        initial = lax.slice_in_dim(array, 0, width, axis=dim)
        before = lax.ppermute(last, axis, up)
        after = lax.ppermute(initial, axis, down)
        array = jnp.concatenate([before, array, after], axis=dim)
    return array


def from_root(array, axis, root):
    mine = lax.axis_index(axis) == root
    return lax.psum(jnp.where(mine, array, jnp.zeros_like(array)), axis)


def score_block(queries, keys_in, key_valid, logit_scale):
    scores = (
        jnp.einsum("qhd,khd->hqk", queries, keys_in, preferred_element_type=jnp.float32)
        * logit_scale
    )
    return jnp.where(key_valid[None, None, :], scores, -jnp.inf)


def block_stats(queries, keys_in, key_valid, logit_scale):
    masked = score_block(queries, keys_in, key_valid, logit_scale)
    peak = jnp.max(masked, axis=-1)
    total = jnp.sum(jnp.exp(masked - peak[..., None]), axis=-1)
    return (peak, total)


def merge_stats(peak_first, total_first, peak_second, total_second):
    peak = jnp.maximum(peak_first, peak_second)
    return (
        peak,
        total_first * jnp.exp(peak_first - peak) + total_second * jnp.exp(peak_second - peak),
    )


def block_delta(queries, grads_in, keys_in, values_in, key_valid, log_total, logit_scale):
    weights = jnp.exp(score_block(queries, keys_in, key_valid, logit_scale) - log_total[..., None])
    weight_grads = jnp.einsum(
        "qhd,khd->hqk", grads_in, values_in, preferred_element_type=jnp.float32
    )
    return jnp.sum(weights * weight_grads, axis=-1)


def block_grads(
    queries, grads_in, keys_in, values_in, key_valid, log_total, row_delta, logit_scale
):
    weights = jnp.exp(score_block(queries, keys_in, key_valid, logit_scale) - log_total[..., None])
    rounded = weights.astype(jnp.bfloat16)
    weight_grads = jnp.einsum(
        "qhd,khd->hqk", grads_in, values_in, preferred_element_type=jnp.float32
    )
    score_grads = (weights * (weight_grads - row_delta[..., None]) * logit_scale).astype(
        jnp.bfloat16
    )
    grad_query = jnp.einsum(
        "hqk,khd->qhd", score_grads, keys_in, preferred_element_type=jnp.float32
    )
    grad_key = jnp.einsum("hqk,qhd->khd", score_grads, queries, preferred_element_type=jnp.float32)
    grad_value = jnp.einsum("hqk,qhd->khd", rounded, grads_in, preferred_element_type=jnp.float32)
    key_count = keys_in.shape[0]
    return (
        grad_query,
        jnp.concatenate(
            [grad_key.reshape(key_count, -1), grad_value.reshape(key_count, -1)], axis=-1
        ),
    )


def to_rows(stats):
    return jnp.transpose(stats, (1, 0, 2)).reshape(stats.shape[1], -1)


def to_blocks(stats, blocks):
    return jnp.transpose(stats.reshape(stats.shape[0], blocks, -1), (1, 0, 2))


def body(query_matrix, key_rows, value_rows, output_gradient_rows, far_pick, far_count, global_ids):
    shard_count = lax.axis_size("seq")
    shard_id = lax.axis_index("seq")
    row_count, width = query_matrix.shape
    blocks = row_count // BLK
    block_total = blocks * shard_count
    slot_total = far_pick.shape[1]
    logit_scale = HD ** (-0.5)
    paired = jnp.concatenate([key_rows, value_rows], axis=1)
    all_pick, all_count = (
        lax.all_gather(far_pick, "seq", axis=0, tiled=True),
        lax.all_gather(far_count, "seq", axis=0, tiled=True),
    )
    my_pick = far_pick[0]
    my_count = far_count[0]
    extended = extended_2(paired, (("seq", 0),), BLK)
    global_list = []
    for slot in range(GLOB):
        global_block = global_ids[slot]
        holder = global_block // blocks
        block_rows = lax.dynamic_slice_in_dim(paired, global_block % blocks * BLK, BLK, 0)
        global_list.append(from_root(block_rows, "seq", holder))
    global_pairs = jnp.concatenate(global_list, axis=0)
    requesters = jnp.arange(shard_count, dtype=jnp.int32)
    slot_of = (shard_id - requesters - 1) % shard_count
    slot_clip = jnp.minimum(slot_of, slot_total - 1)
    wanted = jnp.take_along_axis(all_pick, slot_clip[:, None], axis=1)[:, 0]
    whole = lax.all_gather(paired, "seq", axis=0, tiled=True)

    def far_pair(step):
        source = (shard_id + 1 + step) % shard_count
        start = (source * blocks + my_pick[step]) * BLK
        return lax.dynamic_slice_in_dim(whole, start, BLK, 0)

    def heads_of(pairs):
        lead = pairs.shape[:-1]
        return (
            pairs[..., :width].reshape(lead + (HEADS, HD)),
            pairs[..., width:].reshape(lead + (HEADS, HD)),
        )

    queries = query_matrix.reshape(row_count, HEADS, HD)
    grads_in = output_gradient_rows.reshape(row_count, HEADS, HD)
    query_blocks = queries.reshape(blocks, BLK, HEADS, HD)
    grad_blocks = grads_in.reshape(blocks, BLK, HEADS, HD)
    ext_blocks = extended.reshape(blocks + 2, BLK, 2 * width)
    window_pairs = jnp.concatenate(
        [ext_blocks[offset : offset + blocks] for offset in range(3)], axis=1
    )
    window_ids = (
        shard_id * blocks
        + jnp.arange(blocks, dtype=jnp.int32)[:, None]
        - 1
        + jnp.arange(3, dtype=jnp.int32)[None, :]
    )
    window_valid = jnp.repeat((window_ids >= 0) & (window_ids < block_total), BLK, axis=1)
    window_keys, window_values = heads_of(window_pairs)
    global_keys, global_values = heads_of(global_pairs)
    global_valid = jnp.ones((GLOB * BLK,), jnp.bool_)
    far_valid = jnp.ones((BLK,), jnp.bool_)
    window_peak, window_total = jax.vmap(block_stats, in_axes=(0, 0, 0, None))(
        query_blocks, window_keys, window_valid, logit_scale
    )
    global_peak, global_total = block_stats(queries, global_keys, global_valid, logit_scale)
    run_peak, run_total = merge_stats(
        to_rows(window_peak), to_rows(window_total), global_peak, global_total
    )

    def far_stats(step, state):
        far_keys, unused_values = heads_of(far_pair(step))
        peak_next, total_next = block_stats(queries, far_keys, far_valid, logit_scale)
        return merge_stats(state[0], state[1], peak_next, total_next)

    run_peak, run_total = lax.fori_loop(0, my_count, far_stats, (run_peak, run_total))
    log_total = run_peak + jnp.log(run_total)
    window_lse = to_blocks(log_total, blocks)
    row_delta = to_rows(
        jax.vmap(block_delta, in_axes=(0, 0, 0, 0, 0, 0, None))(
            query_blocks,
            grad_blocks,
            window_keys,
            window_values,
            window_valid,
            window_lse,
            logit_scale,
        )
    )
    row_delta = row_delta + block_delta(
        queries, grads_in, global_keys, global_values, global_valid, log_total, logit_scale
    )

    def far_delta(step, total_delta):
        far_keys, far_values = heads_of(far_pair(step))
        return total_delta + block_delta(
            queries, grads_in, far_keys, far_values, far_valid, log_total, logit_scale
        )

    row_delta = lax.fori_loop(0, my_count, far_delta, row_delta)
    window_delta = to_blocks(row_delta, blocks)
    window_grad_query, window_grad_pairs = jax.vmap(
        block_grads, in_axes=(0, 0, 0, 0, 0, 0, 0, None)
    )(
        query_blocks,
        grad_blocks,
        window_keys,
        window_values,
        window_valid,
        window_lse,
        window_delta,
        logit_scale,
    )
    global_grad_query, global_grad_pairs = block_grads(
        queries,
        grads_in,
        global_keys,
        global_values,
        global_valid,
        log_total,
        row_delta,
        logit_scale,
    )

    def far_grads_step(step, state):
        source = (shard_id + 1 + step) % shard_count
        far_keys, far_values = heads_of(far_pair(step))
        grad_query, grad_pairs = block_grads(
            queries, grads_in, far_keys, far_values, far_valid, log_total, row_delta, logit_scale
        )
        updated = lax.dynamic_update_index_in_dim(
            state[1], grad_pairs.astype(jnp.bfloat16), source, 0
        )
        return (state[0] + grad_query, updated)

    far_init = (
        jnp.zeros((row_count, HEADS, HD), jnp.float32),
        jnp.zeros((shard_count, BLK, 2 * width), jnp.bfloat16),
    )
    far_grad_query, outgoing_grads = lax.fori_loop(0, my_count, far_grads_step, far_init)
    distant_return = lax.all_to_all(outgoing_grads, "seq", split_axis=0, concat_axis=0, tiled=True)
    sender_active = (requesters != shard_id) & (slot_of < all_count)
    block_selector = (
        sender_active[:, None] & (wanted[:, None] == jnp.arange(blocks, dtype=jnp.int32)[None, :])
    ).astype(jnp.bfloat16)
    distant_local = jnp.einsum(
        "hp,hci->pci", block_selector, distant_return, preferred_element_type=jnp.float32
    )
    ext_grads = jnp.zeros((blocks + 2, BLK, 2 * width), jnp.float32)
    pieces = window_grad_pairs.reshape(blocks, 3, BLK, 2 * width)
    for offset in range(3):
        ext_grads = ext_grads.at[offset : offset + blocks].add(pieces[:, offset])
    rims = jnp.concatenate([ext_grads[0], ext_grads[blocks + 1]], axis=0)
    returned = extended_2(rims.astype(jnp.bfloat16), (("seq", 0),), BLK).astype(rims.dtype)
    global_sum = lax.psum(
        global_grad_pairs.reshape(GLOB, BLK, 2 * width).astype(jnp.bfloat16), "seq"
    ).astype(jnp.float32)
    holder_match = (global_ids[:, None] // blocks == shard_id) & (
        global_ids[:, None] % blocks == jnp.arange(blocks, dtype=jnp.int32)[None, :]
    )
    global_own = jnp.sum(
        jnp.where(holder_match[:, :, None, None], global_sum[:, None], 0.0), axis=0
    )
    local_gradients = ext_grads[1 : blocks + 1] + distant_local + global_own
    local_gradients = local_gradients.at[0].add(returned[:BLK])
    local_gradients = local_gradients.at[blocks - 1].add(returned[3 * BLK :])
    own_flat = local_gradients.reshape(row_count, 2 * width)
    query_total = (
        window_grad_query.reshape(row_count, HEADS, HD) + global_grad_query + far_grad_query
    )
    d_query = query_total.reshape(row_count, width).astype(jnp.bfloat16)
    return (
        d_query,
        own_flat[:, :width].astype(jnp.bfloat16),
        own_flat[:, width:].astype(jnp.bfloat16),
    )


def solution(mesh):
    in_specs = (
        P(("pat", "seq"), None),
        P(("pat", "seq"), None),
        P(("pat", "seq"), None),
        P(("pat", "seq"), None),
        P(("pat", "seq"), None),
        P("seq"),
        P("pat"),
    )
    out_specs = (P(("pat", "seq"), None), P(("pat", "seq"), None), P(("pat", "seq"), None))
    return jax.shard_map(body, mesh=mesh, in_specs=in_specs, out_specs=out_specs, check_vma=False)
```

profile of v0, /device:TPU:1, one launch (start us, length us, event | category | flops | bytes accessed | tf_op | source)
XLA Modules:
  0.0 822.8 jit_solution(3598413854668540122)
XLA Ops:
  18.2 4.9 collective-permute-start
  29.4 4.5 collective-permute-done
  33.9 5.8 collective-permute-done.1
  53.4 66.1 %all-reduce.8.cloned.1.call-done = (bf16[128,2048]{1,0:T(8,128)(2,1)}, bf16[128,2048]{1,0:T(8,128)(2,1)}) async-done(((bf16[128,2048]{1,0:T(8,128)(2,1)}, bf16[128,2048]{1,0:T(8,128)(2,1)}), (bf16[128,2048]{1,0:T(8,128)(2,1)}, bf16[128,2048]{1,0:T(8,128)(2,1)})) %all-reduce.8.cloned.1.call-update) | async-done | bytes 1048592 | tf_op jit(solution)/shard_map/psum | solution.py:27
  127.3 111.6 %all-gather.3.cloned.1.call-done = bf16[4096,2048]{1,0:T(8,128)(2,1)} async-done(((bf16[256,2048]{1,0:T(8,128)(2,1)}), bf16[4096,2048]{1,0:T(8,128)(2,1)}) %all-gather.3.cloned.1.call-update) | async-done | bytes 16777232 | tf_op jit(solution)/shard_map/all_gather | solution.py:121
  238.9 21.0 %copy.246 = bf16[4096,2048]{0,1:T(8,128)(2,1)} copy(bf16[4096,2048]{1,0:T(8,128)(2,1)} %all-gather.3.cloned.1.call-done) | data formatting | bytes 33554432 | tf_op jit(solution)/shard_map/while | solution.py:167
  259.9 14.4 %while.45 = (s32[]{:T(128)}, f32[8,256]{1,0:T(8,128)S(1)}, f32[8,256]{1,0:T(8,128)S(1)}, s32[]{:T(128)}, s32[]{:T(128)}, /*index=5*/s32[15]{0:T(128)S(1)}, bf16[...) while((s32[]{:T(128)}, f32[8,256]{1,0:T(8,128)S(1)}, ...), condition=%wide.region_9.10_spmd, body=%wide.region_6.9_spmd.sunk | while | flops 68165656 | bytes 3481990 | solution.py:167
  274.4 3.6 fusion.24
  278.0 3.0 fusion.13
  281.0 15.7 %while.46 = (s32[]{:T(128)}, f32[8,256]{1,0:T(8,128)S(1)}, s32[]{:T(128)}, s32[]{:T(128)}, s32[15]{0:T(128)S(1)}, /*index=5*/bf16[4096,2048]{0,1:T(8,128)(2,1)},...) while((s32[]{:T(128)}, f32[8,256]{1,0:T(8,128)S(1)}, ...), condition=%wide.region_14.15_spmd, body=%wide.region_12.14_spmd.sunk | while | flops 135266336 | bytes 4759974 | solution.py:191
  297.7 4.3 broadcast_in_dim.113.clone
  302.0 32.6 %while.47 = (s32[]{:T(128)}, f32[256,8,128]{0,2,1:T(8,128)}, bf16[16,128,2048]{2,1,0:T(8,128)(2,1)}, s32[]{:T(128)}, s32[]{:T(128)}, /*index=5*/s32[15]{0:T(128)...) while((s32[]{:T(128)}, f32[256,8,128]{0,2,1:T(8,128)}, ...), condition=%wide.region_16.17_spmd, body=%wide.region_15.16_spmd.sunk | while | flops 338952224 | bytes 14434780 | solution.py:231
  334.6 170.9 %all-to-all-start = ((bf16[16,128,2048]{2,1,0:T(8,128)(2,1)}), bf16[16,128,2048]{2,1,0:T(8,128)(2,1)}, u32[]{:S(2)}, u32[]{:S(2)}) async-start(bf16[16,128,2048]{2,1,0:T(8,128)(2,1)} %get-tuple-element.438), calls=%async_computation | async-start | bytes 16777216 | tf_op jit(solution)/shard_map/all_to_all | solution.py:232
  505.6 147.8 %all-reduce.1 = s32[16]{0:T(128)S(1)} all-reduce(s32[16]{0:T(128)S(1)} %dynamic-update-slice.15), channel_id=1, replica_groups=mesh['pat'=16,'seq'=16] {'seq'}, use_global_device_ids=true, to_apply=%add.1 | all-reduce | flops 16 | bytes 128
  653.3 17.2 %all-gather = s32[16,1,15]{2,1,0:T(1,128)S(1)} all-gather(s32[1,1,15]{2,1,0:T(1,128)S(1)} %bitcast.316), channel_id=1, replica_groups=mesh['pat'=16,'seq'=16] {'seq'}, dimensions={0}, use_global_device_ids=true | all-gather | bytes 1020 | tf_op jit(solution)/shard_map/all_gather | solution.py:104
  673.2 3.0 convolution_bitcast_fusion.1
  676.2 3.5 copy.267
  679.7 4.7 concatenate.73
  689.2 4.0 fusion.16
  693.8 3.5 copy.265
  697.3 4.5 concatenate.72
  717.8 5.1 collective-permute-start.2
  725.4 70.4 %all-reduce.6.cloned.1.call-done = bf16[2,128,2048]{2,1,0:T(8,128)(2,1)} async-done(((bf16[2,128,2048]{2,1,0:T(8,128)(2,1)}), bf16[2,128,2048]{2,1,0:T(8,128)(2,1)}) %all-reduce.6.cloned.1.call-update) | async-done | bytes 1048592 | tf_op jit(solution)/shard_map/psum | solution.py:246
  797.7 12.9 %fusion.11 = f32[2,128,2048]{2,0,1:T(2,128)S(1)} fusion(bf16[16,128,2048]{2,1,0:T(8,128)(2,1)} %all-to-all-done, pred[16]{0:T(512)(128)(4,1)S(1)} %compare_and_fusion.1, s32[16]{0:T(128)S(1)} %and_select_fusion.3), kind=kOutput, calls=%fused_computation.27 | convolution fusion | flops 16777280 | bytes 10485840 | tf_op jit(solution)/shard_map/hp,hci->pci/dot_general | solution.py:237
  (218 shorter events, 111.5 us)
Async XLA Ops:
  7.2 112.2 %all-reduce.8.cloned.1.call-start = ((), (), s32[]{:S(2)}) async-start(), calls=%async_computation.3 | async-start | bytes 2097152 | tf_op jit(solution)/shard_map/psum | solution.py:27
  16.0 9.2 %copy-start.20 = (bf16[256,1024]{1,0:T(8,128)(2,1)S(1)}, bf16[256,1024]{1,0:T(8,128)(2,1)}, u32[]{:S(2)}) copy-start(bf16[256,1024]{1,0:T(8,128)(2,1)} %param.26) | copy-start | bytes 1572868
  17.4 8.9 %copy-start.21 = (bf16[256,1024]{1,0:T(8,128)(2,1)S(1)}, bf16[256,1024]{1,0:T(8,128)(2,1)}, u32[]{:S(2)}) copy-start(bf16[256,1024]{1,0:T(8,128)(2,1)} %param.23) | copy-start | bytes 1572868
  17.4 221.5 %all-gather.3.cloned.1.call-start = ((), (), s32[]{:S(2)}) async-start(), calls=%async_computation.1 | async-start | bytes 17825792 | tf_op jit(solution)/shard_map/all_gather | solution.py:121
  18.2 15.7 %collective-permute-start = (bf16[128,2048]{1,0:T(8,128)(2,1)}, bf16[128,2048]{1,0:T(8,128)(2,1)}, u32[]{:S(2)}, u32[]{:S(2)}) collective-permute-start(bf16[128,2048]{1,0:T(8,128)(2,1)} %get-tuple-element.677), channel_id=1, source_target_pairs={{0,1},{1,2},{2,3},{3,4},{4,5},{5,6},{6,7},{7,8},{8,9},{9,10},{10,1... | collective-permute-start | bytes 1572872 | tf_op jit(solution)/shard_map/ppermute | solution.py:19
  23.1 16.6 %collective-permute-start.1 = (bf16[128,2048]{1,0:T(8,128)(2,1)}, bf16[128,2048]{1,0:T(8,128)(2,1)}, u32[]{:S(2)}, u32[]{:S(2)}) collective-permute-start(bf16[128,2048]{1,0:T(8,128)(2,1)} %get-tuple-element.680), channel_id=1, source_target_pairs={{1,0},{2,1},{3,2},{4,3},{5,4},{6,5},{7,6},{8,7},{9,8},{10,9},{11,1... | collective-permute-start | bytes 1572872 | tf_op jit(solution)/shard_map/ppermute | solution.py:20
  25.2 14.5 %copy-start.6 = (bf16[256,2048]{1,0:T(8,128)(2,1)S(1)}, bf16[256,2048]{1,0:T(8,128)(2,1)}, u32[]{:S(2)}) copy-start(bf16[256,2048]{1,0:T(8,128)(2,1)} %copy-done.5) | copy-start | bytes 3145732
  43.3 5.3 copy-start.15
  125.1 134.8 %copy-start.18 = (bf16[256,1024]{0,1:T(8,128)(2,1)}, bf16[256,1024]{0,1:T(8,128)(2,1)S(1)}, u32[]{:S(2)}) copy-start(bf16[256,1024]{0,1:T(8,128)(2,1)S(1)} %copy.241) | copy-start | bytes 1572868
  127.3 132.6 %copy-start.24 = (s32[1,15]{1,0:T(1,128)S(1)}, s32[1,15]{1,0:T(1,128)}, u32[]{:S(2)}) copy-start(s32[1,15]{1,0:T(1,128)} %param.27) | copy-start | bytes 184
  274.4 3.7 copy-start.1
  274.4 3.6 copy-start.14
  334.6 336.6 %copy-start.23 = (s32[2]{0:T(128)S(1)}, s32[2]{0:T(128)}, u32[]{:S(2)}) copy-start(s32[2]{0:T(128)} %param.29) | copy-start | bytes 28
  334.6 336.7 %copy-start.3 = (f32[8,256,256]{2,1,0:T(8,128)S(1)}, f32[8,256,256]{2,1,0:T(8,128)}, u32[]{:S(2)}) copy-start(f32[8,256,256]{2,1,0:T(8,128)} %copy-done.2) | copy-start | bytes 6291460
  334.6 463.1 %all-to-all-start = ((bf16[16,128,2048]{2,1,0:T(8,128)(2,1)}), bf16[16,128,2048]{2,1,0:T(8,128)(2,1)}, u32[]{:S(2)}, u32[]{:S(2)}) async-start(bf16[16,128,2048]{2,1,0:T(8,128)(2,1)} %get-tuple-element.438), calls=%async_computation | async-start | bytes 16777216 | tf_op jit(solution)/shard_map/all_to_all | solution.py:232
  505.5 290.3 %all-reduce.6.cloned.1.call-start = ((), (), s32[]{:S(2)}) async-start(), calls=%async_computation.2 | async-start | bytes 2097152 | tf_op jit(solution)/shard_map/psum | solution.py:246
  689.2 4.0 copy-start.16
  706.9 4.8 copy-start.7
  710.1 12.8 %copy-start.4 = (f32[256,8,128]{0,2,1:T(8,128)S(1)}, f32[256,8,128]{0,2,1:T(8,128)}, u32[]{:S(2)}) copy-start(f32[256,8,128]{0,2,1:T(8,128)} %get-tuple-element.437) | copy-start | bytes 3145732
  710.1 12.8 %copy-start.13 = (bf16[8,256,256]{1,2,0:T(8,128)(2,1)S(1)}, bf16[8,256,256]{1,2,0:T(8,128)(2,1)}, u32[]{:S(2)}) copy-start(bf16[8,256,256]{1,2,0:T(8,128)(2,1)} %copy-done.12) | copy-start | bytes 3145732
  710.1 12.8 %copy-start.19 = (bf16[256,1024]{0,1:T(8,128)(2,1)S(1)}, bf16[256,1024]{0,1:T(8,128)(2,1)}, u32[]{:S(2)}) copy-start(bf16[256,1024]{0,1:T(8,128)(2,1)} %copy-done.18) | copy-start | bytes 1572868
  714.4 97.7 %collective-permute-start.3 = (bf16[128,2048]{1,0:T(8,128)(2,1)}, bf16[128,2048]{1,0:T(8,128)(2,1)}, u32[]{:S(2)}, u32[]{:S(2)}) collective-permute-start(bf16[128,2048]{1,0:T(8,128)(2,1)} %fusion.50), channel_id=1, source_target_pairs={{1,0},{2,1},{3,2},{4,3},{5,4},{6,5},{7,6},{8,7},{9,8},{10,9},{11,1... | collective-permute-start | bytes 1572872 | tf_op jit(solution)/shard_map/ppermute | solution.py:20
  717.8 94.3 %collective-permute-start.2 = (bf16[128,2048]{1,0:T(8,128)(2,1)}, bf16[128,2048]{1,0:T(8,128)(2,1)}, u32[]{:S(2)}, u32[]{:S(2)}) collective-permute-start(bf16[128,2048]{1,0:T(8,128)(2,1)} %fusion.49), channel_id=1, source_target_pairs={{0,1},{1,2},{2,3},{3,4},{4,5},{5,6},{6,7},{7,8},{8,9},{9,10},{10,1... | collective-permute-start | bytes 1572872 | tf_op jit(solution)/shard_map/ppermute | solution.py:19
  797.7 12.9 %copy-start.8 = (f32[4,128,2048]{2,1,0:T(8,128)S(1)}, f32[4,128,2048]{2,1,0:T(8,128)}, u32[]{:S(2)}) copy-start(f32[4,128,2048]{2,1,0:T(8,128)} %copy-done.7) | copy-start | bytes 12582916
  (10 other events, 22.4 us)
Sparse Core Ops, SparseCore 0:
  17.6 101.8 all-reduce.7
  121.8 117.0 all-gather.2
  689.3 106.4 all-reduce.5
where the time goes:
time: 835 us; the launch traced here: 823 us
  waiting for transfers between devices  259 us (31%)
  starting transfers between devices  183 us (22%)
  blocking collectives  165 us (20%)
  local copies, waits for them, and re-layouts  108 us (13%)
  matrix products  48.5 us (6%)
  between operations  20.7 us (2%)
  other arithmetic  19.4 us (2%)
  loops' own time  18.6 us (2%)
    all_to_all x1, starting transfers between devices, body(): lax.all_to_all(outgoing_grads, 'seq', split_axis=0, concat_axis=0, tiled=...  171 us
    unnamed x1, blocking collectives  148 us
    all_gather x1, waiting for transfers between devices, body(): whole = lax.all_gather(paired, 'seq', axis=0, tiled=True)  112 us
    psum x1, waiting for transfers between devices, body(): lax.psum(global_grad_pairs.reshape(GLOB, BLK, 2 * width).astype(jnp.bfloa...  70.4 us
    psum x1, waiting for transfers between devices, from_root(): return lax.psum(jnp.where(mine, array, jnp.zeros_like(array)), axis)  66.1 us
    while x2, local copies, waits for them, and re-layouts, body(): lax.fori_loop(0, my_count, far_stats, (run_peak, run_total))  21.2 us
    all_gather x1, blocking collectives, body(): lax.all_gather(far_pick, 'seq', axis=0, tiled=True)  17.2 us
  transfers between devices with their start and end apart: 8, of which 5 were waited for; matrix products, arithmetic and copies ran while one was open for 10% of the time, Pallas kernels for 0%

commit v1 on v0

v1 whole, which is shorter than its diff:
```python
import jax
import jax.numpy as jnp
from jax import lax
from jax.experimental import pallas as pl
from jax.experimental.pallas import tpu as pltpu
from jax.sharding import PartitionSpec as P

HEADS = 8
HD = 128
BLK = 128
GLOB = 2
SHARDS = 16
SLOTS = 15
LIGHT = 4
ROWS = 2 * BLK
META = 16
IN_ROWS = ROWS + BLK + META
OUT_ROWS = ROWS + BLK // 2
SCALE = HD**-0.5
LOG2E = 1.4426950408889634
MASKED = -1e30
NEAR = 3 + GLOB


def pack_kernel(pick_ref, count_ref, q_ref, k_ref, v_ref, g_ref, out_ref):
    lanes = lax.broadcasted_iota(jnp.int32, (META, 2 * HD), 1)
    meta = jnp.where(lanes == SLOTS, count_ref[0], 0)
    for slot in range(SLOTS):
        meta = jnp.where(lanes == slot, pick_ref[0, slot], meta)
    meta = meta.astype(jnp.float32).astype(jnp.bfloat16)
    for head in range(HEADS):
        cols = slice(head * HD, (head + 1) * HD)
        for half in range(2):
            dev = 2 * head + half
            rows = slice(half * BLK, (half + 1) * BLK)
            out_ref[dev, :ROWS, :HD] = k_ref[:, cols]
            out_ref[dev, :ROWS, HD:] = v_ref[:, cols]
            out_ref[dev, ROWS : ROWS + BLK, :HD] = q_ref[rows, cols]
            out_ref[dev, ROWS : ROWS + BLK, HD:] = g_ref[rows, cols]
            out_ref[dev, ROWS + BLK :, :] = meta


def unpack_kernel(in_ref, dq_ref, dk_ref, dv_ref):
    for head in range(HEADS):
        cols = slice(head * HD, (head + 1) * HD)
        first = in_ref[2 * head, :ROWS, :].astype(jnp.float32)
        second = in_ref[2 * head + 1, :ROWS, :].astype(jnp.float32)
        total = (first + second).astype(jnp.bfloat16)
        dk_ref[:, cols] = total[:, :HD]
        dv_ref[:, cols] = total[:, HD:]
        for half in range(2):
            low = half * BLK
            mid = low + BLK // 2
            dq_ref[low:mid, cols] = in_ref[2 * head + half, ROWS:, :HD]
            dq_ref[mid : low + BLK, cols] = in_ref[2 * head + half, ROWS:, HD:]


def attention_kernel(
    ids_ref, x_ref, o_ref, acc, glob_kv, glob_acc, wmat, kv, sp, gb, meta_v, meta_s, sem
):
    half = lax.rem(lax.axis_index("seq"), 2)
    meta_v[...] = x_ref[:, ROWS + BLK, :HD].astype(jnp.float32).astype(jnp.int32)
    copy = pltpu.make_async_copy(meta_v, meta_s, sem)
    copy.start()
    acc[...] = jnp.zeros_like(acc)
    glob_acc[...] = jnp.zeros_like(glob_acc)
    wmat[...] = jnp.zeros_like(wmat)
    for slot in range(GLOB):
        block = ids_ref[slot]
        glob_kv[slot * BLK : (slot + 1) * BLK, :] = x_ref[
            block // 2, pl.ds(pl.multiple_of(lax.rem(block, 2) * BLK, BLK), BLK), :
        ]
    copy.wait()

    def locate(shard, slot):
        target = lax.rem(shard + 1 + slot, SHARDS)
        return target, pl.ds(pl.multiple_of(meta_s[shard, slot] * BLK, BLK), BLK)

    def process(shard, far, masked):
        count = meta_s[shard, SLOTS]
        beside = jnp.where(half == 0, shard - 1, shard + 1)
        beside_valid = (beside >= 0) & (beside < SHARDS)
        beside = jnp.clip(beside, 0, SHARDS - 1)
        beside_rows = pl.ds(pl.multiple_of((1 - half) * BLK, BLK), BLK)
        wmat[:BLK, :HD] = x_ref[shard, ROWS : ROWS + BLK, :HD]
        wmat[BLK:, HD:] = x_ref[shard, ROWS : ROWS + BLK, HD:]
        kv[:ROWS, :] = x_ref[shard, :ROWS, :]
        kv[ROWS : 2 * ROWS, :] = glob_kv[...]
        kv[2 * ROWS : 2 * ROWS + BLK, :] = x_ref[beside, beside_rows, :]
        for slot in range(far):
            target, rows = locate(shard, slot)
            kv[(NEAR + slot) * BLK : (NEAR + slot + 1) * BLK, :] = x_ref[target, rows, :]
        chunks = NEAR + far
        length = chunks * BLK
        sp[:length, :] = lax.dot_general(
            kv[:length, :], wmat[...], (((1,), (1,)), ((), ())), preferred_element_type=jnp.float32
        )

        def fold(value, op):
            parts = [value[i * 8 : (i + 1) * 8] for i in range(BLK // 8)]
            while len(parts) > 1:
                parts = [op(a, b) for a, b in zip(parts[::2], parts[1::2])]
            return parts[0]

        peak = None
        for chunk in range(chunks):
            rows = slice(chunk * BLK, (chunk + 1) * BLK)
            scores = sp[rows, :HD] * (SCALE * LOG2E)
            if chunk == NEAR - 1:
                scores = scores + jnp.where(beside_valid, 0.0, MASKED)
            elif chunk >= NEAR and masked:
                scores = scores + jnp.where(chunk - NEAR < count, 0.0, MASKED)
            sp[rows, :HD] = scores
            high = fold(scores, jnp.maximum)
            peak = high if peak is None else jnp.maximum(peak, high)
        peak = jnp.max(peak, axis=0, keepdims=True)
        total = jnp.zeros((8, HD), jnp.float32)
        delta = jnp.zeros((8, HD), jnp.float32)
        for chunk in range(chunks):
            rows = slice(chunk * BLK, (chunk + 1) * BLK)
            weights = jnp.exp2(sp[rows, :HD] - peak)
            sp[rows, :HD] = weights
            total = total + fold(weights, jnp.add)
            delta = delta + fold(weights * sp[rows, HD:], jnp.add)
        inverse = 1.0 / jnp.sum(total, axis=0, keepdims=True)
        delta = jnp.sum(delta, axis=0, keepdims=True) * inverse
        for chunk in range(chunks):
            rows = slice(chunk * BLK, (chunk + 1) * BLK)
            weights = sp[rows, :HD] * inverse
            gb[rows, HD:] = weights.astype(jnp.bfloat16)
            gb[rows, :HD] = (weights * (sp[rows, HD:] - delta) * SCALE).astype(jnp.bfloat16)
        grad_query = lax.dot_general(
            gb[:length, :HD],
            kv[:length, :HD],
            (((0,), (0,)), ((), ())),
            preferred_element_type=jnp.float32,
        ).astype(jnp.bfloat16)
        o_ref[shard, ROWS:, :HD] = grad_query[: BLK // 2]
        o_ref[shard, ROWS:, HD:] = grad_query[BLK // 2 :]
        grads = jnp.dot(gb[:length, :], wmat[...], preferred_element_type=jnp.float32)
        acc[shard, :, :] += grads[:ROWS]
        glob_acc[...] += grads[ROWS : 2 * ROWS]
        acc[beside, beside_rows, :] += grads[2 * ROWS : 2 * ROWS + BLK]
        for slot in range(far):
            target, rows = locate(shard, slot)
            acc[target, rows, :] += grads[(NEAR + slot) * BLK : (NEAR + slot + 1) * BLK]

    busy = 0
    for shard in range(SHARDS):
        busy = jnp.where(meta_s[shard, SLOTS] > LIGHT, shard, busy)

    def light_step(step, carry):
        process(step + jnp.where(step >= busy, 1, 0), LIGHT, True)
        return carry

    lax.fori_loop(0, SHARDS - 1, light_step, 0)
    process(busy, SLOTS, False)
    for slot in range(GLOB):
        block = ids_ref[slot]
        rows = pl.ds(pl.multiple_of(lax.rem(block, 2) * BLK, BLK), BLK)
        acc[block // 2, rows, :] += glob_acc[slot * BLK : (slot + 1) * BLK, :]

    def store_step(shard, carry):
        o_ref[shard, :ROWS, :] = acc[shard, :, :].astype(jnp.bfloat16)
        return carry

    lax.fori_loop(0, SHARDS, store_step, 0)


VMEM = pl.BlockSpec(memory_space=pltpu.VMEM)
SMEM = pl.BlockSpec(memory_space=pltpu.SMEM)


def body(query_matrix, key_rows, value_rows, output_gradient_rows, far_pick, far_count, global_ids):
    width = HEADS * HD
    sent = pl.pallas_call(
        pack_kernel,
        out_shape=jax.ShapeDtypeStruct((SHARDS, IN_ROWS, 2 * HD), jnp.bfloat16),
        in_specs=[SMEM, SMEM, VMEM, VMEM, VMEM, VMEM],
        out_specs=VMEM,
        compiler_params=pltpu.CompilerParams(vmem_limit_bytes=24 << 20),
        name="pack",
    )(far_pick, far_count, query_matrix, key_rows, value_rows, output_gradient_rows)
    received = lax.all_to_all(sent, "seq", split_axis=0, concat_axis=0, tiled=True)
    longest = (NEAR + SLOTS) * BLK
    grads = pl.pallas_call(
        attention_kernel,
        out_shape=jax.ShapeDtypeStruct((SHARDS, OUT_ROWS, 2 * HD), jnp.bfloat16),
        in_specs=[SMEM, VMEM],
        out_specs=VMEM,
        scratch_shapes=[
            pltpu.VMEM((SHARDS, ROWS, 2 * HD), jnp.float32),
            pltpu.VMEM((GLOB * BLK, 2 * HD), jnp.bfloat16),
            pltpu.VMEM((GLOB * BLK, 2 * HD), jnp.float32),
            pltpu.VMEM((2 * BLK, 2 * HD), jnp.bfloat16),
            pltpu.VMEM((longest, 2 * HD), jnp.bfloat16),
            pltpu.VMEM((longest, 2 * HD), jnp.float32),
            pltpu.VMEM((longest, 2 * HD), jnp.bfloat16),
            pltpu.VMEM((SHARDS, HD), jnp.int32),
            pltpu.SMEM((SHARDS, HD), jnp.int32),
            pltpu.SemaphoreType.DMA,
        ],
        compiler_params=pltpu.CompilerParams(vmem_limit_bytes=48 << 20),
        name="attention",
    )(global_ids, received)
    returned = lax.all_to_all(grads, "seq", split_axis=0, concat_axis=0, tiled=True)
    out = jax.ShapeDtypeStruct((ROWS, width), jnp.bfloat16)
    return pl.pallas_call(
        unpack_kernel,
        out_shape=(out, out, out),
        in_specs=[VMEM],
        out_specs=(VMEM, VMEM, VMEM),
        compiler_params=pltpu.CompilerParams(vmem_limit_bytes=24 << 20),
        name="unpack",
    )(returned)


def solution(mesh):
    rows = P(("pat", "seq"), None)
    in_specs = (rows, rows, rows, rows, rows, P("seq"), P("pat"))
    return jax.shard_map(
        body, mesh=mesh, in_specs=in_specs, out_specs=(rows, rows, rows), check_vma=False
    )
```

time: 835 us -> 118 us (0.14); the launches traced: 823 us -> 116 us
  waiting for transfers between devices: 259 us -> 0 us
  starting transfers between devices: 183 us -> 0 us
  local copies, waits for them, and re-layouts: 108 us -> 4.82 us
  blocking collectives: 165 us -> 82.6 us
  matrix products: 48.5 us -> 0 us
  Pallas kernels: 0 us -> 27.6 us
  other arithmetic: 19.4 us -> 0 us
  between operations: 20.7 us -> 1.32 us
  loops' own time: 18.6 us -> 0 us
    all_to_all x1 -> x0, starting transfers between devices: 171 us -> none  [body(): lax.all_to_all(outgoing_grads, 'seq', split_axis=0, concat_axis=0, tiled=...]
    unnamed x1 -> x0, blocking collectives: 148 us -> none
    psum x2 -> x0, waiting for transfers between devices: 136 us -> none  [the longest x1 70.4 us: body(): lax.psum(global_grad_pairs.reshape(GLOB, BLK, 2 * width).astype(jnp.bfloa...]
    all_gather x1 -> x0, waiting for transfers between devices: 112 us -> none  [body(): whole = lax.all_gather(paired, 'seq', axis=0, tiled=True)]
    all_to_all x0 -> x2, blocking collectives: none -> 82.6 us  [the longest x1 47.5 us: body(): lax.all_to_all(sent, 'seq', split_axis=0, concat_axis=0, tiled=True)]
    dot_general x43 -> x0, matrix products: 48.5 us -> none  [the longest x1 12.9 us: body(): jnp.einsum('hp,hci->pci', block_selector, distant_return, preferred_eleme...]
    pallas_call x0 -> x3, Pallas kernels: none -> 27.6 us  [the longest x1 25.1 us: body(): pl.pallas_call(attention_kernel, out_shape=jax.ShapeDtypeStruct((SHARDS,...]
    slice x20 -> x0, local copies, waits for them, and re-layouts: 25.7 us -> none  [the longest x12 15.6 us: heads_of(): pairs[..., width:].reshape(lead + (HEADS, HD))]
  transfers between devices with their start and end apart: 8 -> 0, of which waited for: 5 -> 0; matrix products, arithmetic and copies ran while one was open for 10% -> 0% of each run, Pallas kernels for 0% -> 0%
where the time goes in v1:
time: 118 us; the launch traced here: 116 us
  blocking collectives  82.6 us (70%)
  Pallas kernels  27.6 us (23%)
  local copies, waits for them, and re-layouts  4.82 us (4%)
  between operations  1.32 us (1%)
    all_to_all x1, blocking collectives, body(): lax.all_to_all(sent, 'seq', split_axis=0, concat_axis=0, tiled=True)  47.5 us
    all_to_all x1, blocking collectives, body(): lax.all_to_all(grads, 'seq', split_axis=0, concat_axis=0, tiled=True)  35 us
    pallas_call x1, Pallas kernels, body(): pl.pallas_call(attention_kernel, out_shape=jax.ShapeDtypeStruct((SHARDS,...  25.1 us
    unnamed x12, local copies, waits for them, and re-layouts  4.82 us

profile of v1, /device:TPU:1, one launch (start us, length us, event | category | flops | bytes accessed | tf_op | source)
XLA Modules:
  0.0 116.3 jit_solution(8518195159186219663)
XLA Ops:
  1.3 0.0 copy-start
  1.3 1.0 copy-done
  2.3 0.0 copy-start.1
  2.3 1.0 copy-done.1
  3.4 0.0 copy-start.2
  3.4 1.0 copy-done.2
  4.4 0.0 copy-start.3
  4.4 1.0 copy-done.3
  5.4 0.0 copy-start.4
  5.4 0.7 copy-done.4
  6.1 1.0 pack.1
  7.1 0.0 copy-start.5
  7.1 47.5 %all_to_all.10.x_ref = bf16[16,400,256]{2,1,0:T(8,128)(2,1)S(1)} all-to-all(bf16[16,400,256]{2,1,0:T(8,128)(2,1)S(1)} %pack.1), channel_id=1, replica_groups=mesh['pat'=16,'seq'=16] {'seq'}, dimensions={0} | all-to-all | bytes 6553600 | tf_op jit(solution)/shard_map/all_to_all | solution.py:184
  54.7 0.0 copy-done.5
  54.7 25.1 %attention.1 = bf16[16,320,256]{2,1,0:T(8,128)(2,1)S(1)} custom-call(s32[2]{0:T(128)S(1)} %copy-done.5, bf16[16,400,256]{2,1,0:T(8,128)(2,1)S(1)} %all_to_all.10.x_ref), custom_call_target="tpu_custom_call" | custom-call | tf_op jit(solution)/shard_map/attention/pallas_call | solution.py:186
  79.8 35.0 %all_to_all.11.in_ref = bf16[16,320,256]{2,1,0:T(8,128)(2,1)S(1)} all-to-all(bf16[16,320,256]{2,1,0:T(8,128)(2,1)S(1)} %attention.1), channel_id=1, replica_groups=mesh['pat'=16,'seq'=16] {'seq'}, dimensions={0} | all-to-all | bytes 5242880 | tf_op jit(solution)/shard_map/all_to_all | solution.py:206
  114.8 1.5 %unpack.1 = (bf16[256,1024]{1,0:T(8,128)(2,1)}, bf16[256,1024]{1,0:T(8,128)(2,1)}, bf16[256,1024]{1,0:T(8,128)(2,1)}) custom-call(bf16[16,320,256]{2,1,0:T(8,128)(2,1)S(1)} %all_to_all.11.in_ref), custom_call_target="tpu_custom_call" | custom-call | tf_op jit(solution)/shard_map/unpack/pallas_call | solution.py:208
Async XLA Ops:
  1.3 1.0 copy-start
  2.3 1.0 copy-start.1
  3.4 1.0 copy-start.2
  4.4 1.0 copy-start.3
  5.4 0.7 copy-start.4
  7.1 47.6 %copy-start.5 = (s32[2]{0:T(128)S(1)}, s32[2]{0:T(128)}, u32[]{:S(2)}) copy-start(s32[2]{0:T(128)} %ids_ref.1) | copy-start | bytes 28

commit v2 on v1

v2 whole, which is shorter than its diff:
```python
import jax
import jax.numpy as jnp
from jax import lax
from jax.experimental import pallas as pl
from jax.experimental.pallas import tpu as pltpu
from jax.sharding import PartitionSpec as P

HEADS = 8
HD = 128
BLK = 128
GLOB = 2
SHARDS = 16
SLOTS = 15
IDS = 16
LIGHT = 4
ROWS = 2 * BLK
META = 16
IN_ROWS = 2 * BLK + META
OUT_ROWS = BLK + BLK // 2
SCALE = HD**-0.5
LOG2E = 1.4426950408889634
MASKED = -1e30
NEAR = 3 + GLOB


def split_kernel(pick_ref, count_ref, ids_ref, k_ref, v_ref, q_ref, g_ref, out_ref, meta_ref, sems):
    other = 1 - lax.rem(lax.axis_index("pat"), 2)
    source = pl.ds(pl.multiple_of(other * BLK, BLK), BLK)
    copies = []
    for index, ref in enumerate((k_ref, v_ref, q_ref, g_ref)):
        target = out_ref.at[pl.ds(index * BLK, BLK), :]
        copies.append(pltpu.make_async_copy(ref.at[source, :], target, sems.at[index]))
    for copy in copies:
        copy.start()
    lanes = lax.broadcasted_iota(jnp.int32, (META, HEADS * HD), 1)
    meta = jnp.where(lanes == SLOTS, count_ref[0], 0)
    for slot in range(SLOTS):
        meta = jnp.where(lanes == slot, pick_ref[0, slot], meta)
    for slot in range(GLOB):
        meta = jnp.where(lanes == IDS + slot, ids_ref[slot], meta)
    meta = meta.astype(jnp.float32).astype(jnp.bfloat16)
    out_ref[4 * BLK :, :] = meta
    meta_ref[...] = meta[:, : 2 * HD]
    for copy in copies:
        copy.wait()


def pack_kernel(r_ref, meta_ref, k_ref, v_ref, q_ref, g_ref, out_ref, sems):
    core = lax.rem(lax.axis_index("pat"), 2)
    source = pl.ds(pl.multiple_of(core * BLK, BLK), BLK)
    copies = []
    for index, ref in enumerate((k_ref, v_ref, q_ref, g_ref)):
        rows = pl.ds(index // 2 * BLK, BLK)
        lanes = pl.ds(index % 2 * HD, HD)
        for head in range(HEADS):
            target = out_ref.at[core * HEADS + head, rows, lanes]
            origin = ref.at[source, pl.ds(head * HD, HD)]
            copies.append(pltpu.make_async_copy(origin, target, sems.at[index, head]))
    for copy in copies:
        copy.start()
    away = (1 - core) * HEADS
    for head in range(HEADS):
        cols = slice(head * HD, (head + 1) * HD)
        out_ref[away + head, :BLK, :HD] = r_ref[:BLK, cols]
        out_ref[away + head, :BLK, HD:] = r_ref[BLK : 2 * BLK, cols]
        out_ref[away + head, BLK : 2 * BLK, :HD] = r_ref[2 * BLK : 3 * BLK, cols]
        out_ref[away + head, BLK : 2 * BLK, HD:] = r_ref[3 * BLK : 4 * BLK, cols]
        out_ref[away + head, 2 * BLK :, :] = r_ref[4 * BLK :, : 2 * HD]
        out_ref[core * HEADS + head, 2 * BLK :, :] = meta_ref[...]
    for copy in copies:
        copy.wait()


def combine_kernel(own_ref, r_ref, out_ref):
    for shard in range(SHARDS):
        total = own_ref[shard, :BLK, :].astype(jnp.float32) + r_ref[shard].astype(jnp.float32)
        out_ref[shard, :BLK, :] = total.astype(jnp.bfloat16)
        out_ref[shard, BLK:, :] = own_ref[shard, BLK:, :]


def unpack_kernel(own_ref, r_ref, dq_ref, dk_ref, dv_ref):
    core = lax.rem(lax.axis_index("pat"), 2)

    def place(piece, row, cols):
        rows = pl.ds(pl.multiple_of(row, BLK), BLK)
        dk_ref[rows, cols] = piece[:BLK, :HD]
        dv_ref[rows, cols] = piece[:BLK, HD:]
        rows = pl.ds(pl.multiple_of(row, BLK), BLK // 2)
        dq_ref[rows, cols] = piece[BLK:, :HD]
        rows = pl.ds(pl.multiple_of(row + BLK // 2, BLK // 2), BLK // 2)
        dq_ref[rows, cols] = piece[BLK:, HD:]

    for head in range(HEADS):
        cols = slice(head * HD, (head + 1) * HD)
        place(own_ref[core * HEADS + head], core * BLK, cols)
        place(r_ref[head], (1 - core) * BLK, cols)


def attention_kernel(
    x_ref, r_ref, o_ref, send_ref, acc, blocks, glob_kv, glob_acc, wmat, kv, sp, gb, meta_v, meta_s, sem
):
    half = lax.rem(lax.axis_index("pat"), 2)
    meta_v[...] = x_ref[:, 2 * BLK, :HD].astype(jnp.float32).astype(jnp.int32)
    copy = pltpu.make_async_copy(meta_v, meta_s, sem)
    copy.start()
    own_rows = pl.ds(pl.multiple_of(half * BLK, BLK), BLK)
    other_rows = pl.ds(pl.multiple_of((1 - half) * BLK, BLK), BLK)
    for shard in range(SHARDS):
        blocks[shard, own_rows, :] = x_ref[shard, :BLK, :]
        blocks[shard, other_rows, :] = r_ref[shard]
    acc[...] = jnp.zeros_like(acc)
    glob_acc[...] = jnp.zeros_like(glob_acc)
    wmat[...] = jnp.zeros_like(wmat)
    copy.wait()
    for slot in range(GLOB):
        block = meta_s[0, IDS + slot]
        glob_kv[slot * BLK : (slot + 1) * BLK, :] = blocks[
            block // 2, pl.ds(pl.multiple_of(lax.rem(block, 2) * BLK, BLK), BLK), :
        ]

    def locate(shard, slot):
        target = lax.rem(shard + 1 + slot, SHARDS)
        return target, pl.ds(pl.multiple_of(meta_s[shard, slot] * BLK, BLK), BLK)

    def process(shard, far, masked):
        count = meta_s[shard, SLOTS]
        beside = jnp.where(half == 0, shard - 1, shard + 1)
        beside_valid = (beside >= 0) & (beside < SHARDS)
        beside = jnp.clip(beside, 0, SHARDS - 1)
        wmat[:BLK, :HD] = x_ref[shard, BLK : 2 * BLK, :HD]
        wmat[BLK:, HD:] = x_ref[shard, BLK : 2 * BLK, HD:]
        kv[:ROWS, :] = blocks[shard]
        kv[ROWS : 2 * ROWS, :] = glob_kv[...]
        kv[2 * ROWS : 2 * ROWS + BLK, :] = blocks[beside, other_rows, :]
        for slot in range(far):
            target, rows = locate(shard, slot)
            kv[(NEAR + slot) * BLK : (NEAR + slot + 1) * BLK, :] = blocks[target, rows, :]
        chunks = NEAR + far
        length = chunks * BLK
        sp[:length, :] = lax.dot_general(
            kv[:length, :], wmat[...], (((1,), (1,)), ((), ())), preferred_element_type=jnp.float32
        )

        def fold(value, op):
            parts = [value[i * 8 : (i + 1) * 8] for i in range(BLK // 8)]
            while len(parts) > 1:
                parts = [op(a, b) for a, b in zip(parts[::2], parts[1::2])]
            return parts[0]

        peak = None
        for chunk in range(chunks):
            rows = slice(chunk * BLK, (chunk + 1) * BLK)
            scores = sp[rows, :HD] * (SCALE * LOG2E)
            if chunk == NEAR - 1:
                scores = scores + jnp.where(beside_valid, 0.0, MASKED)
            elif chunk >= NEAR and masked:
                scores = scores + jnp.where(chunk - NEAR < count, 0.0, MASKED)
            sp[rows, :HD] = scores
            high = fold(scores, jnp.maximum)
            peak = high if peak is None else jnp.maximum(peak, high)
        peak = jnp.max(peak, axis=0, keepdims=True)
        total = jnp.zeros((8, HD), jnp.float32)
        delta = jnp.zeros((8, HD), jnp.float32)
        for chunk in range(chunks):
            rows = slice(chunk * BLK, (chunk + 1) * BLK)
            weights = jnp.exp2(sp[rows, :HD] - peak)
            sp[rows, :HD] = weights
            total = total + fold(weights, jnp.add)
            delta = delta + fold(weights * sp[rows, HD:], jnp.add)
        inverse = 1.0 / jnp.sum(total, axis=0, keepdims=True)
        delta = jnp.sum(delta, axis=0, keepdims=True) * inverse
        for chunk in range(chunks):
            rows = slice(chunk * BLK, (chunk + 1) * BLK)
            weights = sp[rows, :HD] * inverse
            gb[rows, HD:] = weights.astype(jnp.bfloat16)
            gb[rows, :HD] = (weights * (sp[rows, HD:] - delta) * SCALE).astype(jnp.bfloat16)
        grad_query = lax.dot_general(
            gb[:length, :HD],
            kv[:length, :HD],
            (((0,), (0,)), ((), ())),
            preferred_element_type=jnp.float32,
        ).astype(jnp.bfloat16)
        o_ref[shard, BLK:, :HD] = grad_query[: BLK // 2]
        o_ref[shard, BLK:, HD:] = grad_query[BLK // 2 :]
        grads = jnp.dot(gb[:length, :], wmat[...], preferred_element_type=jnp.float32)
        acc[shard, :, :] += grads[:ROWS]
        glob_acc[...] += grads[ROWS : 2 * ROWS]
        acc[beside, other_rows, :] += grads[2 * ROWS : 2 * ROWS + BLK]
        for slot in range(far):
            target, rows = locate(shard, slot)
            acc[target, rows, :] += grads[(NEAR + slot) * BLK : (NEAR + slot + 1) * BLK]

    busy = 0
    for shard in range(SHARDS):
        busy = jnp.where(meta_s[shard, SLOTS] > LIGHT, shard, busy)

    def light_step(step, carry):
        process(step + jnp.where(step >= busy, 1, 0), LIGHT, True)
        return carry

    lax.fori_loop(0, SHARDS - 1, light_step, 0)
    process(busy, SLOTS, False)
    for slot in range(GLOB):
        block = meta_s[0, IDS + slot]
        rows = pl.ds(pl.multiple_of(lax.rem(block, 2) * BLK, BLK), BLK)
        acc[block // 2, rows, :] += glob_acc[slot * BLK : (slot + 1) * BLK, :]

    def store_step(shard, carry):
        o_ref[shard, :BLK, :] = acc[shard, own_rows, :].astype(jnp.bfloat16)
        send_ref[shard, :, :] = acc[shard, other_rows, :].astype(jnp.bfloat16)
        return carry

    lax.fori_loop(0, SHARDS, store_step, 0)


VMEM = pl.BlockSpec(memory_space=pltpu.VMEM)
SMEM = pl.BlockSpec(memory_space=pltpu.SMEM)
ANY = pl.BlockSpec(memory_space=pl.ANY)


def kernel_params(megabytes):
    return pltpu.CompilerParams(vmem_limit_bytes=megabytes << 20)


def bf16(*shape):
    return jax.ShapeDtypeStruct(shape, jnp.bfloat16)


def body(query_matrix, key_rows, value_rows, output_gradient_rows, far_pick, far_count, global_ids):
    width = HEADS * HD
    core = lax.rem(lax.axis_index("pat"), 2)
    arrays = (key_rows, value_rows, query_matrix, output_gradient_rows)
    pairs = [(i, i ^ 1) for i in range(lax.axis_size("pat"))]
    away, meta = pl.pallas_call(
        split_kernel,
        out_shape=(bf16(4 * BLK + META, width), bf16(META, 2 * HD)),
        in_specs=[SMEM, SMEM, SMEM, ANY, ANY, ANY, ANY],
        out_specs=(VMEM, VMEM),
        scratch_shapes=[pltpu.SemaphoreType.DMA((4,))],
        compiler_params=kernel_params(16),
        name="split",
    )(far_pick, far_count, global_ids, *arrays)
    arrived = lax.ppermute(away, "pat", pairs)
    sent = pl.pallas_call(
        pack_kernel,
        out_shape=bf16(SHARDS, IN_ROWS, 2 * HD),
        in_specs=[VMEM, VMEM, ANY, ANY, ANY, ANY],
        out_specs=VMEM,
        scratch_shapes=[pltpu.SemaphoreType.DMA((4, HEADS))],
        compiler_params=kernel_params(16),
        name="pack",
    )(arrived, meta, *arrays)
    received = lax.all_to_all(sent, "seq", split_axis=0, concat_axis=0, tiled=True)
    other = lax.ppermute(received[:, :BLK, :], "pat", pairs)
    longest = (NEAR + SLOTS) * BLK
    own, partial = pl.pallas_call(
        attention_kernel,
        out_shape=(bf16(SHARDS, OUT_ROWS, 2 * HD), bf16(SHARDS, BLK, 2 * HD)),
        in_specs=[VMEM, VMEM],
        out_specs=(VMEM, VMEM),
        scratch_shapes=[
            pltpu.VMEM((SHARDS, ROWS, 2 * HD), jnp.float32),
            pltpu.VMEM((SHARDS, ROWS, 2 * HD), jnp.bfloat16),
            pltpu.VMEM((GLOB * BLK, 2 * HD), jnp.bfloat16),
            pltpu.VMEM((GLOB * BLK, 2 * HD), jnp.float32),
            pltpu.VMEM((2 * BLK, 2 * HD), jnp.bfloat16),
            pltpu.VMEM((longest, 2 * HD), jnp.bfloat16),
            pltpu.VMEM((longest, 2 * HD), jnp.float32),
            pltpu.VMEM((longest, 2 * HD), jnp.bfloat16),
            pltpu.VMEM((SHARDS, HD), jnp.int32),
            pltpu.SMEM((SHARDS, HD), jnp.int32),
            pltpu.SemaphoreType.DMA,
        ],
        compiler_params=kernel_params(40),
        name="attention",
    )(received, other)
    partial = lax.ppermute(partial, "pat", pairs)
    combined = pl.pallas_call(
        combine_kernel,
        out_shape=bf16(SHARDS, OUT_ROWS, 2 * HD),
        in_specs=[VMEM, VMEM],
        out_specs=VMEM,
        compiler_params=kernel_params(16),
        name="combine",
    )(own, partial)
    returned = lax.all_to_all(combined, "seq", split_axis=0, concat_axis=0, tiled=True)
    foreign = lax.dynamic_slice_in_dim(returned, (1 - core) * HEADS, HEADS, axis=0)
    foreign = lax.ppermute(foreign, "pat", pairs)
    return pl.pallas_call(
        unpack_kernel,
        out_shape=(bf16(ROWS, width),) * 3,
        in_specs=[VMEM, VMEM],
        out_specs=(VMEM, VMEM, VMEM),
        compiler_params=kernel_params(16),
        name="unpack",
    )(returned, foreign)


def solution(mesh):
    rows = P(("pat", "seq"), None)
    in_specs = (rows, rows, rows, rows, rows, P("seq"), P("pat"))
    return jax.shard_map(
        body, mesh=mesh, in_specs=in_specs, out_specs=(rows, rows, rows), check_vma=False
    )
```

time: 118 us -> 114 us (0.966)
  blocking collectives: 82.6 us -> 33.6 us
  waiting for transfers between devices: 0 us -> 32.4 us
  starting transfers between devices: 0 us -> 11.1 us
  Pallas kernels: 27.6 us -> 29.1 us
    all_to_all x1 -> x0, blocking collectives: 35 us -> none  [body(): lax.all_to_all(grads, 'seq', split_axis=0, concat_axis=0, tiled=True)]
    all_to_all x0 -> x1, waiting for transfers between devices: none -> 23.6 us  [body(): lax.all_to_all(combined, 'seq', split_axis=0, concat_axis=0, tiled=True)]
    all_to_all x1, blocking collectives: 47.5 us -> 33.6 us  [body(): lax.all_to_all(sent, 'seq', split_axis=0, concat_axis=0, tiled=True)]
    ppermute x0 -> x4, waiting for transfers between devices: none -> 8.82 us  [the longest x1 2.33 us: body(): arrived = lax.ppermute(away, 'pat', pairs)]
    ppermute x0 -> x4, starting transfers between devices: none -> 7.38 us  [the longest x1 3.33 us: body(): arrived = lax.ppermute(away, 'pat', pairs)]
    all_to_all x0 -> x1, starting transfers between devices: none -> 3.71 us  [body(): lax.all_to_all(combined, 'seq', split_axis=0, concat_axis=0, tiled=True)]
    pallas_call x3 -> x5, Pallas kernels: 27.6 us -> 29.1 us  [the longest x1 24.7 us: body(): pl.pallas_call(attention_kernel, out_shape=(bf16(SHARDS, OUT_ROWS, 2 * HD...]
    unnamed x12 -> x20, local copies, waits for them, and re-layouts: 4.82 us -> 5.48 us
  transfers between devices with their start and end apart: 0 -> 5, of which waited for: 0 -> 5; matrix products, arithmetic and copies ran while one was open for 0% -> 0% of each run, Pallas kernels for 0% -> 0%
where the time goes in v2:
time: 114 us; the launch traced here: 113 us
  blocking collectives  33.6 us (29%)
  waiting for transfers between devices  32.4 us (28%)
  Pallas kernels  29.1 us (26%)
  starting transfers between devices  11.1 us (10%)
  local copies, waits for them, and re-layouts  5.63 us (5%)
  between operations  1.36 us (1%)
    all_to_all x1, blocking collectives, body(): lax.all_to_all(sent, 'seq', split_axis=0, concat_axis=0, tiled=True)  33.6 us
    pallas_call x1, Pallas kernels, body(): pl.pallas_call(attention_kernel, out_shape=(bf16(SHARDS, OUT_ROWS, 2 * HD...  24.7 us
    all_to_all x1, waiting for transfers between devices, body(): lax.all_to_all(combined, 'seq', split_axis=0, concat_axis=0, tiled=True)  23.6 us
    unnamed x20, local copies, waits for them, and re-layouts  5.48 us
    all_to_all x1, starting transfers between devices, body(): lax.all_to_all(combined, 'seq', split_axis=0, concat_axis=0, tiled=True)  3.71 us
    ppermute x1, starting transfers between devices, body(): arrived = lax.ppermute(away, 'pat', pairs)  3.33 us
    ppermute x1, waiting for transfers between devices, body(): arrived = lax.ppermute(away, 'pat', pairs)  2.33 us
    ppermute x1, waiting for transfers between devices, body(): partial = lax.ppermute(partial, 'pat', pairs)  2.29 us
  transfers between devices with their start and end apart: 5, of which 5 were waited for; matrix products, arithmetic and copies ran while one was open for 0% of the time, Pallas kernels for 0%

profile of v2, /device:TPU:1, one launch (start us, length us, event | category | flops | bytes accessed | tf_op | source)
XLA Modules:
  0.0 113.2 jit_solution(11892199839226112932)
XLA Ops:
  1.3 1.0 copy-done
  2.3 1.0 copy-done.2
  3.4 1.0 copy-done.4
  4.4 1.0 copy-done.6
  5.4 0.7 copy-done.8
  6.1 0.7 copy-done.9
  6.8 0.7 split.1
  7.5 3.3 %collective-permute-start = (bf16[528,1024]{1,0:T(8,128)(2,1)S(1)}, bf16[528,1024]{1,0:T(8,128)(2,1)S(1)}, u32[]{:S(2)}, u32[]{:S(2)}) collective-permute-start(bf16[528,1024]{1,0:T(8,128)(2,1)S(1)} %get-tuple-element.7), channel_id=1, source_target_pairs={{0,16},{16,0},{32,48},{48,32},{64,80},{80,64},{96,112},{112,96},{1... | collective-permute-start | bytes 3244040 | tf_op jit(solution)/shard_map/ppermute | solution.py:243
  10.8 2.3 %collective-permute-done.r_ref = bf16[528,1024]{1,0:T(8,128)(2,1)S(1)} collective-permute-done((bf16[528,1024]{1,0:T(8,128)(2,1)S(1)}, bf16[528,1024]{1,0:T(8,128)(2,1)S(1)}, u32[]{:S(2)}, u32[]{:S(2)}) %collective-permute-start) | collective-permute-done | bytes 1081376 | tf_op jit(solution)/shard_map/ppermute | solution.py:243
  13.1 0.8 pack.1
  14.0 33.6 %all_to_all.10.x_ref = bf16[16,272,256]{2,1,0:T(8,128)(2,1)S(1)} all-to-all(bf16[16,272,256]{2,1,0:T(8,128)(2,1)S(1)} %pack.1), channel_id=1, replica_groups=mesh['pat'=16,'seq'=16] {'seq'}, dimensions={0} | all-to-all | bytes 4456448 | tf_op jit(solution)/shard_map/all_to_all | solution.py:253
  47.6 0.1 slice.4
  47.7 1.8 %collective-permute-start.1 = (bf16[16,128,256]{2,1,0:T(8,128)(2,1)S(1)}, bf16[16,128,256]{2,1,0:T(8,128)(2,1)S(1)}, u32[]{:S(2)}, u32[]{:S(2)}) collective-permute-start(bf16[16,128,256]{2,1,0:T(8,128)(2,1)S(1)} %slice.4), channel_id=1, source_target_pairs={{0,16},{16,0},{32,48},{48,32},{64,80},{80,64},{96,112},{112,96},{1... | collective-permute-start | bytes 3145736 | tf_op jit(solution)/shard_map/ppermute | solution.py:254
  49.6 2.3 %collective-permute-done.1.r_ref = bf16[16,128,256]{2,1,0:T(8,128)(2,1)S(1)} collective-permute-done((bf16[16,128,256]{2,1,0:T(8,128)(2,1)S(1)}, bf16[16,128,256]{2,1,0:T(8,128)(2,1)S(1)}, u32[]{:S(2)}, u32[]{:S(2)}) %collective-permute-start.1) | collective-permute-done | bytes 1048608 | tf_op jit(solution)/shard_map/ppermute | solution.py:254
  51.8 24.7 %attention.1 = (bf16[16,192,256]{2,1,0:T(8,128)(2,1)S(1)}, bf16[16,128,256]{2,1,0:T(8,128)(2,1)S(1)}) custom-call(bf16[16,272,256]{2,1,0:T(8,128)(2,1)S(1)} %all_to_all.10.x_ref, bf16[16,128,256]{2,1,0:T(8,128)(2,1)S(1)} %collective-permute-done.1.r_ref), custom_call_target="tpu_custom_call" | custom-call | tf_op jit(solution)/shard_map/attention/pallas_call | solution.py:256
  76.5 0.5 collective-permute-start.2
  77.0 2.3 %collective-permute-done.2.r_ref = bf16[16,128,256]{2,1,0:T(8,128)(2,1)S(1)} collective-permute-done((bf16[16,128,256]{2,1,0:T(8,128)(2,1)S(1)}, bf16[16,128,256]{2,1,0:T(8,128)(2,1)S(1)}, u32[]{:S(2)}, u32[]{:S(2)}) %collective-permute-start.2) | collective-permute-done | bytes 1048608 | tf_op jit(solution)/shard_map/ppermute | solution.py:277
  79.3 1.4 %combine.1 = bf16[16,192,256]{2,1,0:T(8,128)(2,1)} custom-call(bf16[16,192,256]{2,1,0:T(8,128)(2,1)S(1)} %get-tuple-element.9.own_ref, bf16[16,128,256]{2,1,0:T(8,128)(2,1)S(1)} %collective-permute-done.2.r_ref), custom_call_target="tpu_custom_call" | custom-call | tf_op jit(solution)/shard_map/combine/pallas_call | solution.py:278
  80.7 3.7 %all-to-all-start.1 = ((bf16[16,192,256]{2,1,0:T(8,128)(2,1)}), bf16[16,192,256]{2,1,0:T(8,128)(2,1)S(1)}, u32[]{:S(2)}, u32[]{:S(2)}) async-start(bf16[16,192,256]{2,1,0:T(8,128)(2,1)} %combine.1), calls=%async_computation.1 | async-start | bytes 3145728 | tf_op jit(solution)/shard_map/all_to_all | solution.py:286
  84.4 23.6 %all-to-all-done.1.own_ref = bf16[16,192,256]{2,1,0:T(8,128)(2,1)S(1)} async-done(((bf16[16,192,256]{2,1,0:T(8,128)(2,1)}), bf16[16,192,256]{2,1,0:T(8,128)(2,1)S(1)}, u32[]{:S(2)}, u32[]{:S(2)}) %all-to-all-start.1) | async-done | bytes 1572896 | tf_op jit(solution)/shard_map/all_to_all | solution.py:286
  108.0 0.1 constant_dynamic-slice_fusion
  108.1 1.8 %collective-permute-start.3 = (bf16[8,192,256]{2,1,0:T(8,128)(2,1)S(1)}, bf16[8,192,256]{2,1,0:T(8,128)(2,1)S(1)}, u32[]{:S(2)}, u32[]{:S(2)}) collective-permute-start(bf16[8,192,256]{2,1,0:T(8,128)(2,1)S(1)} %constant_dynamic-slice_fusion), channel_id=1, source_target_pairs={{0,16},{16,0},{32,48},{48,32},{64,80},{80,64},{96,112},{112,96},{1... | collective-permute-start | bytes 2359304 | tf_op jit(solution)/shard_map/ppermute | solution.py:288
  109.8 1.9 %collective-permute-done.3.r_ref = bf16[8,192,256]{2,1,0:T(8,128)(2,1)S(1)} collective-permute-done((bf16[8,192,256]{2,1,0:T(8,128)(2,1)S(1)}, bf16[8,192,256]{2,1,0:T(8,128)(2,1)S(1)}, u32[]{:S(2)}, u32[]{:S(2)}) %collective-permute-start.3) | collective-permute-done | bytes 786464 | tf_op jit(solution)/shard_map/ppermute | solution.py:288
  111.7 1.5 %unpack.1 = (bf16[256,1024]{1,0:T(8,128)(2,1)}, bf16[256,1024]{1,0:T(8,128)(2,1)}, bf16[256,1024]{1,0:T(8,128)(2,1)}) custom-call(bf16[16,192,256]{2,1,0:T(8,128)(2,1)S(1)} %all-to-all-done.1.own_ref, bf16[8,192,256]{2,1,0:T(8,128)(2,1)S(1)} %collective-permute-done.3.r_ref), custom_call_target="tpu_custom_call" | custom-call | tf_op jit(solution)/shard_map/unpack/pallas_call | solution.py:289
  (14 shorter events, 0.0 us)
Async XLA Ops:
  1.3 1.0 copy-start
  2.3 1.0 copy-start.2
  3.4 1.0 copy-start.4
  4.4 1.0 copy-start.6
  5.4 0.7 copy-start.8
  6.1 0.7 copy-start.9
  6.8 6.4 %copy-start.1 = (bf16[256,1024]{1,0:T(8,128)(2,1)S(1)}, bf16[256,1024]{1,0:T(8,128)(2,1)}, u32[]{:S(2)}) copy-start(bf16[256,1024]{1,0:T(8,128)(2,1)} %k_ref.3) | copy-start | bytes 1572868
  6.8 6.4 %copy-start.3 = (bf16[256,1024]{1,0:T(8,128)(2,1)S(1)}, bf16[256,1024]{1,0:T(8,128)(2,1)}, u32[]{:S(2)}) copy-start(bf16[256,1024]{1,0:T(8,128)(2,1)} %v_ref.3) | copy-start | bytes 1572868
  6.8 6.4 %copy-start.5 = (bf16[256,1024]{1,0:T(8,128)(2,1)S(1)}, bf16[256,1024]{1,0:T(8,128)(2,1)}, u32[]{:S(2)}) copy-start(bf16[256,1024]{1,0:T(8,128)(2,1)} %q_ref.3) | copy-start | bytes 1572868
  6.8 6.4 %copy-start.7 = (bf16[256,1024]{1,0:T(8,128)(2,1)S(1)}, bf16[256,1024]{1,0:T(8,128)(2,1)}, u32[]{:S(2)}) copy-start(bf16[256,1024]{1,0:T(8,128)(2,1)} %g_ref.3) | copy-start | bytes 1572868
  7.5 5.7 %collective-permute-start = (bf16[528,1024]{1,0:T(8,128)(2,1)S(1)}, bf16[528,1024]{1,0:T(8,128)(2,1)S(1)}, u32[]{:S(2)}, u32[]{:S(2)}) collective-permute-start(bf16[528,1024]{1,0:T(8,128)(2,1)S(1)} %get-tuple-element.7), channel_id=1, source_target_pairs={{0,16},{16,0},{32,48},{48,32},{64,80},{80,64},{96,112},{112,96},{1... | collective-permute-start | bytes 3244040 | tf_op jit(solution)/shard_map/ppermute | solution.py:243
  47.7 4.1 %collective-permute-start.1 = (bf16[16,128,256]{2,1,0:T(8,128)(2,1)S(1)}, bf16[16,128,256]{2,1,0:T(8,128)(2,1)S(1)}, u32[]{:S(2)}, u32[]{:S(2)}) collective-permute-start(bf16[16,128,256]{2,1,0:T(8,128)(2,1)S(1)} %slice.4), channel_id=1, source_target_pairs={{0,16},{16,0},{32,48},{48,32},{64,80},{80,64},{96,112},{112,96},{1... | collective-permute-start | bytes 3145736 | tf_op jit(solution)/shard_map/ppermute | solution.py:254
  76.5 2.7 %collective-permute-start.2 = (bf16[16,128,256]{2,1,0:T(8,128)(2,1)S(1)}, bf16[16,128,256]{2,1,0:T(8,128)(2,1)S(1)}, u32[]{:S(2)}, u32[]{:S(2)}) collective-permute-start(bf16[16,128,256]{2,1,0:T(8,128)(2,1)S(1)} %get-tuple-element.10), channel_id=1, source_target_pairs={{0,16},{16,0},{32,48},{48,32},{64,80},{80,64},{96,112},{112,96},{1... | collective-permute-start | bytes 3145736 | tf_op jit(solution)/shard_map/ppermute | solution.py:277
  80.7 27.3 %all-to-all-start.1 = ((bf16[16,192,256]{2,1,0:T(8,128)(2,1)}), bf16[16,192,256]{2,1,0:T(8,128)(2,1)S(1)}, u32[]{:S(2)}, u32[]{:S(2)}) async-start(bf16[16,192,256]{2,1,0:T(8,128)(2,1)} %combine.1), calls=%async_computation.1 | async-start | bytes 3145728 | tf_op jit(solution)/shard_map/all_to_all | solution.py:286
  108.1 3.7 %collective-permute-start.3 = (bf16[8,192,256]{2,1,0:T(8,128)(2,1)S(1)}, bf16[8,192,256]{2,1,0:T(8,128)(2,1)S(1)}, u32[]{:S(2)}, u32[]{:S(2)}) collective-permute-start(bf16[8,192,256]{2,1,0:T(8,128)(2,1)S(1)} %constant_dynamic-slice_fusion), channel_id=1, source_target_pairs={{0,16},{16,0},{32,48},{48,32},{64,80},{80,64},{96,112},{112,96},{1... | collective-permute-start | bytes 2359304 | tf_op jit(solution)/shard_map/ppermute | solution.py:288

commit v3 on v2

v3 whole, which is shorter than its diff:
```python
import jax
import jax.numpy as jnp
from jax import lax
from jax.experimental import pallas as pl
from jax.experimental.pallas import tpu as pltpu
from jax.sharding import PartitionSpec as P

HEADS = 8
HD = 128
BLK = 128
GLOB = 2
SHARDS = 16
SLOTS = 15
IDS = 16
LIGHT = 4
ROWS = 2 * BLK
META = 16
IN_ROWS = 2 * BLK + META
OUT_ROWS = BLK + BLK // 2
SCALE = HD**-0.5
LOG2E = 1.4426950408889634
MASKED = -1e30
NEAR = 3 + GLOB


def split_kernel(
    pick_hbm, count_ref, ids_hbm, k_ref, v_ref, q_ref, g_ref, out_ref, meta_ref, pick_ref, ids_ref, wide_ref, sems
):
    other = 1 - lax.rem(lax.axis_index("pat"), 2)
    source = pl.ds(pl.multiple_of(other * BLK, BLK), BLK)
    copies = []
    for index, ref in enumerate((k_ref, v_ref, q_ref, g_ref)):
        target = out_ref.at[pl.ds(index * BLK, BLK), :]
        copies.append(pltpu.make_async_copy(ref.at[source, :], target, sems.at[index]))
    tables = [
        pltpu.make_async_copy(pick_hbm, pick_ref, sems.at[4]),
        pltpu.make_async_copy(ids_hbm, ids_ref, sems.at[5]),
    ]
    for copy in tables + copies:
        copy.start()
    for copy in tables:
        copy.wait()
    lanes = lax.broadcasted_iota(jnp.int32, (META, HEADS * HD), 1)
    meta = jnp.where(lanes == SLOTS, count_ref[0], 0)
    for slot in range(SLOTS):
        meta = jnp.where(lanes == slot, pick_ref[0, slot], meta)
    for slot in range(GLOB):
        meta = jnp.where(lanes == IDS + slot, ids_ref[slot], meta)
    meta = meta.astype(jnp.float32).astype(jnp.bfloat16)
    wide_ref[...] = meta
    meta_ref[...] = meta[:, : 2 * HD]
    copies.append(
        pltpu.make_async_copy(wide_ref, out_ref.at[pl.ds(4 * BLK, META), :], sems.at[6])
    )
    copies[-1].start()
    for copy in copies:
        copy.wait()


def pack_kernel(r_ref, meta_ref, k_ref, v_ref, q_ref, g_ref, out_ref, sems):
    core = lax.rem(lax.axis_index("pat"), 2)
    source = pl.ds(pl.multiple_of(core * BLK, BLK), BLK)
    copies = []
    for index, ref in enumerate((k_ref, v_ref, q_ref, g_ref)):
        rows = pl.ds(index // 2 * BLK, BLK)
        lanes = pl.ds(index % 2 * HD, HD)
        for head in range(HEADS):
            target = out_ref.at[core * HEADS + head, rows, lanes]
            origin = ref.at[source, pl.ds(head * HD, HD)]
            copies.append(pltpu.make_async_copy(origin, target, sems.at[index, head]))
    for copy in copies:
        copy.start()
    away = (1 - core) * HEADS
    for head in range(HEADS):
        cols = slice(head * HD, (head + 1) * HD)
        out_ref[away + head, :BLK, :HD] = r_ref[:BLK, cols]
        out_ref[away + head, :BLK, HD:] = r_ref[BLK : 2 * BLK, cols]
        out_ref[away + head, BLK : 2 * BLK, :HD] = r_ref[2 * BLK : 3 * BLK, cols]
        out_ref[away + head, BLK : 2 * BLK, HD:] = r_ref[3 * BLK : 4 * BLK, cols]
        out_ref[away + head, 2 * BLK :, :] = r_ref[4 * BLK :, : 2 * HD]
        out_ref[core * HEADS + head, 2 * BLK :, :] = meta_ref[...]
    for copy in copies:
        copy.wait()


def combine_kernel(own_ref, r_ref, out_ref):
    for shard in range(SHARDS):
        total = own_ref[shard, :BLK, :].astype(jnp.float32) + r_ref[shard].astype(jnp.float32)
        out_ref[shard, :BLK, :] = total.astype(jnp.bfloat16)
        out_ref[shard, BLK:, :] = own_ref[shard, BLK:, :]


def unpack_kernel(own_ref, r_ref, dq_ref, dk_ref, dv_ref):
    core = lax.rem(lax.axis_index("pat"), 2)

    def place(piece, row, cols):
        rows = pl.ds(pl.multiple_of(row, BLK), BLK)
        dk_ref[rows, cols] = piece[:BLK, :HD]
        dv_ref[rows, cols] = piece[:BLK, HD:]
        rows = pl.ds(pl.multiple_of(row, BLK), BLK // 2)
        dq_ref[rows, cols] = piece[BLK:, :HD]
        rows = pl.ds(pl.multiple_of(row + BLK // 2, BLK // 2), BLK // 2)
        dq_ref[rows, cols] = piece[BLK:, HD:]

    for head in range(HEADS):
        cols = slice(head * HD, (head + 1) * HD)
        place(own_ref[core * HEADS + head], core * BLK, cols)
        place(r_ref[head], (1 - core) * BLK, cols)


GROUP = 5


def attention_kernel(
    x_ref, r_ref, o_ref, send_ref, acc, blocks, glob_kv, glob_acc, wmat, kv, sp, gb, meta_v, meta_s, sem
):
    half = lax.rem(lax.axis_index("pat"), 2)
    meta_v[...] = x_ref[:, 2 * BLK, :HD].astype(jnp.float32).astype(jnp.int32)
    copy = pltpu.make_async_copy(meta_v, meta_s, sem)
    copy.start()
    own_rows = pl.ds(pl.multiple_of(half * BLK, BLK), BLK)
    other_rows = pl.ds(pl.multiple_of((1 - half) * BLK, BLK), BLK)
    for shard in range(SHARDS):
        blocks[shard, own_rows, :] = x_ref[shard, :BLK, :]
        blocks[shard, other_rows, :] = r_ref[shard]
    acc[...] = jnp.zeros_like(acc)
    glob_acc[...] = jnp.zeros_like(glob_acc)
    wmat[...] = jnp.zeros_like(wmat)
    copy.wait()
    for slot in range(GLOB):
        block = meta_s[0, IDS + slot]
        glob_kv[slot * BLK : (slot + 1) * BLK, :] = blocks[
            block // 2, pl.ds(pl.multiple_of(lax.rem(block, 2) * BLK, BLK), BLK), :
        ]

    def fold(value, op):
        parts = [value[i * 8 : (i + 1) * 8] for i in range(value.shape[0] // 8)]
        while len(parts) > 1:
            parts = [op(x, y) for x, y in zip(parts[::2], parts[1::2])] + parts[len(parts) // 2 * 2 :]
        return parts[0]

    def process(shards, far, masked):
        chunks = NEAR + far
        length = chunks * BLK
        state = []
        for u, shard in enumerate(shards):
            count = meta_s[shard, SLOTS]
            beside = jnp.where(half == 0, shard - 1, shard + 1)
            valid = (beside >= 0) & (beside < SHARDS)
            beside = jnp.clip(beside, 0, SHARDS - 1)
            bias = {NEAR - 1: jnp.where(valid, 0.0, MASKED)}
            places = []
            for slot in range(far):
                target = lax.rem(shard + 1 + slot, SHARDS)
                pick = meta_s[shard, slot]
                places.append((target, pick))
                if masked and slot:
                    bias[NEAR + slot] = jnp.where(slot < count, 0.0, MASKED)
            state.append((shard, beside, bias, places))
            wmat[u, :BLK, :HD] = x_ref[shard, BLK : 2 * BLK, :HD]
            wmat[u, BLK:, HD:] = x_ref[shard, BLK : 2 * BLK, HD:]
            kv[u, :ROWS, :] = blocks[shard]
            kv[u, ROWS : 2 * ROWS, :] = glob_kv[...]
            kv[u, 2 * ROWS : 2 * ROWS + BLK, :] = blocks[beside, other_rows, :]
            for slot, (target, pick) in enumerate(places):
                rows = pl.ds(pl.multiple_of(pick * BLK, BLK), BLK)
                kv[u, (NEAR + slot) * BLK : (NEAR + slot + 1) * BLK, :] = blocks[target, rows, :]
            sp[u, :length, :] = lax.dot_general(
                kv[u, :length, :], wmat[u], (((1,), (1,)), ((), ())), preferred_element_type=jnp.float32
            )
        for u, (shard, beside, bias, places) in enumerate(state):
            peak = None
            for chunk in range(chunks):
                high = fold(sp[u, chunk * BLK : (chunk + 1) * BLK, :HD], jnp.maximum)
                if chunk in bias:
                    high = high + bias[chunk]
                peak = high if peak is None else jnp.maximum(peak, high)
            peak = jnp.max(peak, axis=0, keepdims=True) * (SCALE * LOG2E)
            peaks = {chunk: peak - bias[chunk] if chunk in bias else peak for chunk in range(chunks)}
            total = jnp.zeros((8, HD), jnp.float32)
            delta = jnp.zeros((8, HD), jnp.float32)
            for chunk in range(chunks):
                rows = slice(chunk * BLK, (chunk + 1) * BLK)
                weights = jnp.exp2(sp[u, rows, :HD] * (SCALE * LOG2E) - peaks[chunk])
                sp[u, rows, :HD] = weights
                total = total + fold(weights, jnp.add)
                delta = delta + fold(weights * sp[u, rows, HD:], jnp.add)
            inverse = 1.0 / jnp.sum(total, axis=0, keepdims=True)
            delta = jnp.sum(delta, axis=0, keepdims=True) * inverse
            inverse_scaled = inverse * SCALE
            for chunk in range(chunks):
                rows = slice(chunk * BLK, (chunk + 1) * BLK)
                weights = sp[u, rows, :HD]
                gb[u, rows, HD:] = (weights * inverse).astype(jnp.bfloat16)
                gb[u, rows, :HD] = (
                    (weights * inverse_scaled) * (sp[u, rows, HD:] - delta)
                ).astype(jnp.bfloat16)
            grad_query = lax.dot_general(
                gb[u, :length, :HD],
                kv[u, :length, :HD],
                (((0,), (0,)), ((), ())),
                preferred_element_type=jnp.float32,
            ).astype(jnp.bfloat16)
            o_ref[shard, BLK:, :HD] = grad_query[: BLK // 2]
            o_ref[shard, BLK:, HD:] = grad_query[BLK // 2 :]
            grads = jnp.dot(gb[u, :length, :], wmat[u], preferred_element_type=jnp.float32)
            acc[shard, :, :] += grads[:ROWS]
            glob_acc[...] += grads[ROWS : 2 * ROWS]
            acc[beside, other_rows, :] += grads[2 * ROWS : 2 * ROWS + BLK]
            for slot, (target, pick) in enumerate(places):
                rows = pl.ds(pl.multiple_of(pick * BLK, BLK), BLK)
                acc[target, rows, :] += grads[(NEAR + slot) * BLK : (NEAR + slot + 1) * BLK]

    busy = 0
    for shard in range(SHARDS):
        busy = jnp.where(meta_s[shard, SLOTS] > LIGHT, shard, busy)

    def light_step(step, carry):
        places = [step * GROUP + u for u in range(GROUP)]
        process([place + jnp.where(place >= busy, 1, 0) for place in places], LIGHT, True)
        return carry

    lax.fori_loop(0, (SHARDS - 1) // GROUP, light_step, 0)
    process([busy], SLOTS, False)
    for slot in range(GLOB):
        block = meta_s[0, IDS + slot]
        rows = pl.ds(pl.multiple_of(lax.rem(block, 2) * BLK, BLK), BLK)
        acc[block // 2, rows, :] += glob_acc[slot * BLK : (slot + 1) * BLK, :]

    def store_step(shard, carry):
        o_ref[shard, :BLK, :] = acc[shard, own_rows, :].astype(jnp.bfloat16)
        send_ref[shard, :, :] = acc[shard, other_rows, :].astype(jnp.bfloat16)
        return carry

    lax.fori_loop(0, SHARDS, store_step, 0)


VMEM = pl.BlockSpec(memory_space=pltpu.VMEM)
SMEM = pl.BlockSpec(memory_space=pltpu.SMEM)
ANY = pl.BlockSpec(memory_space=pl.ANY)


def kernel_params(megabytes):
    return pltpu.CompilerParams(vmem_limit_bytes=megabytes << 20)


def bf16(*shape):
    return jax.ShapeDtypeStruct(shape, jnp.bfloat16)


def attention(received, other):
    longest = (NEAR + SLOTS) * BLK
    return pl.pallas_call(
        attention_kernel,
        out_shape=(bf16(SHARDS, OUT_ROWS, 2 * HD), bf16(SHARDS, BLK, 2 * HD)),
        in_specs=[VMEM, VMEM],
        out_specs=(VMEM, VMEM),
        scratch_shapes=[
            pltpu.VMEM((SHARDS, ROWS, 2 * HD), jnp.float32),
            pltpu.VMEM((SHARDS, ROWS, 2 * HD), jnp.bfloat16),
            pltpu.VMEM((GLOB * BLK, 2 * HD), jnp.bfloat16),
            pltpu.VMEM((GLOB * BLK, 2 * HD), jnp.float32),
            pltpu.VMEM((GROUP, 2 * BLK, 2 * HD), jnp.bfloat16),
            pltpu.VMEM((GROUP, longest, 2 * HD), jnp.bfloat16),
            pltpu.VMEM((GROUP, longest, 2 * HD), jnp.float32),
            pltpu.VMEM((GROUP, longest, 2 * HD), jnp.bfloat16),
            pltpu.VMEM((SHARDS, HD), jnp.int32),
            pltpu.SMEM((SHARDS, HD), jnp.int32),
            pltpu.SemaphoreType.DMA,
        ],
        compiler_params=kernel_params(40),
        name="attention",
    )(received, other)


def body(query_matrix, key_rows, value_rows, output_gradient_rows, far_pick, far_count, global_ids):
    width = HEADS * HD
    core = lax.rem(lax.axis_index("pat"), 2)
    arrays = (key_rows, value_rows, query_matrix, output_gradient_rows)
    pairs = [(i, i ^ 1) for i in range(lax.axis_size("pat"))]
    away, meta = pl.pallas_call(
        split_kernel,
        out_shape=(bf16(4 * BLK + META, width), bf16(META, 2 * HD)),
        in_specs=[ANY, SMEM, ANY, ANY, ANY, ANY, ANY],
        out_specs=(ANY, VMEM),
        scratch_shapes=[
            pltpu.SMEM((1, SLOTS), jnp.int32),
            pltpu.SMEM((GLOB,), jnp.int32),
            pltpu.VMEM((META, HEADS * HD), jnp.bfloat16),
            pltpu.SemaphoreType.DMA((7,)),
        ],
        compiler_params=kernel_params(60),
        name="split",
    )(far_pick, far_count, global_ids, *arrays)
    arrived = lax.ppermute(away, "pat", pairs)
    sent = pl.pallas_call(
        pack_kernel,
        out_shape=bf16(SHARDS, IN_ROWS, 2 * HD),
        in_specs=[VMEM, VMEM, ANY, ANY, ANY, ANY],
        out_specs=VMEM,
        scratch_shapes=[pltpu.SemaphoreType.DMA((4, HEADS))],
        compiler_params=kernel_params(16),
        name="pack",
    )(arrived, meta, *arrays)
    received = lax.all_to_all(sent, "seq", split_axis=0, concat_axis=0, tiled=True)
    other = lax.ppermute(received[:, :BLK, :], "pat", pairs)
    own, partial = attention(received, other)
    partial = lax.ppermute(partial, "pat", pairs)
    combined = pl.pallas_call(
        combine_kernel,
        out_shape=bf16(SHARDS, OUT_ROWS, 2 * HD),
        in_specs=[VMEM, VMEM],
        out_specs=VMEM,
        compiler_params=kernel_params(16),
        name="combine",
    )(own, partial)
    foreign_at = (1 - core) * HEADS
    combined, foreign_at = lax.optimization_barrier((combined, foreign_at))
    returned = lax.all_to_all(combined, "seq", split_axis=0, concat_axis=0, tiled=True)
    foreign = lax.dynamic_slice_in_dim(returned, foreign_at, HEADS, axis=0)
    foreign = lax.ppermute(foreign, "pat", pairs)
    return pl.pallas_call(
        unpack_kernel,
        out_shape=(bf16(ROWS, width),) * 3,
        in_specs=[VMEM, VMEM],
        out_specs=(VMEM, VMEM, VMEM),
        compiler_params=kernel_params(16),
        name="unpack",
    )(returned, foreign)


def solution(mesh):
    rows = P(("pat", "seq"), None)
    in_specs = (rows, rows, rows, rows, rows, P("seq"), P("pat"))
    return jax.shard_map(
        body, mesh=mesh, in_specs=in_specs, out_specs=(rows, rows, rows), check_vma=False
    )
```

time: 114 us -> 134 us (1.18)
  Pallas kernels: 29.1 us -> 53.4 us
  local copies, waits for them, and re-layouts: 5.63 us -> 0.85 us
    pallas_call x1, Pallas kernels: 0.69 us -> 33.5 us  [body(): pl.pallas_call(split_kernel, out_shape=(bf16(4 * BLK + META, width), bf16...]
    pallas_call x1, Pallas kernels: 24.7 us -> 16.2 us  [attention(): pl.pallas_call(attention_kernel, out_shape=(bf16(SHARDS, OUT_ROWS, 2 * HD...]
    unnamed x20 -> x10, local copies, waits for them, and re-layouts: 5.48 us -> 0.71 us
where the time goes in v3:
time: 134 us; the launch traced here: 133 us
  Pallas kernels  53.4 us (40%)
  blocking collectives  33.6 us (25%)
  waiting for transfers between devices  32.8 us (24%)
  starting transfers between devices  11.1 us (8%)
  between operations  1.52 us (1%)
    all_to_all x1, blocking collectives, body(): lax.all_to_all(sent, 'seq', split_axis=0, concat_axis=0, tiled=True)  33.6 us
    pallas_call x1, Pallas kernels, body(): pl.pallas_call(split_kernel, out_shape=(bf16(4 * BLK + META, width), bf16...  33.5 us
    all_to_all x1, waiting for transfers between devices, body(): lax.all_to_all(combined, 'seq', split_axis=0, concat_axis=0, tiled=True)  23.6 us
    pallas_call x1, Pallas kernels, attention(): pl.pallas_call(attention_kernel, out_shape=(bf16(SHARDS, OUT_ROWS, 2 * HD...  16.2 us
    all_to_all x1, starting transfers between devices, body(): lax.all_to_all(combined, 'seq', split_axis=0, concat_axis=0, tiled=True)  3.71 us
    ppermute x1, starting transfers between devices, body(): arrived = lax.ppermute(away, 'pat', pairs)  3.33 us
  transfers between devices with their start and end apart: 5, of which 5 were waited for; matrix products, arithmetic and copies ran while one was open for 0% of the time, Pallas kernels for 0%

profile of v3, /device:TPU:1, one launch (start us, length us, event | category | flops | bytes accessed | tf_op | source)
XLA Modules:
  0.0 133.3 jit_solution(14182767938671615107)
XLA Ops:
  0.6 0.0 copy-start
  0.6 0.0 copy-start.1
  0.7 0.0 copy-start.2
  1.5 33.5 %split.1 = (bf16[528,1024]{1,0:T(8,128)(2,1)}, bf16[16,256]{1,0:T(8,128)(2,1)}) custom-call(s32[1,15]{1,0:T(1,128)} %pick_hbm.1, s32[1]{0:T(128)S(6)} %copy.10.count_ref, s32[2]{0:T(128)} %ids_hbm.1, bf16[256,1024]{1,0:T(8,128)(2,1)} %k_ref.3, bf16[256,1024]{1,0:T(8,128)(2,1)} %v_ref.3, bf16[256,1024]{1,0:T(8,128)(2,1)} %q_ref.3, bf16[256,1024]{1,0:T(8,128)(2,1)} %g_ref.3), custom_call_target="tpu_custom_call" | custom-call | tf_op jit(solution)/shard_map/split/pallas_call | solution.py:281
  35.0 3.3 %collective-permute-start = (bf16[528,1024]{1,0:T(8,128)(2,1)}, bf16[528,1024]{1,0:T(8,128)(2,1)S(1)}, u32[]{:S(2)}, u32[]{:S(2)}) collective-permute-start(bf16[528,1024]{1,0:T(8,128)(2,1)} %get-tuple-element.9), channel_id=1, source_target_pairs={{0,16},{16,0},{32,48},{48,32},{64,80},{80,64},{96,112},{112,96},{1... | collective-permute-start | bytes 3244040 | tf_op jit(solution)/shard_map/ppermute | solution.py:295
  38.3 2.5 %collective-permute-done.r_ref = bf16[528,1024]{1,0:T(8,128)(2,1)S(1)} collective-permute-done((bf16[528,1024]{1,0:T(8,128)(2,1)}, bf16[528,1024]{1,0:T(8,128)(2,1)S(1)}, u32[]{:S(2)}, u32[]{:S(2)}) %collective-permute-start) | collective-permute-done | bytes 1081376 | tf_op jit(solution)/shard_map/ppermute | solution.py:295
  40.9 0.0 copy-done.1
  40.9 0.0 copy-start.4
  40.9 0.7 copy-done.4
  41.6 0.8 pack.1
  42.4 33.6 %all_to_all.10.x_ref = bf16[16,272,256]{2,1,0:T(8,128)(2,1)S(1)} all-to-all(bf16[16,272,256]{2,1,0:T(8,128)(2,1)S(1)} %pack.1), channel_id=1, replica_groups=mesh['pat'=16,'seq'=16] {'seq'}, dimensions={0} | all-to-all | bytes 4456448 | tf_op jit(solution)/shard_map/all_to_all | solution.py:305
  76.1 0.1 slice.4
  76.2 1.8 %collective-permute-start.1 = (bf16[16,128,256]{2,1,0:T(8,128)(2,1)S(1)}, bf16[16,128,256]{2,1,0:T(8,128)(2,1)S(1)}, u32[]{:S(2)}, u32[]{:S(2)}) collective-permute-start(bf16[16,128,256]{2,1,0:T(8,128)(2,1)S(1)} %slice.4), channel_id=1, source_target_pairs={{0,16},{16,0},{32,48},{48,32},{64,80},{80,64},{96,112},{112,96},{1... | collective-permute-start | bytes 3145736 | tf_op jit(solution)/shard_map/ppermute | solution.py:306
  78.0 2.3 %collective-permute-done.1.r_ref = bf16[16,128,256]{2,1,0:T(8,128)(2,1)S(1)} collective-permute-done((bf16[16,128,256]{2,1,0:T(8,128)(2,1)S(1)}, bf16[16,128,256]{2,1,0:T(8,128)(2,1)S(1)}, u32[]{:S(2)}, u32[]{:S(2)}) %collective-permute-start.1) | collective-permute-done | bytes 1048608 | tf_op jit(solution)/shard_map/ppermute | solution.py:306
  80.3 16.2 %attention.1 = (bf16[16,192,256]{2,1,0:T(8,128)(2,1)S(1)}, bf16[16,128,256]{2,1,0:T(8,128)(2,1)}) custom-call(bf16[16,272,256]{2,1,0:T(8,128)(2,1)S(1)} %all_to_all.10.x_ref, bf16[16,128,256]{2,1,0:T(8,128)(2,1)S(1)} %collective-permute-done.1.r_ref), custom_call_target="tpu_custom_call" | custom-call | tf_op jit(solution)/shard_map/attention/pallas_call | solution.py:253
  96.4 0.5 collective-permute-start.2
  96.9 2.5 %collective-permute-done.2.r_ref = bf16[16,128,256]{2,1,0:T(8,128)(2,1)S(1)} collective-permute-done((bf16[16,128,256]{2,1,0:T(8,128)(2,1)}, bf16[16,128,256]{2,1,0:T(8,128)(2,1)S(1)}, u32[]{:S(2)}, u32[]{:S(2)}) %collective-permute-start.2) | collective-permute-done | bytes 1048608 | tf_op jit(solution)/shard_map/ppermute | solution.py:308
  99.4 1.4 %combine.1 = bf16[16,192,256]{2,1,0:T(8,128)(2,1)} custom-call(bf16[16,192,256]{2,1,0:T(8,128)(2,1)S(1)} %get-tuple-element.11.own_ref, bf16[16,128,256]{2,1,0:T(8,128)(2,1)S(1)} %collective-permute-done.2.r_ref), custom_call_target="tpu_custom_call" | custom-call | tf_op jit(solution)/shard_map/combine/pallas_call | solution.py:309
  100.8 3.7 %all-to-all-start.1 = ((bf16[16,192,256]{2,1,0:T(8,128)(2,1)}), bf16[16,192,256]{2,1,0:T(8,128)(2,1)S(1)}, u32[]{:S(2)}, u32[]{:S(2)}) async-start(bf16[16,192,256]{2,1,0:T(8,128)(2,1)} %combine.1), calls=%async_computation.1 | async-start | bytes 3145728 | tf_op jit(solution)/shard_map/all_to_all | solution.py:319
  104.5 23.6 %all-to-all-done.1.own_ref = bf16[16,192,256]{2,1,0:T(8,128)(2,1)S(1)} async-done(((bf16[16,192,256]{2,1,0:T(8,128)(2,1)}), bf16[16,192,256]{2,1,0:T(8,128)(2,1)S(1)}, u32[]{:S(2)}, u32[]{:S(2)}) %all-to-all-start.1) | async-done | bytes 1572896 | tf_op jit(solution)/shard_map/all_to_all | solution.py:319
  128.1 0.1 constant_dynamic-slice_fusion
  128.2 1.8 %collective-permute-start.3 = (bf16[8,192,256]{2,1,0:T(8,128)(2,1)S(1)}, bf16[8,192,256]{2,1,0:T(8,128)(2,1)S(1)}, u32[]{:S(2)}, u32[]{:S(2)}) collective-permute-start(bf16[8,192,256]{2,1,0:T(8,128)(2,1)S(1)} %constant_dynamic-slice_fusion), channel_id=1, source_target_pairs={{0,16},{16,0},{32,48},{48,32},{64,80},{80,64},{96,112},{112,96},{1... | collective-permute-start | bytes 2359304 | tf_op jit(solution)/shard_map/ppermute | solution.py:321
  129.9 1.9 %collective-permute-done.3.r_ref = bf16[8,192,256]{2,1,0:T(8,128)(2,1)S(1)} collective-permute-done((bf16[8,192,256]{2,1,0:T(8,128)(2,1)S(1)}, bf16[8,192,256]{2,1,0:T(8,128)(2,1)S(1)}, u32[]{:S(2)}, u32[]{:S(2)}) %collective-permute-start.3) | collective-permute-done | bytes 786464 | tf_op jit(solution)/shard_map/ppermute | solution.py:321
  131.8 1.5 %unpack.1 = (bf16[256,1024]{1,0:T(8,128)(2,1)}, bf16[256,1024]{1,0:T(8,128)(2,1)}, bf16[256,1024]{1,0:T(8,128)(2,1)}) custom-call(bf16[16,192,256]{2,1,0:T(8,128)(2,1)S(1)} %all-to-all-done.1.own_ref, bf16[8,192,256]{2,1,0:T(8,128)(2,1)S(1)} %collective-permute-done.3.r_ref), custom_call_target="tpu_custom_call" | custom-call | tf_op jit(solution)/shard_map/unpack/pallas_call | solution.py:322
  (4 shorter events, 0.0 us)
Async XLA Ops:
  0.6 40.3 %copy-start = (bf16[256,1024]{1,0:T(8,128)(2,1)S(1)}, bf16[256,1024]{1,0:T(8,128)(2,1)}, u32[]{:S(2)}) copy-start(bf16[256,1024]{1,0:T(8,128)(2,1)} %k_ref.3) | copy-start | bytes 1572868
  0.6 40.2 %copy-start.1 = (bf16[256,1024]{1,0:T(8,128)(2,1)S(1)}, bf16[256,1024]{1,0:T(8,128)(2,1)}, u32[]{:S(2)}) copy-start(bf16[256,1024]{1,0:T(8,128)(2,1)} %v_ref.3) | copy-start | bytes 1572868
  0.7 40.2 %copy-start.2 = (bf16[256,1024]{1,0:T(8,128)(2,1)S(1)}, bf16[256,1024]{1,0:T(8,128)(2,1)}, u32[]{:S(2)}) copy-start(bf16[256,1024]{1,0:T(8,128)(2,1)} %q_ref.3) | copy-start | bytes 1572868
  0.7 40.2 %copy-start.3 = (bf16[256,1024]{1,0:T(8,128)(2,1)S(1)}, bf16[256,1024]{1,0:T(8,128)(2,1)}, u32[]{:S(2)}) copy-start(bf16[256,1024]{1,0:T(8,128)(2,1)} %g_ref.3) | copy-start | bytes 1572868
  35.0 5.9 %collective-permute-start = (bf16[528,1024]{1,0:T(8,128)(2,1)}, bf16[528,1024]{1,0:T(8,128)(2,1)S(1)}, u32[]{:S(2)}, u32[]{:S(2)}) collective-permute-start(bf16[528,1024]{1,0:T(8,128)(2,1)} %get-tuple-element.9), channel_id=1, source_target_pairs={{0,16},{16,0},{32,48},{48,32},{64,80},{80,64},{96,112},{112,96},{1... | collective-permute-start | bytes 3244040 | tf_op jit(solution)/shard_map/ppermute | solution.py:295
  40.9 0.7 copy-start.4
  76.2 4.1 %collective-permute-start.1 = (bf16[16,128,256]{2,1,0:T(8,128)(2,1)S(1)}, bf16[16,128,256]{2,1,0:T(8,128)(2,1)S(1)}, u32[]{:S(2)}, u32[]{:S(2)}) collective-permute-start(bf16[16,128,256]{2,1,0:T(8,128)(2,1)S(1)} %slice.4), channel_id=1, source_target_pairs={{0,16},{16,0},{32,48},{48,32},{64,80},{80,64},{96,112},{112,96},{1... | collective-permute-start | bytes 3145736 | tf_op jit(solution)/shard_map/ppermute | solution.py:306
  96.4 3.0 %collective-permute-start.2 = (bf16[16,128,256]{2,1,0:T(8,128)(2,1)}, bf16[16,128,256]{2,1,0:T(8,128)(2,1)S(1)}, u32[]{:S(2)}, u32[]{:S(2)}) collective-permute-start(bf16[16,128,256]{2,1,0:T(8,128)(2,1)} %get-tuple-element.12), channel_id=1, source_target_pairs={{0,16},{16,0},{32,48},{48,32},{64,80},{80,64},{96,112},{112,96},{1... | collective-permute-start | bytes 3145736 | tf_op jit(solution)/shard_map/ppermute | solution.py:308
  100.8 27.3 %all-to-all-start.1 = ((bf16[16,192,256]{2,1,0:T(8,128)(2,1)}), bf16[16,192,256]{2,1,0:T(8,128)(2,1)S(1)}, u32[]{:S(2)}, u32[]{:S(2)}) async-start(bf16[16,192,256]{2,1,0:T(8,128)(2,1)} %combine.1), calls=%async_computation.1 | async-start | bytes 3145728 | tf_op jit(solution)/shard_map/all_to_all | solution.py:319
  128.2 3.7 %collective-permute-start.3 = (bf16[8,192,256]{2,1,0:T(8,128)(2,1)S(1)}, bf16[8,192,256]{2,1,0:T(8,128)(2,1)S(1)}, u32[]{:S(2)}, u32[]{:S(2)}) collective-permute-start(bf16[8,192,256]{2,1,0:T(8,128)(2,1)S(1)} %constant_dynamic-slice_fusion), channel_id=1, source_target_pairs={{0,16},{16,0},{32,48},{48,32},{64,80},{80,64},{96,112},{112,96},{1... | collective-permute-start | bytes 2359304 | tf_op jit(solution)/shard_map/ppermute | solution.py:321

commit v4 on v3

--- a/solution.py
+++ b/solution.py
@@ -24,7 +24,7 @@
 
 
 def split_kernel(
-    pick_hbm, count_ref, ids_hbm, k_ref, v_ref, q_ref, g_ref, out_ref, meta_ref, pick_ref, ids_ref, wide_ref, sems
+    pick_hbm, count_ref, ids_hbm, k_ref, v_ref, q_ref, g_ref, out_ref, meta_ref, pick_ref, ids_ref, sems
 ):
     other = 1 - lax.rem(lax.axis_index("pat"), 2)
     source = pl.ds(pl.multiple_of(other * BLK, BLK), BLK)
@@ -47,12 +47,8 @@
     for slot in range(GLOB):
         meta = jnp.where(lanes == IDS + slot, ids_ref[slot], meta)
     meta = meta.astype(jnp.float32).astype(jnp.bfloat16)
-    wide_ref[...] = meta
+    out_ref[4 * BLK :, :] = meta
     meta_ref[...] = meta[:, : 2 * HD]
-    copies.append(
-        pltpu.make_async_copy(wide_ref, out_ref.at[pl.ds(4 * BLK, META), :], sems.at[6])
-    )
-    copies[-1].start()
     for copy in copies:
         copy.wait()
 
@@ -282,12 +278,11 @@
         split_kernel,
         out_shape=(bf16(4 * BLK + META, width), bf16(META, 2 * HD)),
         in_specs=[ANY, SMEM, ANY, ANY, ANY, ANY, ANY],
-        out_specs=(ANY, VMEM),
+        out_specs=(VMEM, VMEM),
         scratch_shapes=[
             pltpu.SMEM((1, SLOTS), jnp.int32),
             pltpu.SMEM((GLOB,), jnp.int32),
-            pltpu.VMEM((META, HEADS * HD), jnp.bfloat16),
-            pltpu.SemaphoreType.DMA((7,)),
+            pltpu.SemaphoreType.DMA((6,)),
         ],
         compiler_params=kernel_params(60),
         name="split",
@@ -314,7 +309,7 @@
         compiler_params=kernel_params(16),
         name="combine",
     )(own, partial)
-    foreign_at = (1 - core) * HEADS
+    foreign_at = ((1 - core) * HEADS).astype(jnp.uint32)
     combined, foreign_at = lax.optimization_barrier((combined, foreign_at))
     returned = lax.all_to_all(combined, "seq", split_axis=0, concat_axis=0, tiled=True)
     foreign = lax.dynamic_slice_in_dim(returned, foreign_at, HEADS, axis=0)

time: 134 us -> 98.9 us (0.74)
  Pallas kernels: 53.4 us -> 20.9 us
  blocking collectives: 33.6 us -> 58.3 us
  waiting for transfers between devices: 32.8 us -> 9.24 us
  starting transfers between devices: 11.1 us -> 7.79 us
    pallas_call x1, Pallas kernels: 33.5 us -> 2.24 us  [body(): pl.pallas_call(split_kernel, out_shape=(bf16(4 * BLK + META, width), bf16...]
    all_to_all x0 -> x1, blocking collectives: none -> 24.7 us  [body(): lax.all_to_all(combined, 'seq', split_axis=0, concat_axis=0, tiled=True)]
    all_to_all x1 -> x0, waiting for transfers between devices: 23.6 us -> none  [body(): lax.all_to_all(combined, 'seq', split_axis=0, concat_axis=0, tiled=True)]
    all_to_all x1 -> x0, starting transfers between devices: 3.71 us -> none  [body(): lax.all_to_all(combined, 'seq', split_axis=0, concat_axis=0, tiled=True)]
  transfers between devices with their start and end apart: 5 -> 4, of which waited for: 5 -> 4; matrix products, arithmetic and copies ran while one was open for 0% -> 0% of each run, Pallas kernels for 0% -> 0%
where the time goes in v4:
time: 98.9 us; the launch traced here: 98.7 us
  blocking collectives  58.3 us (59%)
  Pallas kernels  20.9 us (21%)
  waiting for transfers between devices  9.24 us (9%)
  starting transfers between devices  7.79 us (8%)
  between operations  1.51 us (2%)
    all_to_all x1, blocking collectives, body(): lax.all_to_all(sent, 'seq', split_axis=0, concat_axis=0, tiled=True)  33.6 us
    all_to_all x1, blocking collectives, body(): lax.all_to_all(combined, 'seq', split_axis=0, concat_axis=0, tiled=True)  24.7 us
    pallas_call x1, Pallas kernels, attention(): pl.pallas_call(attention_kernel, out_shape=(bf16(SHARDS, OUT_ROWS, 2 * HD...  16.2 us
    ppermute x1, starting transfers between devices, body(): arrived = lax.ppermute(away, 'pat', pairs)  3.33 us
    ppermute x1, waiting for transfers between devices, body(): arrived = lax.ppermute(away, 'pat', pairs)  2.54 us
    ppermute x1, waiting for transfers between devices, body(): partial = lax.ppermute(partial, 'pat', pairs)  2.5 us
    ppermute x1, waiting for transfers between devices, body(): other = lax.ppermute(received[:, :BLK, :], 'pat', pairs)  2.29 us
    pallas_call x1, Pallas kernels, body(): pl.pallas_call(split_kernel, out_shape=(bf16(4 * BLK + META, width), bf16...  2.24 us
  transfers between devices with their start and end apart: 4, of which 4 were waited for; matrix products, arithmetic and copies ran while one was open for 0% of the time, Pallas kernels for 0%

profile of v4, /device:TPU:1, one launch (start us, length us, event | category | flops | bytes accessed | tf_op | source)
XLA Modules:
  0.0 98.7 jit_solution(6770243760030462714)
XLA Ops:
  0.6 0.0 copy-start
  0.6 0.0 copy-start.1
  0.7 0.0 copy-start.2
  0.7 0.0 copy-start.3
  1.5 2.2 %split.1 = (bf16[528,1024]{1,0:T(8,128)(2,1)}, bf16[16,256]{1,0:T(8,128)(2,1)}) custom-call(s32[1,15]{1,0:T(1,128)} %pick_hbm.1, s32[1]{0:T(128)S(6)} %copy.10.count_ref, s32[2]{0:T(128)} %ids_hbm.1, bf16[256,1024]{1,0:T(8,128)(2,1)} %k_ref.3, bf16[256,1024]{1,0:T(8,128)(2,1)} %v_ref.3, bf16[256,1024]{1,0:T(8,128)(2,1)} %q_ref.3, bf16[256,1024]{1,0:T(8,128)(2,1)} %g_ref.3), custom_call_target="tpu_custom_call" | custom-call | tf_op jit(solution)/shard_map/split/pallas_call | solution.py:277
  3.7 3.3 %collective-permute-start = (bf16[528,1024]{1,0:T(8,128)(2,1)}, bf16[528,1024]{1,0:T(8,128)(2,1)S(1)}, u32[]{:S(2)}, u32[]{:S(2)}) collective-permute-start(bf16[528,1024]{1,0:T(8,128)(2,1)} %get-tuple-element.9), channel_id=1, source_target_pairs={{0,16},{16,0},{32,48},{48,32},{64,80},{80,64},{96,112},{112,96},{1... | collective-permute-start | bytes 3244040 | tf_op jit(solution)/shard_map/ppermute | solution.py:290
  7.0 2.5 %collective-permute-done.r_ref = bf16[528,1024]{1,0:T(8,128)(2,1)S(1)} collective-permute-done((bf16[528,1024]{1,0:T(8,128)(2,1)}, bf16[528,1024]{1,0:T(8,128)(2,1)S(1)}, u32[]{:S(2)}, u32[]{:S(2)}) %collective-permute-start) | collective-permute-done | bytes 1081376 | tf_op jit(solution)/shard_map/ppermute | solution.py:290
  9.6 0.0 copy-done.3
  9.6 0.0 copy-start.4
  9.6 0.7 copy-done.4
  10.3 0.8 pack.1
  11.1 33.6 %all_to_all.10.x_ref = bf16[16,272,256]{2,1,0:T(8,128)(2,1)S(1)} all-to-all(bf16[16,272,256]{2,1,0:T(8,128)(2,1)S(1)} %pack.1), channel_id=1, replica_groups=mesh['pat'=16,'seq'=16] {'seq'}, dimensions={0} | all-to-all | bytes 4456448 | tf_op jit(solution)/shard_map/all_to_all | solution.py:300
  44.8 0.1 slice.4
  44.9 1.8 %collective-permute-start.1 = (bf16[16,128,256]{2,1,0:T(8,128)(2,1)S(1)}, bf16[16,128,256]{2,1,0:T(8,128)(2,1)S(1)}, u32[]{:S(2)}, u32[]{:S(2)}) collective-permute-start(bf16[16,128,256]{2,1,0:T(8,128)(2,1)S(1)} %slice.4), channel_id=1, source_target_pairs={{0,16},{16,0},{32,48},{48,32},{64,80},{80,64},{96,112},{112,96},{1... | collective-permute-start | bytes 3145736 | tf_op jit(solution)/shard_map/ppermute | solution.py:301
  46.7 2.3 %collective-permute-done.1.r_ref = bf16[16,128,256]{2,1,0:T(8,128)(2,1)S(1)} collective-permute-done((bf16[16,128,256]{2,1,0:T(8,128)(2,1)S(1)}, bf16[16,128,256]{2,1,0:T(8,128)(2,1)S(1)}, u32[]{:S(2)}, u32[]{:S(2)}) %collective-permute-start.1) | collective-permute-done | bytes 1048608 | tf_op jit(solution)/shard_map/ppermute | solution.py:301
  49.0 16.2 %attention.1 = (bf16[16,192,256]{2,1,0:T(8,128)(2,1)S(1)}, bf16[16,128,256]{2,1,0:T(8,128)(2,1)}) custom-call(bf16[16,272,256]{2,1,0:T(8,128)(2,1)S(1)} %all_to_all.10.x_ref, bf16[16,128,256]{2,1,0:T(8,128)(2,1)S(1)} %collective-permute-done.1.r_ref), custom_call_target="tpu_custom_call" | custom-call | tf_op jit(solution)/shard_map/attention/pallas_call | solution.py:249
  65.1 0.5 collective-permute-start.2
  65.6 2.5 %collective-permute-done.2.r_ref = bf16[16,128,256]{2,1,0:T(8,128)(2,1)S(1)} collective-permute-done((bf16[16,128,256]{2,1,0:T(8,128)(2,1)}, bf16[16,128,256]{2,1,0:T(8,128)(2,1)S(1)}, u32[]{:S(2)}, u32[]{:S(2)}) %collective-permute-start.2) | collective-permute-done | bytes 1048608 | tf_op jit(solution)/shard_map/ppermute | solution.py:303
  68.1 0.2 combine.1
  68.3 24.7 %all_to_all.11.own_ref = bf16[16,192,256]{2,1,0:T(8,128)(2,1)S(1)} all-to-all(bf16[16,192,256]{2,1,0:T(8,128)(2,1)S(1)} %combine.1), channel_id=1, replica_groups=mesh['pat'=16,'seq'=16] {'seq'}, dimensions={0} | all-to-all | bytes 3145728 | tf_op jit(solution)/shard_map/all_to_all | solution.py:314
  93.0 0.1 constant_dynamic-slice_fusion
  93.1 2.2 %collective-permute-start.3 = (bf16[8,192,256]{2,1,0:T(8,128)(2,1)S(1)}, bf16[8,192,256]{2,1,0:T(8,128)(2,1)S(1)}, u32[]{:S(2)}, u32[]{:S(2)}) collective-permute-start(bf16[8,192,256]{2,1,0:T(8,128)(2,1)S(1)} %constant_dynamic-slice_fusion), channel_id=1, source_target_pairs={{0,16},{16,0},{32,48},{48,32},{64,80},{80,64},{96,112},{112,96},{1... | collective-permute-start | bytes 2359304 | tf_op jit(solution)/shard_map/ppermute | solution.py:316
  95.3 1.9 %collective-permute-done.3.r_ref = bf16[8,192,256]{2,1,0:T(8,128)(2,1)S(1)} collective-permute-done((bf16[8,192,256]{2,1,0:T(8,128)(2,1)S(1)}, bf16[8,192,256]{2,1,0:T(8,128)(2,1)S(1)}, u32[]{:S(2)}, u32[]{:S(2)}) %collective-permute-start.3) | collective-permute-done | bytes 786464 | tf_op jit(solution)/shard_map/ppermute | solution.py:316
  97.2 1.5 %unpack.1 = (bf16[256,1024]{1,0:T(8,128)(2,1)}, bf16[256,1024]{1,0:T(8,128)(2,1)}, bf16[256,1024]{1,0:T(8,128)(2,1)}) custom-call(bf16[16,192,256]{2,1,0:T(8,128)(2,1)S(1)} %all_to_all.11.own_ref, bf16[8,192,256]{2,1,0:T(8,128)(2,1)S(1)} %collective-permute-done.3.r_ref), custom_call_target="tpu_custom_call" | custom-call | tf_op jit(solution)/shard_map/unpack/pallas_call | solution.py:317
  (3 shorter events, 0.0 us)
Async XLA Ops:
  0.6 9.0 %copy-start = (bf16[256,1024]{1,0:T(8,128)(2,1)S(1)}, bf16[256,1024]{1,0:T(8,128)(2,1)}, u32[]{:S(2)}) copy-start(bf16[256,1024]{1,0:T(8,128)(2,1)} %k_ref.3) | copy-start | bytes 1572868
  0.6 8.9 %copy-start.1 = (bf16[256,1024]{1,0:T(8,128)(2,1)S(1)}, bf16[256,1024]{1,0:T(8,128)(2,1)}, u32[]{:S(2)}) copy-start(bf16[256,1024]{1,0:T(8,128)(2,1)} %v_ref.3) | copy-start | bytes 1572868
  0.7 8.9 %copy-start.2 = (bf16[256,1024]{1,0:T(8,128)(2,1)S(1)}, bf16[256,1024]{1,0:T(8,128)(2,1)}, u32[]{:S(2)}) copy-start(bf16[256,1024]{1,0:T(8,128)(2,1)} %q_ref.3) | copy-start | bytes 1572868
  0.7 8.9 %copy-start.3 = (bf16[256,1024]{1,0:T(8,128)(2,1)S(1)}, bf16[256,1024]{1,0:T(8,128)(2,1)}, u32[]{:S(2)}) copy-start(bf16[256,1024]{1,0:T(8,128)(2,1)} %g_ref.3) | copy-start | bytes 1572868
  3.7 5.9 %collective-permute-start = (bf16[528,1024]{1,0:T(8,128)(2,1)}, bf16[528,1024]{1,0:T(8,128)(2,1)S(1)}, u32[]{:S(2)}, u32[]{:S(2)}) collective-permute-start(bf16[528,1024]{1,0:T(8,128)(2,1)} %get-tuple-element.9), channel_id=1, source_target_pairs={{0,16},{16,0},{32,48},{48,32},{64,80},{80,64},{96,112},{112,96},{1... | collective-permute-start | bytes 3244040 | tf_op jit(solution)/shard_map/ppermute | solution.py:290
  9.6 0.7 copy-start.4
  44.9 4.1 %collective-permute-start.1 = (bf16[16,128,256]{2,1,0:T(8,128)(2,1)S(1)}, bf16[16,128,256]{2,1,0:T(8,128)(2,1)S(1)}, u32[]{:S(2)}, u32[]{:S(2)}) collective-permute-start(bf16[16,128,256]{2,1,0:T(8,128)(2,1)S(1)} %slice.4), channel_id=1, source_target_pairs={{0,16},{16,0},{32,48},{48,32},{64,80},{80,64},{96,112},{112,96},{1... | collective-permute-start | bytes 3145736 | tf_op jit(solution)/shard_map/ppermute | solution.py:301
  65.1 3.0 %collective-permute-start.2 = (bf16[16,128,256]{2,1,0:T(8,128)(2,1)}, bf16[16,128,256]{2,1,0:T(8,128)(2,1)S(1)}, u32[]{:S(2)}, u32[]{:S(2)}) collective-permute-start(bf16[16,128,256]{2,1,0:T(8,128)(2,1)} %get-tuple-element.12), channel_id=1, source_target_pairs={{0,16},{16,0},{32,48},{48,32},{64,80},{80,64},{96,112},{112,96},{1... | collective-permute-start | bytes 3145736 | tf_op jit(solution)/shard_map/ppermute | solution.py:303
  93.1 4.1 %collective-permute-start.3 = (bf16[8,192,256]{2,1,0:T(8,128)(2,1)S(1)}, bf16[8,192,256]{2,1,0:T(8,128)(2,1)S(1)}, u32[]{:S(2)}, u32[]{:S(2)}) collective-permute-start(bf16[8,192,256]{2,1,0:T(8,128)(2,1)S(1)} %constant_dynamic-slice_fusion), channel_id=1, source_target_pairs={{0,16},{16,0},{32,48},{48,32},{64,80},{80,64},{96,112},{112,96},{1... | collective-permute-start | bytes 2359304 | tf_op jit(solution)/shard_map/ppermute | solution.py:316

commit v5 on v2

v5 whole, which is shorter than its diff:
```python
import jax
import jax.numpy as jnp
from jax import lax
from jax.experimental import pallas as pl
from jax.experimental.pallas import tpu as pltpu
from jax.sharding import PartitionSpec as P

HEADS = 8
HD = 128
BLK = 128
GLOB = 2
SHARDS = 16
SLOTS = 15
IDS = 16
LIGHT = 4
ROWS = 2 * BLK
META = 16
IN_ROWS = 2 * BLK + META
OUT_ROWS = BLK + BLK // 2
SCALE = HD**-0.5
LOG2E = 1.4426950408889634
MASKED = -1e30
NEAR = 3 + GLOB


def table_rows(pick_ref, count_ref, ids_ref, width):
    lanes = lax.broadcasted_iota(jnp.int32, (META, width), 1)
    table = jnp.where(lanes == SLOTS, count_ref[0], 0)
    for slot in range(SLOTS):
        table = jnp.where(lanes == slot, pick_ref[0, slot], table)
    for slot in range(GLOB):
        table = jnp.where(lanes == IDS + slot, ids_ref[slot], table)
    return table.astype(jnp.float32).astype(jnp.bfloat16)


def split_kernel(
    pick_hbm, count_ref, ids_hbm, k_ref, v_ref, q_ref, g_ref, out_ref, pick_ref, ids_ref, sems
):
    other = 1 - lax.rem(lax.axis_index("pat"), 2)
    source = pl.ds(pl.multiple_of(other * BLK, BLK), BLK)
    copies = []
    for index, ref in enumerate((k_ref, v_ref, q_ref, g_ref)):
        target = out_ref.at[pl.ds(index * BLK, BLK), :]
        copies.append(pltpu.make_async_copy(ref.at[source, :], target, sems.at[index]))
    tables = [
        pltpu.make_async_copy(pick_hbm, pick_ref, sems.at[4]),
        pltpu.make_async_copy(ids_hbm, ids_ref, sems.at[5]),
    ]
    for copy in tables + copies:
        copy.start()
    for copy in tables:
        copy.wait()
    out_ref[4 * BLK :, :] = table_rows(pick_ref, count_ref, ids_ref, HEADS * HD)
    for copy in copies:
        copy.wait()


def pack_kernel(pick_ref, count_ref, ids_ref, r_ref, k_ref, v_ref, q_ref, g_ref, out_ref, sems):
    core = lax.rem(lax.axis_index("pat"), 2)
    source = pl.ds(pl.multiple_of(core * BLK, BLK), BLK)
    copies = []
    for index, ref in enumerate((k_ref, v_ref, q_ref, g_ref)):
        rows = pl.ds(index // 2 * BLK, BLK)
        lanes = pl.ds(index % 2 * HD, HD)
        for head in range(HEADS):
            target = out_ref.at[core * HEADS + head, rows, lanes]
            origin = ref.at[source, pl.ds(head * HD, HD)]
            copies.append(pltpu.make_async_copy(origin, target, sems.at[index, head]))
    for copy in copies:
        copy.start()
    away = (1 - core) * HEADS
    table = table_rows(pick_ref, count_ref, ids_ref, 2 * HD)
    for head in range(HEADS):
        cols = slice(head * HD, (head + 1) * HD)
        out_ref[away + head, :BLK, :HD] = r_ref[:BLK, cols]
        out_ref[away + head, :BLK, HD:] = r_ref[BLK : 2 * BLK, cols]
        out_ref[away + head, BLK : 2 * BLK, :HD] = r_ref[2 * BLK : 3 * BLK, cols]
        out_ref[away + head, BLK : 2 * BLK, HD:] = r_ref[3 * BLK : 4 * BLK, cols]
        out_ref[away + head, 2 * BLK :, :] = r_ref[4 * BLK :, : 2 * HD]
        out_ref[core * HEADS + head, 2 * BLK :, :] = table
    for copy in copies:
        copy.wait()


def combine_kernel(own_ref, r_ref, out_ref):
    for shard in range(SHARDS):
        total = own_ref[shard, :BLK, :].astype(jnp.float32) + r_ref[shard].astype(jnp.float32)
        out_ref[shard, :BLK, :] = total.astype(jnp.bfloat16)
        out_ref[shard, BLK:, :] = own_ref[shard, BLK:, :]


def place(source, lead, block, outs, sems):
    copies = []
    half = BLK // 2
    for head in range(HEADS):
        cols = pl.ds(head * HD, HD)
        for index, (low, lane, out, row, size) in enumerate(
            (
                (0, 0, 1, 0, BLK),
                (0, HD, 2, 0, BLK),
                (BLK, 0, 0, 0, half),
                (BLK, HD, 0, half, half),
            )
        ):
            rows = pl.ds(pl.multiple_of(block * BLK + row, half), size)
            copies.append(
                pltpu.make_async_copy(
                    source.at[lead + head, pl.ds(low, size), pl.ds(lane, HD)],
                    outs[out].at[rows, cols],
                    sems.at[index, head],
                )
            )
    for copy in copies:
        copy.start()
    for copy in copies:
        copy.wait()


def own_kernel(own_ref, dq_ref, dk_ref, dv_ref, sems):
    core = lax.rem(lax.axis_index("pat"), 2)
    place(own_ref, core * HEADS, core, (dq_ref, dk_ref, dv_ref), sems)


def foreign_kernel(r_ref, dq_in, dk_in, dv_in, dq_ref, dk_ref, dv_ref, sems):
    core = lax.rem(lax.axis_index("pat"), 2)
    place(r_ref, 0, 1 - core, (dq_ref, dk_ref, dv_ref), sems)


GROUP = 5


def attention_kernel(
    x_ref, r_ref, o_ref, send_ref, acc, blocks, glob_kv, glob_acc, wmat, kv, sp, gb,
    long_kv, long_sp, long_gb, meta_v, meta_s, sem
):
    half = lax.rem(lax.axis_index("pat"), 2)
    meta_v[...] = x_ref[:, 2 * BLK, :HD].astype(jnp.float32).astype(jnp.int32)
    copy = pltpu.make_async_copy(meta_v, meta_s, sem)
    copy.start()
    own_rows = pl.ds(pl.multiple_of(half * BLK, BLK), BLK)
    other_rows = pl.ds(pl.multiple_of((1 - half) * BLK, BLK), BLK)
    for shard in range(SHARDS):
        blocks[shard, own_rows, :] = x_ref[shard, :BLK, :]
        blocks[shard, other_rows, :] = r_ref[shard]
    acc[...] = jnp.zeros_like(acc)
    glob_acc[...] = jnp.zeros_like(glob_acc)
    wmat[...] = jnp.zeros_like(wmat)
    copy.wait()
    for slot in range(GLOB):
        block = meta_s[0, IDS + slot]
        glob_kv[slot * BLK : (slot + 1) * BLK, :] = blocks[
            block // 2, pl.ds(pl.multiple_of(lax.rem(block, 2) * BLK, BLK), BLK), :
        ]

    def fold(value, op):
        parts = [value[i * 8 : (i + 1) * 8] for i in range(value.shape[0] // 8)]
        while len(parts) > 1:
            parts = [op(x, y) for x, y in zip(parts[::2], parts[1::2])] + parts[len(parts) // 2 * 2 :]
        return parts[0]

    def describe(shard, far, masked):
        count = meta_s[shard, SLOTS]
        beside = jnp.where(half == 0, shard - 1, shard + 1)
        valid = (beside >= 0) & (beside < SHARDS)
        beside = jnp.clip(beside, 0, SHARDS - 1)
        bias = {NEAR - 1: jnp.where(valid, 0.0, MASKED)}
        places = []
        for slot in range(far):
            pick = meta_s[shard, slot]
            rows = pl.ds(pl.multiple_of(pick * BLK, BLK), BLK)
            places.append((lax.rem(shard + 1 + slot, SHARDS), rows))
            if masked and slot:
                bias[NEAR + slot] = jnp.where(slot < count, 0.0, MASKED)
        return shard, beside, bias, places

    def scores(refs, job):
        wmat, kv, sp, gb = refs
        shard, beside, bias, places = job
        length = (NEAR + len(places)) * BLK
        wmat[:BLK, :HD] = x_ref[shard, BLK : 2 * BLK, :HD]
        wmat[BLK:, HD:] = x_ref[shard, BLK : 2 * BLK, HD:]
        kv[:ROWS, :] = blocks[shard]
        kv[ROWS : 2 * ROWS, :] = glob_kv[...]
        kv[2 * ROWS : 2 * ROWS + BLK, :] = blocks[beside, other_rows, :]
        for slot, (target, rows) in enumerate(places):
            kv[(NEAR + slot) * BLK : (NEAR + slot + 1) * BLK, :] = blocks[target, rows, :]
        sp[:length, :] = lax.dot_general(
            kv[:length, :], wmat[...], (((1,), (1,)), ((), ())), preferred_element_type=jnp.float32
        )

    def soften(refs, job):
        wmat, kv, sp, gb = refs
        shard, beside, bias, places = job
        chunks = NEAR + len(places)
        peak = None
        for chunk in range(chunks):
            high = fold(sp[chunk * BLK : (chunk + 1) * BLK, :HD], jnp.maximum)
            if chunk in bias:
                high = high + bias[chunk]
            peak = high if peak is None else jnp.maximum(peak, high)
        peak = jnp.max(peak, axis=0, keepdims=True) * (SCALE * LOG2E)
        peaks = {chunk: peak - bias[chunk] if chunk in bias else peak for chunk in range(chunks)}
        total = jnp.zeros((8, HD), jnp.float32)
        delta = jnp.zeros((8, HD), jnp.float32)
        for chunk in range(chunks):
            rows = slice(chunk * BLK, (chunk + 1) * BLK)
            weights = jnp.exp2(sp[rows, :HD] * (SCALE * LOG2E) - peaks[chunk])
            sp[rows, :HD] = weights
            total = total + fold(weights, jnp.add)
            delta = delta + fold(weights * sp[rows, HD:], jnp.add)
        inverse = 1.0 / jnp.sum(total, axis=0, keepdims=True)
        delta = jnp.sum(delta, axis=0, keepdims=True) * inverse
        inverse_scaled = inverse * SCALE
        for chunk in range(chunks):
            rows = slice(chunk * BLK, (chunk + 1) * BLK)
            weights = sp[rows, :HD]
            gb[rows, HD:] = (weights * inverse).astype(jnp.bfloat16)
            gb[rows, :HD] = ((weights * inverse_scaled) * (sp[rows, HD:] - delta)).astype(jnp.bfloat16)

    def backward(refs, job):
        wmat, kv, sp, gb = refs
        shard, beside, bias, places = job
        length = (NEAR + len(places)) * BLK
        grad_query = lax.dot_general(
            gb[:length, :HD], kv[:length, :HD], (((0,), (0,)), ((), ())), preferred_element_type=jnp.float32
        ).astype(jnp.bfloat16)
        o_ref[shard, BLK:, :HD] = grad_query[: BLK // 2]
        o_ref[shard, BLK:, HD:] = grad_query[BLK // 2 :]
        grads = jnp.dot(gb[:length, :], wmat[...], preferred_element_type=jnp.float32)
        acc[shard, :, :] += grads[:ROWS]
        glob_acc[...] += grads[ROWS : 2 * ROWS]
        acc[beside, other_rows, :] += grads[2 * ROWS : 2 * ROWS + BLK]
        for slot, (target, rows) in enumerate(places):
            acc[target, rows, :] += grads[(NEAR + slot) * BLK : (NEAR + slot + 1) * BLK]

    busy = 0
    for shard in range(SHARDS):
        busy = jnp.where(meta_s[shard, SLOTS] > LIGHT, shard, busy)

    def light(step, u):
        place = step * GROUP + u
        return describe(place + jnp.where(place >= busy, 1, 0), LIGHT, True)

    slots = [tuple(ref.at[u] for ref in (wmat, kv, sp, gb)) for u in range(GROUP)]
    steps = (SHARDS - 1) // GROUP
    long_refs = (wmat.at[GROUP], long_kv, long_sp, long_gb)
    long_job = describe(busy, SLOTS, False)
    scores(long_refs, long_job)
    for u in range(GROUP):
        scores(slots[u], light(0, u))
    soften(long_refs, long_job)
    backward(long_refs, long_job)

    def light_step(step, carry):
        for u in range(GROUP):
            job = light(step, u)
            soften(slots[u], job)
            backward(slots[u], job)
            scores(slots[u], light(step + 1, u))
        return carry

    lax.fori_loop(0, steps - 1, light_step, 0)
    for u in range(GROUP):
        job = light(steps - 1, u)
        soften(slots[u], job)
        backward(slots[u], job)

    for slot in range(GLOB):
        block = meta_s[0, IDS + slot]
        rows = pl.ds(pl.multiple_of(lax.rem(block, 2) * BLK, BLK), BLK)
        acc[block // 2, rows, :] += glob_acc[slot * BLK : (slot + 1) * BLK, :]

    def store_step(shard, carry):
        o_ref[shard, :BLK, :] = acc[shard, own_rows, :].astype(jnp.bfloat16)
        send_ref[shard, :, :] = acc[shard, other_rows, :].astype(jnp.bfloat16)
        return carry

    lax.fori_loop(0, SHARDS, store_step, 0)


VMEM = pl.BlockSpec(memory_space=pltpu.VMEM)
SMEM = pl.BlockSpec(memory_space=pltpu.SMEM)
ANY = pl.BlockSpec(memory_space=pl.ANY)


def kernel_params(megabytes):
    return pltpu.CompilerParams(vmem_limit_bytes=megabytes << 20)


def bf16(*shape):
    return jax.ShapeDtypeStruct(shape, jnp.bfloat16)


def attention(received, other):
    length = (NEAR + LIGHT) * BLK
    longest = (NEAR + SLOTS) * BLK
    return pl.pallas_call(
        attention_kernel,
        out_shape=(bf16(SHARDS, OUT_ROWS, 2 * HD), bf16(SHARDS, BLK, 2 * HD)),
        in_specs=[VMEM, VMEM],
        out_specs=(VMEM, VMEM),
        scratch_shapes=[
            pltpu.VMEM((SHARDS, ROWS, 2 * HD), jnp.float32),
            pltpu.VMEM((SHARDS, ROWS, 2 * HD), jnp.bfloat16),
            pltpu.VMEM((GLOB * BLK, 2 * HD), jnp.bfloat16),
            pltpu.VMEM((GLOB * BLK, 2 * HD), jnp.float32),
            pltpu.VMEM((GROUP + 1, 2 * BLK, 2 * HD), jnp.bfloat16),
            pltpu.VMEM((GROUP, length, 2 * HD), jnp.bfloat16),
            pltpu.VMEM((GROUP, length, 2 * HD), jnp.float32),
            pltpu.VMEM((GROUP, length, 2 * HD), jnp.bfloat16),
            pltpu.VMEM((longest, 2 * HD), jnp.bfloat16),
            pltpu.VMEM((longest, 2 * HD), jnp.float32),
            pltpu.VMEM((longest, 2 * HD), jnp.bfloat16),
            pltpu.VMEM((SHARDS, HD), jnp.int32),
            pltpu.SMEM((SHARDS, HD), jnp.int32),
            pltpu.SemaphoreType.DMA,
        ],
        compiler_params=kernel_params(40),
        name="attention",
    )(received, other)


def body(query_matrix, key_rows, value_rows, output_gradient_rows, far_pick, far_count, global_ids):
    width = HEADS * HD
    core = lax.rem(lax.axis_index("pat"), 2)
    arrays = (key_rows, value_rows, query_matrix, output_gradient_rows)
    pairs = [(i, i ^ 1) for i in range(lax.axis_size("pat"))]
    away = pl.pallas_call(
        split_kernel,
        out_shape=bf16(4 * BLK + META, width),
        in_specs=[ANY, SMEM, ANY, ANY, ANY, ANY, ANY],
        out_specs=VMEM,
        scratch_shapes=[
            pltpu.SMEM((1, SLOTS), jnp.int32),
            pltpu.SMEM((GLOB,), jnp.int32),
            pltpu.SemaphoreType.DMA((6,)),
        ],
        compiler_params=kernel_params(60),
        name="split",
    )(far_pick, far_count, global_ids, *arrays)
    arrived = lax.ppermute(away, "pat", pairs)
    sent = pl.pallas_call(
        pack_kernel,
        out_shape=bf16(SHARDS, IN_ROWS, 2 * HD),
        in_specs=[SMEM, SMEM, SMEM, VMEM, ANY, ANY, ANY, ANY],
        out_specs=VMEM,
        scratch_shapes=[pltpu.SemaphoreType.DMA((4, HEADS))],
        compiler_params=kernel_params(16),
        name="pack",
    )(far_pick, far_count, global_ids, arrived, *arrays)
    received = lax.all_to_all(sent, "seq", split_axis=0, concat_axis=0, tiled=True)
    other = lax.ppermute(received[:, :BLK, :], "pat", pairs)
    own, partial = attention(received, other)
    partial = lax.ppermute(partial, "pat", pairs)
    combined = pl.pallas_call(
        combine_kernel,
        out_shape=bf16(SHARDS, OUT_ROWS, 2 * HD),
        in_specs=[VMEM, VMEM],
        out_specs=VMEM,
        compiler_params=kernel_params(16),
        name="combine",
    )(own, partial)
    foreign_at = ((1 - core) * HEADS).astype(jnp.uint32)
    combined, foreign_at = lax.optimization_barrier((combined, foreign_at))
    returned = lax.all_to_all(combined, "seq", split_axis=0, concat_axis=0, tiled=True)
    foreign = lax.dynamic_slice_in_dim(returned, foreign_at, HEADS, axis=0)
    foreign = lax.ppermute(foreign, "pat", pairs)
    outputs = pl.pallas_call(
        own_kernel,
        out_shape=(bf16(ROWS, width),) * 3,
        in_specs=[VMEM],
        out_specs=(ANY,) * 3,
        scratch_shapes=[pltpu.SemaphoreType.DMA((4, HEADS))],
        compiler_params=kernel_params(16),
        cost_estimate=pl.CostEstimate(flops=0, bytes_accessed=3 << 20, transcendentals=0),
        name="own",
    )(returned)
    return pl.pallas_call(
        foreign_kernel,
        out_shape=(bf16(ROWS, width),) * 3,
        in_specs=[VMEM, ANY, ANY, ANY],
        out_specs=(ANY,) * 3,
        scratch_shapes=[pltpu.SemaphoreType.DMA((4, HEADS))],
        input_output_aliases={1: 0, 2: 1, 3: 2},
        compiler_params=kernel_params(16),
        name="foreign",
    )(foreign, *outputs)


def solution(mesh):
    rows = P(("pat", "seq"), None)
    in_specs = (rows, rows, rows, rows, rows, P("seq"), P("pat"))
    return jax.shard_map(
        body, mesh=mesh, in_specs=in_specs, out_specs=(rows, rows, rows), check_vma=False
    )
```

time: 114 us -> 96.4 us (0.85)
  blocking collectives: 33.6 us -> 58.3 us
  waiting for transfers between devices: 32.4 us -> 8.1 us
  Pallas kernels: 29.1 us -> 20.4 us
  local copies, waits for them, and re-layouts: 5.63 us -> 0.18 us
  starting transfers between devices: 11.1 us -> 7.8 us
    all_to_all x0 -> x1, blocking collectives: none -> 24.7 us  [body(): lax.all_to_all(combined, 'seq', split_axis=0, concat_axis=0, tiled=True)]
    all_to_all x1 -> x0, waiting for transfers between devices: 23.6 us -> none  [body(): lax.all_to_all(combined, 'seq', split_axis=0, concat_axis=0, tiled=True)]
    pallas_call x3 -> x4, Pallas kernels: 26.9 us -> 18.8 us  [the longest x1 14.1 us: attention(): pl.pallas_call(attention_kernel, out_shape=(bf16(SHARDS, OUT_ROWS, 2 * HD...]
    unnamed x20 -> x12, local copies, waits for them, and re-layouts: 5.48 us -> 0.03 us
    all_to_all x1 -> x0, starting transfers between devices: 3.71 us -> none  [body(): lax.all_to_all(combined, 'seq', split_axis=0, concat_axis=0, tiled=True)]
    pallas_call x1, Pallas kernels: 1.41 us -> 0.24 us  [body(): pl.pallas_call(combine_kernel, out_shape=bf16(SHARDS, OUT_ROWS, 2 * HD),...]
    ppermute x1, waiting for transfers between devices: 1.91 us -> 0.77 us  [body(): foreign = lax.ppermute(foreign, 'pat', pairs)]
  transfers between devices with their start and end apart: 5 -> 4, of which waited for: 5 -> 4; matrix products, arithmetic and copies ran while one was open for 0% -> 0% of each run, Pallas kernels for 0% -> 1%
where the time goes in v5:
time: 96.4 us; the launch traced here: 96.2 us
  blocking collectives  58.3 us (60%)
  Pallas kernels  20.4 us (21%)
  waiting for transfers between devices  8.1 us (8%)
  starting transfers between devices  7.8 us (8%)
  between operations  1.4 us (1%)
    all_to_all x1, blocking collectives, body(): lax.all_to_all(sent, 'seq', split_axis=0, concat_axis=0, tiled=True)  33.6 us
    all_to_all x1, blocking collectives, body(): lax.all_to_all(combined, 'seq', split_axis=0, concat_axis=0, tiled=True)  24.7 us
    pallas_call x1, Pallas kernels, attention(): pl.pallas_call(attention_kernel, out_shape=(bf16(SHARDS, OUT_ROWS, 2 * HD...  14.1 us
    ppermute x1, starting transfers between devices, body(): arrived = lax.ppermute(away, 'pat', pairs)  3.33 us
    ppermute x1, waiting for transfers between devices, body(): arrived = lax.ppermute(away, 'pat', pairs)  2.54 us
    ppermute x1, waiting for transfers between devices, body(): partial = lax.ppermute(partial, 'pat', pairs)  2.5 us
    pallas_call x1, Pallas kernels, body(): pl.pallas_call(split_kernel, out_shape=bf16(4 * BLK + META, width), in_sp...  2.37 us
    ppermute x1, waiting for transfers between devices, body(): other = lax.ppermute(received[:, :BLK, :], 'pat', pairs)  2.29 us
  transfers between devices with their start and end apart: 4, of which 4 were waited for; matrix products, arithmetic and copies ran while one was open for 0% of the time, Pallas kernels for 1%

profile of v5, /device:TPU:1, one launch (start us, length us, event | category | flops | bytes accessed | tf_op | source)
XLA Modules:
  0.0 96.2 jit_solution(17083124246209584469)
XLA Ops:
  1.3 0.0 copy-start
  1.3 0.0 copy-start.1
  1.3 0.0 copy-start.2
  1.3 0.0 copy-start.3
  1.3 0.0 copy-start.4
  1.3 0.0 copy-start.5
  1.3 2.4 %split.1 = bf16[528,1024]{1,0:T(8,128)(2,1)} custom-call(s32[1,15]{1,0:T(1,128)} %pick_ref.1, s32[1]{0:T(128)S(6)} %copy.16.count_ref, s32[2]{0:T(128)} %ids_ref.1, bf16[256,1024]{1,0:T(8,128)(2,1)} %k_ref.3, bf16[256,1024]{1,0:T(8,128)(2,1)} %v_ref.3, bf16[256,1024]{1,0:T(8,128)(2,1)} %q_ref.3, bf16[256,1024]{1,0:T(8,128)(2,1)} %g_ref.3), custom_call_target="tpu_custom_call" | custom-call | tf_op jit(solution)/shard_map/split/pallas_call | solution.py:328
  3.7 3.3 %collective-permute-start = (bf16[528,1024]{1,0:T(8,128)(2,1)}, bf16[528,1024]{1,0:T(8,128)(2,1)S(1)}, u32[]{:S(2)}, u32[]{:S(2)}) collective-permute-start(bf16[528,1024]{1,0:T(8,128)(2,1)} %split.1), channel_id=1, source_target_pairs={{0,16},{16,0},{32,48},{48,32},{64,80},{80,64},{96,112},{112,96},{1... | collective-permute-start | bytes 3244040 | tf_op jit(solution)/shard_map/ppermute | solution.py:341
  7.0 2.5 %collective-permute-done.r_ref = bf16[528,1024]{1,0:T(8,128)(2,1)S(1)} collective-permute-done((bf16[528,1024]{1,0:T(8,128)(2,1)}, bf16[528,1024]{1,0:T(8,128)(2,1)S(1)}, u32[]{:S(2)}, u32[]{:S(2)}) %collective-permute-start) | collective-permute-done | bytes 1081376 | tf_op jit(solution)/shard_map/ppermute | solution.py:341
  9.6 1.4 %pack.1 = bf16[16,272,256]{2,1,0:T(8,128)(2,1)S(1)} custom-call(s32[1,15]{1,0:T(1,128)S(1)} %copy-done.4, s32[1]{0:T(128)S(6)} %copy.16.count_ref, s32[2]{0:T(128)S(1)} %copy-done.5, bf16[528,1024]{1,0:T(8,128)(2,1)S(1)} %collective-permute-done.r_ref, bf16[256,1024]{1,0:T(8,128)(2,1)S(1)} %copy-done, bf16[256,1024]{1,0:T(8,128)(2,1)S(1)} %copy-done.1, ...), custom_call_target="tpu_custom_call" | custom-call | tf_op jit(solution)/shard_map/pack/pallas_call | solution.py:342
  11.0 33.6 %all_to_all.10.x_ref = bf16[16,272,256]{2,1,0:T(8,128)(2,1)S(1)} all-to-all(bf16[16,272,256]{2,1,0:T(8,128)(2,1)S(1)} %pack.1), channel_id=1, replica_groups=mesh['pat'=16,'seq'=16] {'seq'}, dimensions={0} | all-to-all | bytes 4456448 | tf_op jit(solution)/shard_map/all_to_all | solution.py:351
  44.6 0.1 slice.4
  44.8 1.8 %collective-permute-start.1 = (bf16[16,128,256]{2,1,0:T(8,128)(2,1)S(1)}, bf16[16,128,256]{2,1,0:T(8,128)(2,1)S(1)}, u32[]{:S(2)}, u32[]{:S(2)}) collective-permute-start(bf16[16,128,256]{2,1,0:T(8,128)(2,1)S(1)} %slice.4), channel_id=1, source_target_pairs={{0,16},{16,0},{32,48},{48,32},{64,80},{80,64},{96,112},{112,96},{1... | collective-permute-start | bytes 3145736 | tf_op jit(solution)/shard_map/ppermute | solution.py:352
  46.6 2.3 %collective-permute-done.1.r_ref = bf16[16,128,256]{2,1,0:T(8,128)(2,1)S(1)} collective-permute-done((bf16[16,128,256]{2,1,0:T(8,128)(2,1)S(1)}, bf16[16,128,256]{2,1,0:T(8,128)(2,1)S(1)}, u32[]{:S(2)}, u32[]{:S(2)}) %collective-permute-start.1) | collective-permute-done | bytes 1048608 | tf_op jit(solution)/shard_map/ppermute | solution.py:352
  48.9 14.1 %attention.1 = (bf16[16,192,256]{2,1,0:T(8,128)(2,1)S(1)}, bf16[16,128,256]{2,1,0:T(8,128)(2,1)}) custom-call(bf16[16,272,256]{2,1,0:T(8,128)(2,1)S(1)} %all_to_all.10.x_ref, bf16[16,128,256]{2,1,0:T(8,128)(2,1)S(1)} %collective-permute-done.1.r_ref), custom_call_target="tpu_custom_call" | custom-call | tf_op jit(solution)/shard_map/attention/pallas_call | solution.py:297
  63.0 0.5 collective-permute-start.2
  63.5 2.5 %collective-permute-done.2.r_ref = bf16[16,128,256]{2,1,0:T(8,128)(2,1)S(1)} collective-permute-done((bf16[16,128,256]{2,1,0:T(8,128)(2,1)}, bf16[16,128,256]{2,1,0:T(8,128)(2,1)S(1)}, u32[]{:S(2)}, u32[]{:S(2)}) %collective-permute-start.2) | collective-permute-done | bytes 1048608 | tf_op jit(solution)/shard_map/ppermute | solution.py:354
  66.0 0.2 combine.1
  66.2 24.7 %all_to_all.11.own_ref = bf16[16,192,256]{2,1,0:T(8,128)(2,1)S(1)} all-to-all(bf16[16,192,256]{2,1,0:T(8,128)(2,1)S(1)} %combine.1), channel_id=1, replica_groups=mesh['pat'=16,'seq'=16] {'seq'}, dimensions={0} | all-to-all | bytes 3145728 | tf_op jit(solution)/shard_map/all_to_all | solution.py:365
  90.9 0.1 constant_dynamic-slice_fusion
  91.0 2.2 %collective-permute-start.3 = (bf16[8,192,256]{2,1,0:T(8,128)(2,1)S(1)}, bf16[8,192,256]{2,1,0:T(8,128)(2,1)S(1)}, u32[]{:S(2)}, u32[]{:S(2)}) collective-permute-start(bf16[8,192,256]{2,1,0:T(8,128)(2,1)S(1)} %constant_dynamic-slice_fusion), channel_id=1, source_target_pairs={{0,16},{16,0},{32,48},{48,32},{64,80},{80,64},{96,112},{112,96},{1... | collective-permute-start | bytes 2359304 | tf_op jit(solution)/shard_map/ppermute | solution.py:367
  93.1 1.1 %own.1 = (bf16[256,1024]{1,0:T(8,128)(2,1)}, bf16[256,1024]{1,0:T(8,128)(2,1)}, bf16[256,1024]{1,0:T(8,128)(2,1)}) custom-call(bf16[16,192,256]{2,1,0:T(8,128)(2,1)S(1)} %all_to_all.11.own_ref), custom_call_target="tpu_custom_call" | custom-call | bytes 3145728 | tf_op jit(solution)/shard_map/own/pallas_call | solution.py:368
  94.3 0.8 collective-permute-done.3.r_ref
  95.1 1.1 %foreign.1 = (bf16[256,1024]{1,0:T(8,128)(2,1)}, bf16[256,1024]{1,0:T(8,128)(2,1)}, bf16[256,1024]{1,0:T(8,128)(2,1)}) custom-call(bf16[8,192,256]{2,1,0:T(8,128)(2,1)S(1)} %collective-permute-done.3.r_ref, bf16[256,1024]{1,0:T(8,128)(2,1)} %get-tuple-element.14.dq_in, ...), custom_call_target="tpu_custom_call", output_to_operand_aliasing={{0}: (1, {}), {1}: (2, {}), {2}: (3, {})} | custom-call | tf_op jit(solution)/shard_map/foreign/pallas_call | solution.py:378
  (6 shorter events, 0.0 us)
Async XLA Ops:
  1.3 8.3 %copy-start = (bf16[256,1024]{1,0:T(8,128)(2,1)S(1)}, bf16[256,1024]{1,0:T(8,128)(2,1)}, u32[]{:S(2)}) copy-start(bf16[256,1024]{1,0:T(8,128)(2,1)} %k_ref.3) | copy-start | bytes 1572868
  1.3 8.3 %copy-start.1 = (bf16[256,1024]{1,0:T(8,128)(2,1)S(1)}, bf16[256,1024]{1,0:T(8,128)(2,1)}, u32[]{:S(2)}) copy-start(bf16[256,1024]{1,0:T(8,128)(2,1)} %v_ref.3) | copy-start | bytes 1572868
  1.3 8.3 %copy-start.2 = (bf16[256,1024]{1,0:T(8,128)(2,1)S(1)}, bf16[256,1024]{1,0:T(8,128)(2,1)}, u32[]{:S(2)}) copy-start(bf16[256,1024]{1,0:T(8,128)(2,1)} %q_ref.3) | copy-start | bytes 1572868
  1.3 8.3 %copy-start.3 = (bf16[256,1024]{1,0:T(8,128)(2,1)S(1)}, bf16[256,1024]{1,0:T(8,128)(2,1)}, u32[]{:S(2)}) copy-start(bf16[256,1024]{1,0:T(8,128)(2,1)} %g_ref.3) | copy-start | bytes 1572868
  1.3 8.3 %copy-start.4 = (s32[1,15]{1,0:T(1,128)S(1)}, s32[1,15]{1,0:T(1,128)}, u32[]{:S(2)}) copy-start(s32[1,15]{1,0:T(1,128)} %pick_ref.1) | copy-start | bytes 184
  1.3 8.3 %copy-start.5 = (s32[2]{0:T(128)S(1)}, s32[2]{0:T(128)}, u32[]{:S(2)}) copy-start(s32[2]{0:T(128)} %ids_ref.1) | copy-start | bytes 28
  3.7 5.9 %collective-permute-start = (bf16[528,1024]{1,0:T(8,128)(2,1)}, bf16[528,1024]{1,0:T(8,128)(2,1)S(1)}, u32[]{:S(2)}, u32[]{:S(2)}) collective-permute-start(bf16[528,1024]{1,0:T(8,128)(2,1)} %split.1), channel_id=1, source_target_pairs={{0,16},{16,0},{32,48},{48,32},{64,80},{80,64},{96,112},{112,96},{1... | collective-permute-start | bytes 3244040 | tf_op jit(solution)/shard_map/ppermute | solution.py:341
  44.8 4.1 %collective-permute-start.1 = (bf16[16,128,256]{2,1,0:T(8,128)(2,1)S(1)}, bf16[16,128,256]{2,1,0:T(8,128)(2,1)S(1)}, u32[]{:S(2)}, u32[]{:S(2)}) collective-permute-start(bf16[16,128,256]{2,1,0:T(8,128)(2,1)S(1)} %slice.4), channel_id=1, source_target_pairs={{0,16},{16,0},{32,48},{48,32},{64,80},{80,64},{96,112},{112,96},{1... | collective-permute-start | bytes 3145736 | tf_op jit(solution)/shard_map/ppermute | solution.py:352
  63.0 3.0 %collective-permute-start.2 = (bf16[16,128,256]{2,1,0:T(8,128)(2,1)}, bf16[16,128,256]{2,1,0:T(8,128)(2,1)S(1)}, u32[]{:S(2)}, u32[]{:S(2)}) collective-permute-start(bf16[16,128,256]{2,1,0:T(8,128)(2,1)} %get-tuple-element.11), channel_id=1, source_target_pairs={{0,16},{16,0},{32,48},{48,32},{64,80},{80,64},{96,112},{112,96},{1... | collective-permute-start | bytes 3145736 | tf_op jit(solution)/shard_map/ppermute | solution.py:354
  91.0 4.1 %collective-permute-start.3 = (bf16[8,192,256]{2,1,0:T(8,128)(2,1)S(1)}, bf16[8,192,256]{2,1,0:T(8,128)(2,1)S(1)}, u32[]{:S(2)}, u32[]{:S(2)}) collective-permute-start(bf16[8,192,256]{2,1,0:T(8,128)(2,1)S(1)} %constant_dynamic-slice_fusion), channel_id=1, source_target_pairs={{0,16},{16,0},{32,48},{48,32},{64,80},{80,64},{96,112},{112,96},{1... | collective-permute-start | bytes 2359304 | tf_op jit(solution)/shard_map/ppermute | solution.py:367

commit v6 on v5

--- a/solution.py
+++ b/solution.py
@@ -15,7 +15,8 @@
 LIGHT = 4
 ROWS = 2 * BLK
 META = 16
-IN_ROWS = 2 * BLK + META
+TAIL = 8
+IN_ROWS = 2 * BLK + TAIL
 OUT_ROWS = BLK + BLK // 2
 SCALE = HD**-0.5
 LOG2E = 1.4426950408889634
@@ -23,8 +24,18 @@
 NEAR = 3 + GLOB
 
 
-def table_rows(pick_ref, count_ref, ids_ref, width):
-    lanes = lax.broadcasted_iota(jnp.int32, (META, width), 1)
+def fetch_tables(pick_hbm, ids_hbm, pick_ref, ids_ref, sems):
+    copies = [
+        pltpu.make_async_copy(pick_hbm, pick_ref, sems.at[0]),
+        pltpu.make_async_copy(ids_hbm, ids_ref, sems.at[1]),
+    ]
+    for copy in copies:
+        copy.start()
+    return copies
+
+
+def table_rows(pick_ref, count_ref, ids_ref, shape):
+    lanes = lax.broadcasted_iota(jnp.int32, shape, 1)
     table = jnp.where(lanes == SLOTS, count_ref[0], 0)
     for slot in range(SLOTS):
         table = jnp.where(lanes == slot, pick_ref[0, slot], table)
@@ -34,29 +45,39 @@
 
 
 def split_kernel(
-    pick_hbm, count_ref, ids_hbm, k_ref, v_ref, q_ref, g_ref, out_ref, pick_ref, ids_ref, sems
+    pick_hbm, count_ref, ids_hbm, k_ref, v_ref, q_ref, g_ref, out_ref, pick_ref, ids_ref, held, sems, in_sems, out_sems
 ):
     other = 1 - lax.rem(lax.axis_index("pat"), 2)
-    source = pl.ds(pl.multiple_of(other * BLK, BLK), BLK)
-    copies = []
+    tables = fetch_tables(pick_hbm, ids_hbm, pick_ref, ids_ref, sems)
+    arriving, leaving = [], []
+    half = BLK // 2
     for index, ref in enumerate((k_ref, v_ref, q_ref, g_ref)):
-        target = out_ref.at[pl.ds(index * BLK, BLK), :]
-        copies.append(pltpu.make_async_copy(ref.at[source, :], target, sems.at[index]))
-    tables = [
-        pltpu.make_async_copy(pick_hbm, pick_ref, sems.at[4]),
-        pltpu.make_async_copy(ids_hbm, ids_ref, sems.at[5]),
-    ]
-    for copy in tables + copies:
+        for part in range(2):
+            source = pl.ds(pl.multiple_of(other * BLK + part * half, half), half)
+            rows = pl.ds(index * BLK + part * half, half)
+            piece = 2 * index + part
+            arriving.append(pltpu.make_async_copy(ref.at[source, :], held.at[rows, :], in_sems.at[piece]))
+            leaving.append(pltpu.make_async_copy(held.at[rows, :], out_ref.at[rows, :], out_sems.at[piece]))
+    for copy in arriving:
         copy.start()
     for copy in tables:
         copy.wait()
-    out_ref[4 * BLK :, :] = table_rows(pick_ref, count_ref, ids_ref, HEADS * HD)
-    for copy in copies:
-        copy.wait()
-
-
-def pack_kernel(pick_ref, count_ref, ids_ref, r_ref, k_ref, v_ref, q_ref, g_ref, out_ref, sems):
+    held[4 * BLK :, :] = table_rows(pick_ref, count_ref, ids_ref, (META, HEADS * HD))
+    rows = pl.ds(4 * BLK, META)
+    leaving.append(pltpu.make_async_copy(held.at[rows, :], out_ref.at[rows, :], out_sems.at[8]))
+    leaving[-1].start()
+    for copy, onward in zip(arriving, leaving):
+        copy.wait()
+        onward.start()
+    for copy in leaving:
+        copy.wait()
+
+
+def pack_kernel(
+    pick_hbm, count_ref, ids_hbm, r_ref, k_ref, v_ref, q_ref, g_ref, out_ref, pick_ref, ids_ref, table_sems, sems
+):
     core = lax.rem(lax.axis_index("pat"), 2)
+    tables = fetch_tables(pick_hbm, ids_hbm, pick_ref, ids_ref, table_sems)
     source = pl.ds(pl.multiple_of(core * BLK, BLK), BLK)
     copies = []
     for index, ref in enumerate((k_ref, v_ref, q_ref, g_ref)):
@@ -69,14 +90,17 @@
     for copy in copies:
         copy.start()
     away = (1 - core) * HEADS
-    table = table_rows(pick_ref, count_ref, ids_ref, 2 * HD)
     for head in range(HEADS):
         cols = slice(head * HD, (head + 1) * HD)
         out_ref[away + head, :BLK, :HD] = r_ref[:BLK, cols]
         out_ref[away + head, :BLK, HD:] = r_ref[BLK : 2 * BLK, cols]
         out_ref[away + head, BLK : 2 * BLK, :HD] = r_ref[2 * BLK : 3 * BLK, cols]
         out_ref[away + head, BLK : 2 * BLK, HD:] = r_ref[3 * BLK : 4 * BLK, cols]
-        out_ref[away + head, 2 * BLK :, :] = r_ref[4 * BLK :, : 2 * HD]
+        out_ref[away + head, 2 * BLK :, :] = r_ref[4 * BLK : 4 * BLK + TAIL, : 2 * HD]
+    for copy in tables:
+        copy.wait()
+    table = table_rows(pick_ref, count_ref, ids_ref, (TAIL, 2 * HD))
+    for head in range(HEADS):
         out_ref[core * HEADS + head, 2 * BLK :, :] = table
     for copy in copies:
         copy.wait()
@@ -275,7 +299,7 @@
         send_ref[shard, :, :] = acc[shard, other_rows, :].astype(jnp.bfloat16)
         return carry
 
-    lax.fori_loop(0, SHARDS, store_step, 0)
+    lax.fori_loop(0, SHARDS, store_step, 0, unroll=4)
 
 
 VMEM = pl.BlockSpec(memory_space=pltpu.VMEM)
@@ -325,29 +349,37 @@
     core = lax.rem(lax.axis_index("pat"), 2)
     arrays = (key_rows, value_rows, query_matrix, output_gradient_rows)
     pairs = [(i, i ^ 1) for i in range(lax.axis_size("pat"))]
+    tables = (far_pick, far_count, global_ids)
+    table_scratch = [
+        pltpu.SMEM((1, SLOTS), jnp.int32),
+        pltpu.SMEM((GLOB,), jnp.int32),
+    ]
     away = pl.pallas_call(
         split_kernel,
         out_shape=bf16(4 * BLK + META, width),
         in_specs=[ANY, SMEM, ANY, ANY, ANY, ANY, ANY],
-        out_specs=VMEM,
-        scratch_shapes=[
-            pltpu.SMEM((1, SLOTS), jnp.int32),
-            pltpu.SMEM((GLOB,), jnp.int32),
-            pltpu.SemaphoreType.DMA((6,)),
+        out_specs=ANY,
+        scratch_shapes=table_scratch
+        + [
+            pltpu.VMEM((4 * BLK + META, width), jnp.bfloat16),
+            pltpu.SemaphoreType.DMA((2,)),
+            pltpu.SemaphoreType.DMA((8,)),
+            pltpu.SemaphoreType.DMA((9,)),
         ],
         compiler_params=kernel_params(60),
         name="split",
-    )(far_pick, far_count, global_ids, *arrays)
+    )(*tables, *arrays)
     arrived = lax.ppermute(away, "pat", pairs)
     sent = pl.pallas_call(
         pack_kernel,
         out_shape=bf16(SHARDS, IN_ROWS, 2 * HD),
-        in_specs=[SMEM, SMEM, SMEM, VMEM, ANY, ANY, ANY, ANY],
+        in_specs=[ANY, SMEM, ANY, VMEM, ANY, ANY, ANY, ANY],
         out_specs=VMEM,
-        scratch_shapes=[pltpu.SemaphoreType.DMA((4, HEADS))],
+        scratch_shapes=table_scratch
+        + [pltpu.SemaphoreType.DMA((2,)), pltpu.SemaphoreType.DMA((4, HEADS))],
         compiler_params=kernel_params(16),
         name="pack",
-    )(far_pick, far_count, global_ids, arrived, *arrays)
+    )(*tables, arrived, *arrays)
     received = lax.all_to_all(sent, "seq", split_axis=0, concat_axis=0, tiled=True)
     other = lax.ppermute(received[:, :BLK, :], "pat", pairs)
     own, partial = attention(received, other)

time: 96.4 us -> 95.1 us (0.987)
  no operation moved by 1% of the time
where the time goes in v6:
time: 95.1 us; the launch traced here: 94.9 us
  blocking collectives  57.7 us (61%)
  Pallas kernels  19.8 us (21%)
  waiting for transfers between devices  8.1 us (9%)
  starting transfers between devices  7.72 us (8%)
  between operations  1.4 us (1%)
    all_to_all x1, blocking collectives, body(): lax.all_to_all(sent, 'seq', split_axis=0, concat_axis=0, tiled=True)  33.2 us
    all_to_all x1, blocking collectives, body(): lax.all_to_all(combined, 'seq', split_axis=0, concat_axis=0, tiled=True)  24.5 us
    pallas_call x1, Pallas kernels, attention(): pl.pallas_call(attention_kernel, out_shape=(bf16(SHARDS, OUT_ROWS, 2 * HD...  14.1 us
    ppermute x1, starting transfers between devices, body(): arrived = lax.ppermute(away, 'pat', pairs)  3.33 us
    ppermute x1, waiting for transfers between devices, body(): arrived = lax.ppermute(away, 'pat', pairs)  2.54 us
    ppermute x1, waiting for transfers between devices, body(): partial = lax.ppermute(partial, 'pat', pairs)  2.5 us
    ppermute x1, waiting for transfers between devices, body(): other = lax.ppermute(received[:, :BLK, :], 'pat', pairs)  2.29 us
    pallas_call x1, Pallas kernels, body(): pl.pallas_call(split_kernel, out_shape=bf16(4 * BLK + META, width), in_sp...  2.26 us
  transfers between devices with their start and end apart: 4, of which 4 were waited for; matrix products, arithmetic and copies ran while one was open for 0% of the time, Pallas kernels for 1%

profile of v6, /device:TPU:1, one launch (start us, length us, event | category | flops | bytes accessed | tf_op | source)
XLA Modules:
  0.0 94.9 jit_solution(13595196628967058474)
XLA Ops:
  1.3 0.0 copy-start
  1.3 0.0 copy-start.1
  1.3 0.0 copy-start.2
  1.3 0.0 copy-start.3
  1.3 0.0 copy-start.4
  1.3 2.3 %split.1 = bf16[528,1024]{1,0:T(8,128)(2,1)} custom-call(s32[1,15]{1,0:T(1,128)} %pick_hbm.3, s32[1]{0:T(128)S(6)} %copy.16.count_ref, s32[2]{0:T(128)} %ids_hbm.3, bf16[256,1024]{1,0:T(8,128)(2,1)} %k_ref.3, bf16[256,1024]{1,0:T(8,128)(2,1)} %v_ref.3, bf16[256,1024]{1,0:T(8,128)(2,1)} %q_ref.3, bf16[256,1024]{1,0:T(8,128)(2,1)} %g_ref.3), custom_call_target="tpu_custom_call" | custom-call | tf_op jit(solution)/shard_map/split/pallas_call | solution.py:357
  3.6 3.3 %collective-permute-start = (bf16[528,1024]{1,0:T(8,128)(2,1)}, bf16[528,1024]{1,0:T(8,128)(2,1)S(1)}, u32[]{:S(2)}, u32[]{:S(2)}) collective-permute-start(bf16[528,1024]{1,0:T(8,128)(2,1)} %split.1), channel_id=1, source_target_pairs={{0,16},{16,0},{32,48},{48,32},{64,80},{80,64},{96,112},{112,96},{1... | collective-permute-start | bytes 3244040 | tf_op jit(solution)/shard_map/ppermute | solution.py:372
  6.9 2.5 %collective-permute-done.r_ref = bf16[528,1024]{1,0:T(8,128)(2,1)S(1)} collective-permute-done((bf16[528,1024]{1,0:T(8,128)(2,1)}, bf16[528,1024]{1,0:T(8,128)(2,1)S(1)}, u32[]{:S(2)}, u32[]{:S(2)}) %collective-permute-start) | collective-permute-done | bytes 1081376 | tf_op jit(solution)/shard_map/ppermute | solution.py:372
  9.5 0.0 copy-done.2
  9.5 0.9 pack.1
  10.4 33.2 %all_to_all.10.x_ref = bf16[16,264,256]{2,1,0:T(8,128)(2,1)S(1)} all-to-all(bf16[16,264,256]{2,1,0:T(8,128)(2,1)S(1)} %pack.1), channel_id=1, replica_groups=mesh['pat'=16,'seq'=16] {'seq'}, dimensions={0} | all-to-all | bytes 4325376 | tf_op jit(solution)/shard_map/all_to_all | solution.py:383
  43.6 0.1 slice.4
  43.7 1.8 %collective-permute-start.1 = (bf16[16,128,256]{2,1,0:T(8,128)(2,1)S(1)}, bf16[16,128,256]{2,1,0:T(8,128)(2,1)S(1)}, u32[]{:S(2)}, u32[]{:S(2)}) collective-permute-start(bf16[16,128,256]{2,1,0:T(8,128)(2,1)S(1)} %slice.4), channel_id=1, source_target_pairs={{0,16},{16,0},{32,48},{48,32},{64,80},{80,64},{96,112},{112,96},{1... | collective-permute-start | bytes 3145736 | tf_op jit(solution)/shard_map/ppermute | solution.py:384
  45.5 2.3 %collective-permute-done.1.r_ref = bf16[16,128,256]{2,1,0:T(8,128)(2,1)S(1)} collective-permute-done((bf16[16,128,256]{2,1,0:T(8,128)(2,1)S(1)}, bf16[16,128,256]{2,1,0:T(8,128)(2,1)S(1)}, u32[]{:S(2)}, u32[]{:S(2)}) %collective-permute-start.1) | collective-permute-done | bytes 1048608 | tf_op jit(solution)/shard_map/ppermute | solution.py:384
  47.8 14.1 %attention.1 = (bf16[16,192,256]{2,1,0:T(8,128)(2,1)S(1)}, bf16[16,128,256]{2,1,0:T(8,128)(2,1)}) custom-call(bf16[16,264,256]{2,1,0:T(8,128)(2,1)S(1)} %all_to_all.10.x_ref, bf16[16,128,256]{2,1,0:T(8,128)(2,1)S(1)} %collective-permute-done.1.r_ref), custom_call_target="tpu_custom_call" | custom-call | tf_op jit(solution)/shard_map/attention/pallas_call | solution.py:321
  61.9 0.5 collective-permute-start.2
  62.3 2.5 %collective-permute-done.2.r_ref = bf16[16,128,256]{2,1,0:T(8,128)(2,1)S(1)} collective-permute-done((bf16[16,128,256]{2,1,0:T(8,128)(2,1)}, bf16[16,128,256]{2,1,0:T(8,128)(2,1)S(1)}, u32[]{:S(2)}, u32[]{:S(2)}) %collective-permute-start.2) | collective-permute-done | bytes 1048608 | tf_op jit(solution)/shard_map/ppermute | solution.py:386
  64.8 0.2 combine.1
  65.1 24.5 %all_to_all.11.own_ref = bf16[16,192,256]{2,1,0:T(8,128)(2,1)S(1)} all-to-all(bf16[16,192,256]{2,1,0:T(8,128)(2,1)S(1)} %combine.1), channel_id=1, replica_groups=mesh['pat'=16,'seq'=16] {'seq'}, dimensions={0} | all-to-all | bytes 3145728 | tf_op jit(solution)/shard_map/all_to_all | solution.py:397
  89.6 0.1 constant_dynamic-slice_fusion
  89.6 2.2 %collective-permute-start.3 = (bf16[8,192,256]{2,1,0:T(8,128)(2,1)S(1)}, bf16[8,192,256]{2,1,0:T(8,128)(2,1)S(1)}, u32[]{:S(2)}, u32[]{:S(2)}) collective-permute-start(bf16[8,192,256]{2,1,0:T(8,128)(2,1)S(1)} %constant_dynamic-slice_fusion), channel_id=1, source_target_pairs={{0,16},{16,0},{32,48},{48,32},{64,80},{80,64},{96,112},{112,96},{1... | collective-permute-start | bytes 2359304 | tf_op jit(solution)/shard_map/ppermute | solution.py:399
  91.8 1.1 %own.1 = (bf16[256,1024]{1,0:T(8,128)(2,1)}, bf16[256,1024]{1,0:T(8,128)(2,1)}, bf16[256,1024]{1,0:T(8,128)(2,1)}) custom-call(bf16[16,192,256]{2,1,0:T(8,128)(2,1)S(1)} %all_to_all.11.own_ref), custom_call_target="tpu_custom_call" | custom-call | bytes 3145728 | tf_op jit(solution)/shard_map/own/pallas_call | solution.py:400
  93.0 0.8 collective-permute-done.3.r_ref
  93.7 1.1 %foreign.1 = (bf16[256,1024]{1,0:T(8,128)(2,1)}, bf16[256,1024]{1,0:T(8,128)(2,1)}, bf16[256,1024]{1,0:T(8,128)(2,1)}) custom-call(bf16[8,192,256]{2,1,0:T(8,128)(2,1)S(1)} %collective-permute-done.3.r_ref, bf16[256,1024]{1,0:T(8,128)(2,1)} %get-tuple-element.14.dq_in, ...), custom_call_target="tpu_custom_call", output_to_operand_aliasing={{0}: (1, {}), {1}: (2, {}), {2}: (3, {})} | custom-call | tf_op jit(solution)/shard_map/foreign/pallas_call | solution.py:410
  (6 shorter events, 0.0 us)
Async XLA Ops:
  1.3 8.2 %copy-start = (bf16[256,1024]{1,0:T(8,128)(2,1)S(1)}, bf16[256,1024]{1,0:T(8,128)(2,1)}, u32[]{:S(2)}) copy-start(bf16[256,1024]{1,0:T(8,128)(2,1)} %k_ref.3) | copy-start | bytes 1572868
  1.3 8.2 %copy-start.1 = (bf16[256,1024]{1,0:T(8,128)(2,1)S(1)}, bf16[256,1024]{1,0:T(8,128)(2,1)}, u32[]{:S(2)}) copy-start(bf16[256,1024]{1,0:T(8,128)(2,1)} %v_ref.3) | copy-start | bytes 1572868
  1.3 8.2 %copy-start.2 = (bf16[256,1024]{1,0:T(8,128)(2,1)S(1)}, bf16[256,1024]{1,0:T(8,128)(2,1)}, u32[]{:S(2)}) copy-start(bf16[256,1024]{1,0:T(8,128)(2,1)} %q_ref.3) | copy-start | bytes 1572868
  1.3 8.2 %copy-start.3 = (bf16[256,1024]{1,0:T(8,128)(2,1)S(1)}, bf16[256,1024]{1,0:T(8,128)(2,1)}, u32[]{:S(2)}) copy-start(bf16[256,1024]{1,0:T(8,128)(2,1)} %g_ref.3) | copy-start | bytes 1572868
  1.3 8.2 %copy-start.4 = (s32[1,15]{1,0:T(1,128)S(1)}, s32[1,15]{1,0:T(1,128)}, u32[]{:S(2)}) copy-start(s32[1,15]{1,0:T(1,128)} %pick_hbm.3) | copy-start | bytes 184
  1.3 8.2 %copy-start.5 = (s32[2]{0:T(128)S(1)}, s32[2]{0:T(128)}, u32[]{:S(2)}) copy-start(s32[2]{0:T(128)} %ids_hbm.3) | copy-start | bytes 28
  3.6 5.9 %collective-permute-start = (bf16[528,1024]{1,0:T(8,128)(2,1)}, bf16[528,1024]{1,0:T(8,128)(2,1)S(1)}, u32[]{:S(2)}, u32[]{:S(2)}) collective-permute-start(bf16[528,1024]{1,0:T(8,128)(2,1)} %split.1), channel_id=1, source_target_pairs={{0,16},{16,0},{32,48},{48,32},{64,80},{80,64},{96,112},{112,96},{1... | collective-permute-start | bytes 3244040 | tf_op jit(solution)/shard_map/ppermute | solution.py:372
  43.7 4.0 %collective-permute-start.1 = (bf16[16,128,256]{2,1,0:T(8,128)(2,1)S(1)}, bf16[16,128,256]{2,1,0:T(8,128)(2,1)S(1)}, u32[]{:S(2)}, u32[]{:S(2)}) collective-permute-start(bf16[16,128,256]{2,1,0:T(8,128)(2,1)S(1)} %slice.4), channel_id=1, source_target_pairs={{0,16},{16,0},{32,48},{48,32},{64,80},{80,64},{96,112},{112,96},{1... | collective-permute-start | bytes 3145736 | tf_op jit(solution)/shard_map/ppermute | solution.py:384
  61.9 3.0 %collective-permute-start.2 = (bf16[16,128,256]{2,1,0:T(8,128)(2,1)}, bf16[16,128,256]{2,1,0:T(8,128)(2,1)S(1)}, u32[]{:S(2)}, u32[]{:S(2)}) collective-permute-start(bf16[16,128,256]{2,1,0:T(8,128)(2,1)} %get-tuple-element.11), channel_id=1, source_target_pairs={{0,16},{16,0},{32,48},{48,32},{64,80},{80,64},{96,112},{112,96},{1... | collective-permute-start | bytes 3145736 | tf_op jit(solution)/shard_map/ppermute | solution.py:386
  89.6 4.1 %collective-permute-start.3 = (bf16[8,192,256]{2,1,0:T(8,128)(2,1)S(1)}, bf16[8,192,256]{2,1,0:T(8,128)(2,1)S(1)}, u32[]{:S(2)}, u32[]{:S(2)}) collective-permute-start(bf16[8,192,256]{2,1,0:T(8,128)(2,1)S(1)} %constant_dynamic-slice_fusion), channel_id=1, source_target_pairs={{0,16},{16,0},{32,48},{48,32},{64,80},{80,64},{96,112},{112,96},{1... | collective-permute-start | bytes 2359304 | tf_op jit(solution)/shard_map/ppermute | solution.py:399

commit v7 on v6

--- a/solution.py
+++ b/solution.py
@@ -24,10 +24,10 @@
 NEAR = 3 + GLOB
 
 
-def fetch_tables(pick_hbm, ids_hbm, pick_ref, ids_ref, sems):
+def fetch_tables(origins, targets, sems):
     copies = [
-        pltpu.make_async_copy(pick_hbm, pick_ref, sems.at[0]),
-        pltpu.make_async_copy(ids_hbm, ids_ref, sems.at[1]),
+        pltpu.make_async_copy(origin, target, sems.at[index])
+        for index, (origin, target) in enumerate(zip(origins, targets))
     ]
     for copy in copies:
         copy.start()
@@ -45,10 +45,11 @@
 
 
 def split_kernel(
-    pick_hbm, count_ref, ids_hbm, k_ref, v_ref, q_ref, g_ref, out_ref, pick_ref, ids_ref, held, sems, in_sems, out_sems
+    pick_hbm, count_hbm, ids_hbm, k_ref, v_ref, q_ref, g_ref, out_ref,
+    pick_ref, count_ref, ids_ref, held, sems, in_sems, out_sems
 ):
     other = 1 - lax.rem(lax.axis_index("pat"), 2)
-    tables = fetch_tables(pick_hbm, ids_hbm, pick_ref, ids_ref, sems)
+    tables = fetch_tables((pick_hbm, count_hbm, ids_hbm), (pick_ref, count_ref, ids_ref), sems)
     arriving, leaving = [], []
     half = BLK // 2
     for index, ref in enumerate((k_ref, v_ref, q_ref, g_ref)):
@@ -74,10 +75,11 @@
 
 
 def pack_kernel(
-    pick_hbm, count_ref, ids_hbm, r_ref, k_ref, v_ref, q_ref, g_ref, out_ref, pick_ref, ids_ref, table_sems, sems
+    pick_hbm, count_hbm, ids_hbm, r_ref, k_ref, v_ref, q_ref, g_ref, out_ref,
+    pick_ref, count_ref, ids_ref, table_sems, sems
 ):
     core = lax.rem(lax.axis_index("pat"), 2)
-    tables = fetch_tables(pick_hbm, ids_hbm, pick_ref, ids_ref, table_sems)
+    tables = fetch_tables((pick_hbm, count_hbm, ids_hbm), (pick_ref, count_ref, ids_ref), table_sems)
     source = pl.ds(pl.multiple_of(core * BLK, BLK), BLK)
     copies = []
     for index, ref in enumerate((k_ref, v_ref, q_ref, g_ref)):
@@ -154,7 +156,7 @@
 
 
 def attention_kernel(
-    x_ref, r_ref, o_ref, send_ref, acc, blocks, glob_kv, glob_acc, wmat, kv, sp, gb,
+    x_ref, r_ref, o_ref, send_ref, acc, blocks, glob_kv, glob_acc, wmat, kv, sp, gb, stats,
     long_kv, long_sp, long_gb, meta_v, meta_s, sem
 ):
     half = lax.rem(lax.axis_index("pat"), 2)
@@ -176,12 +178,6 @@
             block // 2, pl.ds(pl.multiple_of(lax.rem(block, 2) * BLK, BLK), BLK), :
         ]
 
-    def fold(value, op):
-        parts = [value[i * 8 : (i + 1) * 8] for i in range(value.shape[0] // 8)]
-        while len(parts) > 1:
-            parts = [op(x, y) for x, y in zip(parts[::2], parts[1::2])] + parts[len(parts) // 2 * 2 :]
-        return parts[0]
-
     def describe(shard, far, masked):
         count = meta_s[shard, SLOTS]
         beside = jnp.where(half == 0, shard - 1, shard + 1)
@@ -198,7 +194,7 @@
         return shard, beside, bias, places
 
     def scores(refs, job):
-        wmat, kv, sp, gb = refs
+        wmat, kv, sp, gb, stats = refs
         shard, beside, bias, places = job
         length = (NEAR + len(places)) * BLK
         wmat[:BLK, :HD] = x_ref[shard, BLK : 2 * BLK, :HD]
@@ -211,38 +207,49 @@
         sp[:length, :] = lax.dot_general(
             kv[:length, :], wmat[...], (((1,), (1,)), ((), ())), preferred_element_type=jnp.float32
         )
-
-    def soften(refs, job):
-        wmat, kv, sp, gb = refs
+        for chunk in range(NEAR + len(places)):
+            rows = slice(chunk * BLK, (chunk + 1) * BLK)
+            soften(refs, bias, chunk, sp[rows, :HD], sp[rows, HD:], False)
+
+    def soften(refs, bias, chunk, logits, weight_grads, keep):
+        wmat, kv, sp, gb, stats = refs
+        rows = slice(chunk * BLK, (chunk + 1) * BLK)
+        logits = logits.reshape(BLK // 8, 8, HD) * (SCALE * LOG2E)
+        weight_grads = weight_grads.reshape(BLK // 8, 8, HD)
+        peak = jnp.max(logits, axis=0)
+        weights = jnp.exp2(logits - peak[None])
+        sp[rows, :HD] = weights.reshape(BLK, HD)
+        if keep:
+            sp[rows, HD:] = weight_grads.reshape(BLK, HD)
+        stats[chunk, 0] = peak + bias[chunk] if chunk in bias else peak
+        stats[chunk, 1] = jnp.sum(weights, axis=0)
+        stats[chunk, 2] = jnp.sum(weights * weight_grads, axis=0)
+
+    def normalise(refs, job):
+        wmat, kv, sp, gb, stats = refs
         shard, beside, bias, places = job
         chunks = NEAR + len(places)
-        peak = None
-        for chunk in range(chunks):
-            high = fold(sp[chunk * BLK : (chunk + 1) * BLK, :HD], jnp.maximum)
-            if chunk in bias:
-                high = high + bias[chunk]
-            peak = high if peak is None else jnp.maximum(peak, high)
-        peak = jnp.max(peak, axis=0, keepdims=True) * (SCALE * LOG2E)
-        peaks = {chunk: peak - bias[chunk] if chunk in bias else peak for chunk in range(chunks)}
-        total = jnp.zeros((8, HD), jnp.float32)
-        delta = jnp.zeros((8, HD), jnp.float32)
+        peak = stats[0, 0]
+        for chunk in range(1, chunks):
+            peak = jnp.maximum(peak, stats[chunk, 0])
+        peak = jnp.max(peak, axis=0, keepdims=True)
+        factors = [jnp.exp2(stats[chunk, 0] - peak) for chunk in range(chunks)]
+        total = sum(factors[chunk] * stats[chunk, 1] for chunk in range(chunks))
+        delta = sum(factors[chunk] * stats[chunk, 2] for chunk in range(chunks))
+        inverse = 1.0 / jnp.sum(total, axis=0, keepdims=True)
+        delta = jnp.sum(delta, axis=0, keepdims=True) * inverse
         for chunk in range(chunks):
             rows = slice(chunk * BLK, (chunk + 1) * BLK)
-            weights = jnp.exp2(sp[rows, :HD] * (SCALE * LOG2E) - peaks[chunk])
-            sp[rows, :HD] = weights
-            total = total + fold(weights, jnp.add)
-            delta = delta + fold(weights * sp[rows, HD:], jnp.add)
-        inverse = 1.0 / jnp.sum(total, axis=0, keepdims=True)
-        delta = jnp.sum(delta, axis=0, keepdims=True) * inverse
-        inverse_scaled = inverse * SCALE
-        for chunk in range(chunks):
-            rows = slice(chunk * BLK, (chunk + 1) * BLK)
-            weights = sp[rows, :HD]
-            gb[rows, HD:] = (weights * inverse).astype(jnp.bfloat16)
-            gb[rows, :HD] = ((weights * inverse_scaled) * (sp[rows, HD:] - delta)).astype(jnp.bfloat16)
+            factor = factors[chunk] * inverse
+            weights = sp[rows, :HD].reshape(BLK // 8, 8, HD)
+            lifted = sp[rows, HD:] - delta
+            gb[rows, HD:] = (weights * factor[None]).reshape(BLK, HD).astype(jnp.bfloat16)
+            gb[rows, :HD] = (
+                (weights * (factor * SCALE)[None]).reshape(BLK, HD) * lifted
+            ).astype(jnp.bfloat16)
 
     def backward(refs, job):
-        wmat, kv, sp, gb = refs
+        wmat, kv, sp, gb, stats = refs
         shard, beside, bias, places = job
         length = (NEAR + len(places)) * BLK
         grad_query = lax.dot_general(
@@ -265,20 +272,20 @@
         place = step * GROUP + u
         return describe(place + jnp.where(place >= busy, 1, 0), LIGHT, True)
 
-    slots = [tuple(ref.at[u] for ref in (wmat, kv, sp, gb)) for u in range(GROUP)]
+    slots = [tuple(ref.at[u] for ref in (wmat, kv, sp, gb, stats)) for u in range(GROUP)]
     steps = (SHARDS - 1) // GROUP
-    long_refs = (wmat.at[GROUP], long_kv, long_sp, long_gb)
+    long_refs = (wmat.at[GROUP], long_kv, long_sp, long_gb, stats.at[GROUP])
     long_job = describe(busy, SLOTS, False)
     scores(long_refs, long_job)
     for u in range(GROUP):
         scores(slots[u], light(0, u))
-    soften(long_refs, long_job)
+    normalise(long_refs, long_job)
     backward(long_refs, long_job)
 
     def light_step(step, carry):
         for u in range(GROUP):
             job = light(step, u)
-            soften(slots[u], job)
+            normalise(slots[u], job)
             backward(slots[u], job)
             scores(slots[u], light(step + 1, u))
         return carry
@@ -286,7 +293,7 @@
     lax.fori_loop(0, steps - 1, light_step, 0)
     for u in range(GROUP):
         job = light(steps - 1, u)
-        soften(slots[u], job)
+        normalise(slots[u], job)
         backward(slots[u], job)
 
     for slot in range(GLOB):
@@ -303,7 +310,6 @@
 
 
 VMEM = pl.BlockSpec(memory_space=pltpu.VMEM)
-SMEM = pl.BlockSpec(memory_space=pltpu.SMEM)
 ANY = pl.BlockSpec(memory_space=pl.ANY)
 
 
@@ -332,6 +338,7 @@
             pltpu.VMEM((GROUP, length, 2 * HD), jnp.bfloat16),
             pltpu.VMEM((GROUP, length, 2 * HD), jnp.float32),
             pltpu.VMEM((GROUP, length, 2 * HD), jnp.bfloat16),
+            pltpu.VMEM((GROUP + 1, NEAR + SLOTS, 3, 8, HD), jnp.float32),
             pltpu.VMEM((longest, 2 * HD), jnp.bfloat16),
             pltpu.VMEM((longest, 2 * HD), jnp.float32),
             pltpu.VMEM((longest, 2 * HD), jnp.bfloat16),
@@ -352,17 +359,18 @@
     tables = (far_pick, far_count, global_ids)
     table_scratch = [
         pltpu.SMEM((1, SLOTS), jnp.int32),
+        pltpu.SMEM((1,), jnp.int32),
         pltpu.SMEM((GLOB,), jnp.int32),
     ]
     away = pl.pallas_call(
         split_kernel,
         out_shape=bf16(4 * BLK + META, width),
-        in_specs=[ANY, SMEM, ANY, ANY, ANY, ANY, ANY],
+        in_specs=[ANY] * 7,
         out_specs=ANY,
         scratch_shapes=table_scratch
         + [
             pltpu.VMEM((4 * BLK + META, width), jnp.bfloat16),
-            pltpu.SemaphoreType.DMA((2,)),
+            pltpu.SemaphoreType.DMA((3,)),
             pltpu.SemaphoreType.DMA((8,)),
             pltpu.SemaphoreType.DMA((9,)),
         ],
@@ -373,10 +381,10 @@
     sent = pl.pallas_call(
         pack_kernel,
         out_shape=bf16(SHARDS, IN_ROWS, 2 * HD),
-        in_specs=[ANY, SMEM, ANY, VMEM, ANY, ANY, ANY, ANY],
+        in_specs=[ANY] * 3 + [VMEM] + [ANY] * 4,
         out_specs=VMEM,
         scratch_shapes=table_scratch
-        + [pltpu.SemaphoreType.DMA((2,)), pltpu.SemaphoreType.DMA((4, HEADS))],
+        + [pltpu.SemaphoreType.DMA((3,)), pltpu.SemaphoreType.DMA((4, HEADS))],
         compiler_params=kernel_params(16),
         name="pack",
     )(*tables, arrived, *arrays)

time: 95.1 us -> 93.7 us (0.985)
  Pallas kernels: 19.8 us -> 18.5 us
    pallas_call x1, Pallas kernels: 14.1 us -> 12.7 us  [attention(): pl.pallas_call(attention_kernel, out_shape=(bf16(SHARDS, OUT_ROWS, 2 * HD...]
where the time goes in v7:
time: 93.7 us; the launch traced here: 93.5 us
  blocking collectives  57.7 us (62%)
  Pallas kernels  18.5 us (20%)
  waiting for transfers between devices  8.1 us (9%)
  starting transfers between devices  7.71 us (8%)
  between operations  1.4 us (1%)
    all_to_all x1, blocking collectives, body(): lax.all_to_all(sent, 'seq', split_axis=0, concat_axis=0, tiled=True)  33.2 us
    all_to_all x1, blocking collectives, body(): lax.all_to_all(combined, 'seq', split_axis=0, concat_axis=0, tiled=True)  24.5 us
    pallas_call x1, Pallas kernels, attention(): pl.pallas_call(attention_kernel, out_shape=(bf16(SHARDS, OUT_ROWS, 2 * HD...  12.7 us
    ppermute x1, starting transfers between devices, body(): arrived = lax.ppermute(away, 'pat', pairs)  3.33 us
    ppermute x1, waiting for transfers between devices, body(): arrived = lax.ppermute(away, 'pat', pairs)  2.54 us
    ppermute x1, waiting for transfers between devices, body(): partial = lax.ppermute(partial, 'pat', pairs)  2.5 us
    ppermute x1, waiting for transfers between devices, body(): other = lax.ppermute(received[:, :BLK, :], 'pat', pairs)  2.29 us
    pallas_call x1, Pallas kernels, body(): pl.pallas_call(split_kernel, out_shape=bf16(4 * BLK + META, width), in_sp...  2.27 us
  transfers between devices with their start and end apart: 4, of which 4 were waited for; matrix products, arithmetic and copies ran while one was open for 0% of the time, Pallas kernels for 1%

profile of v7, /device:TPU:1, one launch (start us, length us, event | category | flops | bytes accessed | tf_op | source)
XLA Modules:
  0.0 93.5 jit_solution(7455488211678029914)
XLA Ops:
  1.3 0.0 copy-start
  1.3 0.0 copy-start.1
  1.3 0.0 copy-start.2
  1.3 0.0 copy-start.3
  1.3 0.0 copy-start.4
  1.3 0.0 copy-start.5
  1.3 2.3 %split.1 = bf16[528,1024]{1,0:T(8,128)(2,1)} custom-call(s32[1,15]{1,0:T(1,128)} %pick_hbm.3, s32[1]{0:T(128)S(6)} %copy.16.count_hbm, s32[2]{0:T(128)} %ids_hbm.3, bf16[256,1024]{1,0:T(8,128)(2,1)} %k_ref.3, bf16[256,1024]{1,0:T(8,128)(2,1)} %v_ref.3, bf16[256,1024]{1,0:T(8,128)(2,1)} %q_ref.3, bf16[256,1024]{1,0:T(8,128)(2,1)} %g_ref.3), custom_call_target="tpu_custom_call" | custom-call | tf_op jit(solution)/shard_map/split/pallas_call | solution.py:365
  3.6 3.3 %collective-permute-start = (bf16[528,1024]{1,0:T(8,128)(2,1)}, bf16[528,1024]{1,0:T(8,128)(2,1)S(1)}, u32[]{:S(2)}, u32[]{:S(2)}) collective-permute-start(bf16[528,1024]{1,0:T(8,128)(2,1)} %split.1), channel_id=1, source_target_pairs={{0,16},{16,0},{32,48},{48,32},{64,80},{80,64},{96,112},{112,96},{1... | collective-permute-start | bytes 3244040 | tf_op jit(solution)/shard_map/ppermute | solution.py:380
  6.9 2.5 %collective-permute-done.r_ref = bf16[528,1024]{1,0:T(8,128)(2,1)S(1)} collective-permute-done((bf16[528,1024]{1,0:T(8,128)(2,1)}, bf16[528,1024]{1,0:T(8,128)(2,1)S(1)}, u32[]{:S(2)}, u32[]{:S(2)}) %collective-permute-start) | collective-permute-done | bytes 1081376 | tf_op jit(solution)/shard_map/ppermute | solution.py:380
  9.5 0.9 %pack.1 = bf16[16,264,256]{2,1,0:T(8,128)(2,1)S(1)} custom-call(s32[1,15]{1,0:T(1,128)S(1)} %copy-done.4, s32[1]{0:T(128)S(6)} %copy.16.count_hbm, s32[2]{0:T(128)S(1)} %copy-done.5, bf16[528,1024]{1,0:T(8,128)(2,1)S(1)} %collective-permute-done.r_ref, bf16[256,1024]{1,0:T(8,128)(2,1)S(1)} %copy-done, bf16[256,1024]{1,0:T(8,128)(2,1)S(1)} %copy-done.1, ...), custom_call_target="tpu_custom_call" | custom-call | tf_op jit(solution)/shard_map/pack/pallas_call | solution.py:381
  10.5 33.2 %all_to_all.10.x_ref = bf16[16,264,256]{2,1,0:T(8,128)(2,1)S(1)} all-to-all(bf16[16,264,256]{2,1,0:T(8,128)(2,1)S(1)} %pack.1), channel_id=1, replica_groups=mesh['pat'=16,'seq'=16] {'seq'}, dimensions={0} | all-to-all | bytes 4325376 | tf_op jit(solution)/shard_map/all_to_all | solution.py:391
  43.6 0.1 slice.4
  43.7 1.8 %collective-permute-start.1 = (bf16[16,128,256]{2,1,0:T(8,128)(2,1)S(1)}, bf16[16,128,256]{2,1,0:T(8,128)(2,1)S(1)}, u32[]{:S(2)}, u32[]{:S(2)}) collective-permute-start(bf16[16,128,256]{2,1,0:T(8,128)(2,1)S(1)} %slice.4), channel_id=1, source_target_pairs={{0,16},{16,0},{32,48},{48,32},{64,80},{80,64},{96,112},{112,96},{1... | collective-permute-start | bytes 3145736 | tf_op jit(solution)/shard_map/ppermute | solution.py:392
  45.5 2.3 %collective-permute-done.1.r_ref = bf16[16,128,256]{2,1,0:T(8,128)(2,1)S(1)} collective-permute-done((bf16[16,128,256]{2,1,0:T(8,128)(2,1)S(1)}, bf16[16,128,256]{2,1,0:T(8,128)(2,1)S(1)}, u32[]{:S(2)}, u32[]{:S(2)}) %collective-permute-start.1) | collective-permute-done | bytes 1048608 | tf_op jit(solution)/shard_map/ppermute | solution.py:392
  47.8 12.7 %attention.1 = (bf16[16,192,256]{2,1,0:T(8,128)(2,1)S(1)}, bf16[16,128,256]{2,1,0:T(8,128)(2,1)}) custom-call(bf16[16,264,256]{2,1,0:T(8,128)(2,1)S(1)} %all_to_all.10.x_ref, bf16[16,128,256]{2,1,0:T(8,128)(2,1)S(1)} %collective-permute-done.1.r_ref), custom_call_target="tpu_custom_call" | custom-call | tf_op jit(solution)/shard_map/attention/pallas_call | solution.py:327
  60.5 0.5 collective-permute-start.2
  61.0 2.5 %collective-permute-done.2.r_ref = bf16[16,128,256]{2,1,0:T(8,128)(2,1)S(1)} collective-permute-done((bf16[16,128,256]{2,1,0:T(8,128)(2,1)}, bf16[16,128,256]{2,1,0:T(8,128)(2,1)S(1)}, u32[]{:S(2)}, u32[]{:S(2)}) %collective-permute-start.2) | collective-permute-done | bytes 1048608 | tf_op jit(solution)/shard_map/ppermute | solution.py:394
  63.5 0.2 combine.1
  63.7 24.5 %all_to_all.11.own_ref = bf16[16,192,256]{2,1,0:T(8,128)(2,1)S(1)} all-to-all(bf16[16,192,256]{2,1,0:T(8,128)(2,1)S(1)} %combine.1), channel_id=1, replica_groups=mesh['pat'=16,'seq'=16] {'seq'}, dimensions={0} | all-to-all | bytes 3145728 | tf_op jit(solution)/shard_map/all_to_all | solution.py:405
  88.3 0.1 constant_dynamic-slice_fusion
  88.3 2.2 %collective-permute-start.3 = (bf16[8,192,256]{2,1,0:T(8,128)(2,1)S(1)}, bf16[8,192,256]{2,1,0:T(8,128)(2,1)S(1)}, u32[]{:S(2)}, u32[]{:S(2)}) collective-permute-start(bf16[8,192,256]{2,1,0:T(8,128)(2,1)S(1)} %constant_dynamic-slice_fusion), channel_id=1, source_target_pairs={{0,16},{16,0},{32,48},{48,32},{64,80},{80,64},{96,112},{112,96},{1... | collective-permute-start | bytes 2359304 | tf_op jit(solution)/shard_map/ppermute | solution.py:407
  90.5 1.1 %own.1 = (bf16[256,1024]{1,0:T(8,128)(2,1)}, bf16[256,1024]{1,0:T(8,128)(2,1)}, bf16[256,1024]{1,0:T(8,128)(2,1)}) custom-call(bf16[16,192,256]{2,1,0:T(8,128)(2,1)S(1)} %all_to_all.11.own_ref), custom_call_target="tpu_custom_call" | custom-call | bytes 3145728 | tf_op jit(solution)/shard_map/own/pallas_call | solution.py:408
  91.6 0.8 collective-permute-done.3.r_ref
  92.4 1.1 %foreign.1 = (bf16[256,1024]{1,0:T(8,128)(2,1)}, bf16[256,1024]{1,0:T(8,128)(2,1)}, bf16[256,1024]{1,0:T(8,128)(2,1)}) custom-call(bf16[8,192,256]{2,1,0:T(8,128)(2,1)S(1)} %collective-permute-done.3.r_ref, bf16[256,1024]{1,0:T(8,128)(2,1)} %get-tuple-element.14.dq_in, ...), custom_call_target="tpu_custom_call", output_to_operand_aliasing={{0}: (1, {}), {1}: (2, {}), {2}: (3, {})} | custom-call | tf_op jit(solution)/shard_map/foreign/pallas_call | solution.py:418
  (6 shorter events, 0.0 us)
Async XLA Ops:
  1.3 8.2 %copy-start = (bf16[256,1024]{1,0:T(8,128)(2,1)S(1)}, bf16[256,1024]{1,0:T(8,128)(2,1)}, u32[]{:S(2)}) copy-start(bf16[256,1024]{1,0:T(8,128)(2,1)} %k_ref.3) | copy-start | bytes 1572868
  1.3 8.2 %copy-start.1 = (bf16[256,1024]{1,0:T(8,128)(2,1)S(1)}, bf16[256,1024]{1,0:T(8,128)(2,1)}, u32[]{:S(2)}) copy-start(bf16[256,1024]{1,0:T(8,128)(2,1)} %v_ref.3) | copy-start | bytes 1572868
  1.3 8.2 %copy-start.2 = (bf16[256,1024]{1,0:T(8,128)(2,1)S(1)}, bf16[256,1024]{1,0:T(8,128)(2,1)}, u32[]{:S(2)}) copy-start(bf16[256,1024]{1,0:T(8,128)(2,1)} %q_ref.3) | copy-start | bytes 1572868
  1.3 8.2 %copy-start.3 = (bf16[256,1024]{1,0:T(8,128)(2,1)S(1)}, bf16[256,1024]{1,0:T(8,128)(2,1)}, u32[]{:S(2)}) copy-start(bf16[256,1024]{1,0:T(8,128)(2,1)} %g_ref.3) | copy-start | bytes 1572868
  1.3 8.2 %copy-start.4 = (s32[1,15]{1,0:T(1,128)S(1)}, s32[1,15]{1,0:T(1,128)}, u32[]{:S(2)}) copy-start(s32[1,15]{1,0:T(1,128)} %pick_hbm.3) | copy-start | bytes 184
  1.3 8.2 %copy-start.5 = (s32[2]{0:T(128)S(1)}, s32[2]{0:T(128)}, u32[]{:S(2)}) copy-start(s32[2]{0:T(128)} %ids_hbm.3) | copy-start | bytes 28
  3.6 5.9 %collective-permute-start = (bf16[528,1024]{1,0:T(8,128)(2,1)}, bf16[528,1024]{1,0:T(8,128)(2,1)S(1)}, u32[]{:S(2)}, u32[]{:S(2)}) collective-permute-start(bf16[528,1024]{1,0:T(8,128)(2,1)} %split.1), channel_id=1, source_target_pairs={{0,16},{16,0},{32,48},{48,32},{64,80},{80,64},{96,112},{112,96},{1... | collective-permute-start | bytes 3244040 | tf_op jit(solution)/shard_map/ppermute | solution.py:380
  43.7 4.0 %collective-permute-start.1 = (bf16[16,128,256]{2,1,0:T(8,128)(2,1)S(1)}, bf16[16,128,256]{2,1,0:T(8,128)(2,1)S(1)}, u32[]{:S(2)}, u32[]{:S(2)}) collective-permute-start(bf16[16,128,256]{2,1,0:T(8,128)(2,1)S(1)} %slice.4), channel_id=1, source_target_pairs={{0,16},{16,0},{32,48},{48,32},{64,80},{80,64},{96,112},{112,96},{1... | collective-permute-start | bytes 3145736 | tf_op jit(solution)/shard_map/ppermute | solution.py:392
  60.5 3.0 %collective-permute-start.2 = (bf16[16,128,256]{2,1,0:T(8,128)(2,1)}, bf16[16,128,256]{2,1,0:T(8,128)(2,1)S(1)}, u32[]{:S(2)}, u32[]{:S(2)}) collective-permute-start(bf16[16,128,256]{2,1,0:T(8,128)(2,1)} %get-tuple-element.11), channel_id=1, source_target_pairs={{0,16},{16,0},{32,48},{48,32},{64,80},{80,64},{96,112},{112,96},{1... | collective-permute-start | bytes 3145736 | tf_op jit(solution)/shard_map/ppermute | solution.py:394
  88.3 4.1 %collective-permute-start.3 = (bf16[8,192,256]{2,1,0:T(8,128)(2,1)S(1)}, bf16[8,192,256]{2,1,0:T(8,128)(2,1)S(1)}, u32[]{:S(2)}, u32[]{:S(2)}) collective-permute-start(bf16[8,192,256]{2,1,0:T(8,128)(2,1)S(1)} %constant_dynamic-slice_fusion), channel_id=1, source_target_pairs={{0,16},{16,0},{32,48},{48,32},{64,80},{80,64},{96,112},{112,96},{1... | collective-permute-start | bytes 2359304 | tf_op jit(solution)/shard_map/ppermute | solution.py:407

commit v8 on v7

--- a/solution.py
+++ b/solution.py
@@ -34,9 +34,9 @@
     return copies
 
 
-def table_rows(pick_ref, count_ref, ids_ref, shape):
+def table_rows(pick_ref, ids_ref, shape):
     lanes = lax.broadcasted_iota(jnp.int32, shape, 1)
-    table = jnp.where(lanes == SLOTS, count_ref[0], 0)
+    table = jnp.zeros(shape, jnp.int32)
     for slot in range(SLOTS):
         table = jnp.where(lanes == slot, pick_ref[0, slot], table)
     for slot in range(GLOB):
@@ -45,11 +45,11 @@
 
 
 def split_kernel(
-    pick_hbm, count_hbm, ids_hbm, k_ref, v_ref, q_ref, g_ref, out_ref,
-    pick_ref, count_ref, ids_ref, held, sems, in_sems, out_sems
+    pick_hbm, ids_hbm, k_ref, v_ref, q_ref, g_ref, out_ref,
+    pick_ref, ids_ref, held, sems, in_sems, out_sems
 ):
     other = 1 - lax.rem(lax.axis_index("pat"), 2)
-    tables = fetch_tables((pick_hbm, count_hbm, ids_hbm), (pick_ref, count_ref, ids_ref), sems)
+    tables = fetch_tables((pick_hbm, ids_hbm), (pick_ref, ids_ref), sems)
     arriving, leaving = [], []
     half = BLK // 2
     for index, ref in enumerate((k_ref, v_ref, q_ref, g_ref)):
@@ -63,7 +63,7 @@
         copy.start()
     for copy in tables:
         copy.wait()
-    held[4 * BLK :, :] = table_rows(pick_ref, count_ref, ids_ref, (META, HEADS * HD))
+    held[4 * BLK :, :] = table_rows(pick_ref, ids_ref, (META, HEADS * HD))
     rows = pl.ds(4 * BLK, META)
     leaving.append(pltpu.make_async_copy(held.at[rows, :], out_ref.at[rows, :], out_sems.at[8]))
     leaving[-1].start()
@@ -75,11 +75,11 @@
 
 
 def pack_kernel(
-    pick_hbm, count_hbm, ids_hbm, r_ref, k_ref, v_ref, q_ref, g_ref, out_ref,
-    pick_ref, count_ref, ids_ref, table_sems, sems
+    pick_hbm, ids_hbm, count_ref, r_ref, k_ref, v_ref, q_ref, g_ref, out_ref,
+    pick_ref, ids_ref, table_sems, sems
 ):
     core = lax.rem(lax.axis_index("pat"), 2)
-    tables = fetch_tables((pick_hbm, count_hbm, ids_hbm), (pick_ref, count_ref, ids_ref), table_sems)
+    tables = fetch_tables((pick_hbm, ids_hbm), (pick_ref, ids_ref), table_sems)
     source = pl.ds(pl.multiple_of(core * BLK, BLK), BLK)
     copies = []
     for index, ref in enumerate((k_ref, v_ref, q_ref, g_ref)):
@@ -98,12 +98,15 @@
         out_ref[away + head, :BLK, HD:] = r_ref[BLK : 2 * BLK, cols]
         out_ref[away + head, BLK : 2 * BLK, :HD] = r_ref[2 * BLK : 3 * BLK, cols]
         out_ref[away + head, BLK : 2 * BLK, HD:] = r_ref[3 * BLK : 4 * BLK, cols]
-        out_ref[away + head, 2 * BLK :, :] = r_ref[4 * BLK : 4 * BLK + TAIL, : 2 * HD]
     for copy in tables:
         copy.wait()
-    table = table_rows(pick_ref, count_ref, ids_ref, (TAIL, 2 * HD))
+    lanes = lax.broadcasted_iota(jnp.int32, (TAIL, 2 * HD), 1)
+    count = jnp.where(lanes == SLOTS, count_ref[0], 0).astype(jnp.float32).astype(jnp.bfloat16)
+    table = table_rows(pick_ref, ids_ref, (TAIL, 2 * HD)) + count
+    far_table = r_ref[4 * BLK : 4 * BLK + TAIL, : 2 * HD] + count
     for head in range(HEADS):
         out_ref[core * HEADS + head, 2 * BLK :, :] = table
+        out_ref[away + head, 2 * BLK :, :] = far_table
     for copy in copies:
         copy.wait()
 
@@ -310,6 +313,7 @@
 
 
 VMEM = pl.BlockSpec(memory_space=pltpu.VMEM)
+SMEM = pl.BlockSpec(memory_space=pltpu.SMEM)
 ANY = pl.BlockSpec(memory_space=pl.ANY)
 
 
@@ -356,21 +360,20 @@
     core = lax.rem(lax.axis_index("pat"), 2)
     arrays = (key_rows, value_rows, query_matrix, output_gradient_rows)
     pairs = [(i, i ^ 1) for i in range(lax.axis_size("pat"))]
-    tables = (far_pick, far_count, global_ids)
+    tables = (far_pick, global_ids)
     table_scratch = [
         pltpu.SMEM((1, SLOTS), jnp.int32),
-        pltpu.SMEM((1,), jnp.int32),
         pltpu.SMEM((GLOB,), jnp.int32),
     ]
     away = pl.pallas_call(
         split_kernel,
         out_shape=bf16(4 * BLK + META, width),
-        in_specs=[ANY] * 7,
+        in_specs=[ANY] * 6,
         out_specs=ANY,
         scratch_shapes=table_scratch
         + [
             pltpu.VMEM((4 * BLK + META, width), jnp.bfloat16),
-            pltpu.SemaphoreType.DMA((3,)),
+            pltpu.SemaphoreType.DMA((2,)),
             pltpu.SemaphoreType.DMA((8,)),
             pltpu.SemaphoreType.DMA((9,)),
         ],
@@ -381,13 +384,13 @@
     sent = pl.pallas_call(
         pack_kernel,
         out_shape=bf16(SHARDS, IN_ROWS, 2 * HD),
-        in_specs=[ANY] * 3 + [VMEM] + [ANY] * 4,
+        in_specs=[ANY, ANY, SMEM, VMEM] + [ANY] * 4,
         out_specs=VMEM,
         scratch_shapes=table_scratch
-        + [pltpu.SemaphoreType.DMA((3,)), pltpu.SemaphoreType.DMA((4, HEADS))],
+        + [pltpu.SemaphoreType.DMA((2,)), pltpu.SemaphoreType.DMA((4, HEADS))],
         compiler_params=kernel_params(16),
         name="pack",
-    )(*tables, arrived, *arrays)
+    )(*tables, far_count, arrived, *arrays)
     received = lax.all_to_all(sent, "seq", split_axis=0, concat_axis=0, tiled=True)
     other = lax.ppermute(received[:, :BLK, :], "pat", pairs)
     own, partial = attention(received, other)

time: 93.7 us -> 93.1 us (level)
  no operation moved by 1% of the time
where the time goes in v8:
time: 93.1 us; the launch traced here: 92.9 us
  blocking collectives  57.7 us (62%)
  Pallas kernels  18.4 us (20%)
  starting transfers between devices  7.72 us (8%)
  waiting for transfers between devices  7.45 us (8%)
  between operations  1.4 us (2%)
    all_to_all x1, blocking collectives, body(): lax.all_to_all(sent, 'seq', split_axis=0, concat_axis=0, tiled=True)  33.2 us
    all_to_all x1, blocking collectives, body(): lax.all_to_all(combined, 'seq', split_axis=0, concat_axis=0, tiled=True)  24.5 us
    pallas_call x1, Pallas kernels, attention(): pl.pallas_call(attention_kernel, out_shape=(bf16(SHARDS, OUT_ROWS, 2 * HD...  12.7 us
    ppermute x1, starting transfers between devices, body(): arrived = lax.ppermute(away, 'pat', pairs)  3.33 us
    ppermute x1, waiting for transfers between devices, body(): partial = lax.ppermute(partial, 'pat', pairs)  2.5 us
    ppermute x1, waiting for transfers between devices, body(): other = lax.ppermute(received[:, :BLK, :], 'pat', pairs)  2.29 us
    pallas_call x1, Pallas kernels, body(): pl.pallas_call(split_kernel, out_shape=bf16(4 * BLK + META, width), in_sp...  2.26 us
    ppermute x1, starting transfers between devices, body(): foreign = lax.ppermute(foreign, 'pat', pairs)  2.18 us
  transfers between devices with their start and end apart: 4, of which 4 were waited for; matrix products, arithmetic and copies ran while one was open for 0% of the time, Pallas kernels for 1%

profile of v8, /device:TPU:1, one launch (start us, length us, event | category | flops | bytes accessed | tf_op | source)
XLA Modules:
  0.0 92.9 jit_solution(10304765762473317092)
XLA Ops:
  0.6 0.0 copy-start.4
  0.6 0.0 copy-start.5
  0.7 0.0 copy-start
  0.7 0.0 copy-start.1
  0.7 0.0 copy-start.2
  0.7 0.0 copy-start.3
  0.7 2.3 %split.1 = bf16[528,1024]{1,0:T(8,128)(2,1)} custom-call(s32[1,15]{1,0:T(1,128)} %pick_hbm.3, s32[2]{0:T(128)} %ids_hbm.3, bf16[256,1024]{1,0:T(8,128)(2,1)} %k_ref.3, bf16[256,1024]{1,0:T(8,128)(2,1)} %v_ref.3, bf16[256,1024]{1,0:T(8,128)(2,1)} %q_ref.3, bf16[256,1024]{1,0:T(8,128)(2,1)} %g_ref.3), custom_call_target="tpu_custom_call" | custom-call | tf_op jit(solution)/shard_map/split/pallas_call | solution.py:368
  3.0 3.3 %collective-permute-start = (bf16[528,1024]{1,0:T(8,128)(2,1)}, bf16[528,1024]{1,0:T(8,128)(2,1)S(1)}, u32[]{:S(2)}, u32[]{:S(2)}) collective-permute-start(bf16[528,1024]{1,0:T(8,128)(2,1)} %split.1), channel_id=1, source_target_pairs={{0,16},{16,0},{32,48},{48,32},{64,80},{80,64},{96,112},{112,96},{1... | collective-permute-start | bytes 3244040 | tf_op jit(solution)/shard_map/ppermute | solution.py:383
  6.9 1.9 %collective-permute-done.r_ref = bf16[528,1024]{1,0:T(8,128)(2,1)S(1)} collective-permute-done((bf16[528,1024]{1,0:T(8,128)(2,1)}, bf16[528,1024]{1,0:T(8,128)(2,1)S(1)}, u32[]{:S(2)}, u32[]{:S(2)}) %collective-permute-start) | collective-permute-done | bytes 1081376 | tf_op jit(solution)/shard_map/ppermute | solution.py:383
  8.9 0.9 pack.1
  9.8 33.2 %all_to_all.10.x_ref = bf16[16,264,256]{2,1,0:T(8,128)(2,1)S(1)} all-to-all(bf16[16,264,256]{2,1,0:T(8,128)(2,1)S(1)} %pack.1), channel_id=1, replica_groups=mesh['pat'=16,'seq'=16] {'seq'}, dimensions={0} | all-to-all | bytes 4325376 | tf_op jit(solution)/shard_map/all_to_all | solution.py:394
  43.0 0.1 slice.4
  43.1 1.8 %collective-permute-start.1 = (bf16[16,128,256]{2,1,0:T(8,128)(2,1)S(1)}, bf16[16,128,256]{2,1,0:T(8,128)(2,1)S(1)}, u32[]{:S(2)}, u32[]{:S(2)}) collective-permute-start(bf16[16,128,256]{2,1,0:T(8,128)(2,1)S(1)} %slice.4), channel_id=1, source_target_pairs={{0,16},{16,0},{32,48},{48,32},{64,80},{80,64},{96,112},{112,96},{1... | collective-permute-start | bytes 3145736 | tf_op jit(solution)/shard_map/ppermute | solution.py:395
  44.8 2.3 %collective-permute-done.1.r_ref = bf16[16,128,256]{2,1,0:T(8,128)(2,1)S(1)} collective-permute-done((bf16[16,128,256]{2,1,0:T(8,128)(2,1)S(1)}, bf16[16,128,256]{2,1,0:T(8,128)(2,1)S(1)}, u32[]{:S(2)}, u32[]{:S(2)}) %collective-permute-start.1) | collective-permute-done | bytes 1048608 | tf_op jit(solution)/shard_map/ppermute | solution.py:395
  47.1 12.7 %attention.1 = (bf16[16,192,256]{2,1,0:T(8,128)(2,1)S(1)}, bf16[16,128,256]{2,1,0:T(8,128)(2,1)}) custom-call(bf16[16,264,256]{2,1,0:T(8,128)(2,1)S(1)} %all_to_all.10.x_ref, bf16[16,128,256]{2,1,0:T(8,128)(2,1)S(1)} %collective-permute-done.1.r_ref), custom_call_target="tpu_custom_call" | custom-call | tf_op jit(solution)/shard_map/attention/pallas_call | solution.py:331
  59.9 0.5 collective-permute-start.2
  60.3 2.5 %collective-permute-done.2.r_ref = bf16[16,128,256]{2,1,0:T(8,128)(2,1)S(1)} collective-permute-done((bf16[16,128,256]{2,1,0:T(8,128)(2,1)}, bf16[16,128,256]{2,1,0:T(8,128)(2,1)S(1)}, u32[]{:S(2)}, u32[]{:S(2)}) %collective-permute-start.2) | collective-permute-done | bytes 1048608 | tf_op jit(solution)/shard_map/ppermute | solution.py:397
  62.8 0.2 combine.1
  63.1 24.5 %all_to_all.11.own_ref = bf16[16,192,256]{2,1,0:T(8,128)(2,1)S(1)} all-to-all(bf16[16,192,256]{2,1,0:T(8,128)(2,1)S(1)} %combine.1), channel_id=1, replica_groups=mesh['pat'=16,'seq'=16] {'seq'}, dimensions={0} | all-to-all | bytes 3145728 | tf_op jit(solution)/shard_map/all_to_all | solution.py:408
  87.6 0.1 constant_dynamic-slice_fusion
  87.6 2.2 %collective-permute-start.3 = (bf16[8,192,256]{2,1,0:T(8,128)(2,1)S(1)}, bf16[8,192,256]{2,1,0:T(8,128)(2,1)S(1)}, u32[]{:S(2)}, u32[]{:S(2)}) collective-permute-start(bf16[8,192,256]{2,1,0:T(8,128)(2,1)S(1)} %constant_dynamic-slice_fusion), channel_id=1, source_target_pairs={{0,16},{16,0},{32,48},{48,32},{64,80},{80,64},{96,112},{112,96},{1... | collective-permute-start | bytes 2359304 | tf_op jit(solution)/shard_map/ppermute | solution.py:410
  89.8 1.1 %own.1 = (bf16[256,1024]{1,0:T(8,128)(2,1)}, bf16[256,1024]{1,0:T(8,128)(2,1)}, bf16[256,1024]{1,0:T(8,128)(2,1)}) custom-call(bf16[16,192,256]{2,1,0:T(8,128)(2,1)S(1)} %all_to_all.11.own_ref), custom_call_target="tpu_custom_call" | custom-call | bytes 3145728 | tf_op jit(solution)/shard_map/own/pallas_call | solution.py:411
  91.0 0.8 collective-permute-done.3.r_ref
  91.7 1.1 %foreign.1 = (bf16[256,1024]{1,0:T(8,128)(2,1)}, bf16[256,1024]{1,0:T(8,128)(2,1)}, bf16[256,1024]{1,0:T(8,128)(2,1)}) custom-call(bf16[8,192,256]{2,1,0:T(8,128)(2,1)S(1)} %collective-permute-done.3.r_ref, bf16[256,1024]{1,0:T(8,128)(2,1)} %get-tuple-element.14.dq_in, ...), custom_call_target="tpu_custom_call", output_to_operand_aliasing={{0}: (1, {}), {1}: (2, {}), {2}: (3, {})} | custom-call | tf_op jit(solution)/shard_map/foreign/pallas_call | solution.py:421
  (6 shorter events, 0.0 us)
Async XLA Ops:
  0.6 8.2 %copy-start.4 = (s32[1,15]{1,0:T(1,128)S(1)}, s32[1,15]{1,0:T(1,128)}, u32[]{:S(2)}) copy-start(s32[1,15]{1,0:T(1,128)} %pick_hbm.3) | copy-start | bytes 184
  0.6 8.2 %copy-start.5 = (s32[2]{0:T(128)S(1)}, s32[2]{0:T(128)}, u32[]{:S(2)}) copy-start(s32[2]{0:T(128)} %ids_hbm.3) | copy-start | bytes 28
  0.7 8.2 %copy-start = (bf16[256,1024]{1,0:T(8,128)(2,1)S(1)}, bf16[256,1024]{1,0:T(8,128)(2,1)}, u32[]{:S(2)}) copy-start(bf16[256,1024]{1,0:T(8,128)(2,1)} %k_ref.3) | copy-start | bytes 1572868
  0.7 8.2 %copy-start.1 = (bf16[256,1024]{1,0:T(8,128)(2,1)S(1)}, bf16[256,1024]{1,0:T(8,128)(2,1)}, u32[]{:S(2)}) copy-start(bf16[256,1024]{1,0:T(8,128)(2,1)} %v_ref.3) | copy-start | bytes 1572868
  0.7 8.2 %copy-start.2 = (bf16[256,1024]{1,0:T(8,128)(2,1)S(1)}, bf16[256,1024]{1,0:T(8,128)(2,1)}, u32[]{:S(2)}) copy-start(bf16[256,1024]{1,0:T(8,128)(2,1)} %q_ref.3) | copy-start | bytes 1572868
  0.7 8.2 %copy-start.3 = (bf16[256,1024]{1,0:T(8,128)(2,1)S(1)}, bf16[256,1024]{1,0:T(8,128)(2,1)}, u32[]{:S(2)}) copy-start(bf16[256,1024]{1,0:T(8,128)(2,1)} %g_ref.3) | copy-start | bytes 1572868
  3.0 5.9 %collective-permute-start = (bf16[528,1024]{1,0:T(8,128)(2,1)}, bf16[528,1024]{1,0:T(8,128)(2,1)S(1)}, u32[]{:S(2)}, u32[]{:S(2)}) collective-permute-start(bf16[528,1024]{1,0:T(8,128)(2,1)} %split.1), channel_id=1, source_target_pairs={{0,16},{16,0},{32,48},{48,32},{64,80},{80,64},{96,112},{112,96},{1... | collective-permute-start | bytes 3244040 | tf_op jit(solution)/shard_map/ppermute | solution.py:383
  43.1 4.0 %collective-permute-start.1 = (bf16[16,128,256]{2,1,0:T(8,128)(2,1)S(1)}, bf16[16,128,256]{2,1,0:T(8,128)(2,1)S(1)}, u32[]{:S(2)}, u32[]{:S(2)}) collective-permute-start(bf16[16,128,256]{2,1,0:T(8,128)(2,1)S(1)} %slice.4), channel_id=1, source_target_pairs={{0,16},{16,0},{32,48},{48,32},{64,80},{80,64},{96,112},{112,96},{1... | collective-permute-start | bytes 3145736 | tf_op jit(solution)/shard_map/ppermute | solution.py:395
  59.9 3.0 %collective-permute-start.2 = (bf16[16,128,256]{2,1,0:T(8,128)(2,1)}, bf16[16,128,256]{2,1,0:T(8,128)(2,1)S(1)}, u32[]{:S(2)}, u32[]{:S(2)}) collective-permute-start(bf16[16,128,256]{2,1,0:T(8,128)(2,1)} %get-tuple-element.11), channel_id=1, source_target_pairs={{0,16},{16,0},{32,48},{48,32},{64,80},{80,64},{96,112},{112,96},{1... | collective-permute-start | bytes 3145736 | tf_op jit(solution)/shard_map/ppermute | solution.py:397
  87.6 4.1 %collective-permute-start.3 = (bf16[8,192,256]{2,1,0:T(8,128)(2,1)S(1)}, bf16[8,192,256]{2,1,0:T(8,128)(2,1)S(1)}, u32[]{:S(2)}, u32[]{:S(2)}) collective-permute-start(bf16[8,192,256]{2,1,0:T(8,128)(2,1)S(1)} %constant_dynamic-slice_fusion), channel_id=1, source_target_pairs={{0,16},{16,0},{32,48},{48,32},{64,80},{80,64},{96,112},{112,96},{1... | collective-permute-start | bytes 2359304 | tf_op jit(solution)/shard_map/ppermute | solution.py:410

commit v9 on v8

--- a/solution.py
+++ b/solution.py
@@ -76,24 +76,18 @@
 
 def pack_kernel(
     pick_hbm, ids_hbm, count_ref, r_ref, k_ref, v_ref, q_ref, g_ref, out_ref,
-    pick_ref, ids_ref, table_sems, sems
+    pick_ref, ids_ref, table_sems
 ):
     core = lax.rem(lax.axis_index("pat"), 2)
     tables = fetch_tables((pick_hbm, ids_hbm), (pick_ref, ids_ref), table_sems)
     source = pl.ds(pl.multiple_of(core * BLK, BLK), BLK)
-    copies = []
-    for index, ref in enumerate((k_ref, v_ref, q_ref, g_ref)):
-        rows = pl.ds(index // 2 * BLK, BLK)
-        lanes = pl.ds(index % 2 * HD, HD)
-        for head in range(HEADS):
-            target = out_ref.at[core * HEADS + head, rows, lanes]
-            origin = ref.at[source, pl.ds(head * HD, HD)]
-            copies.append(pltpu.make_async_copy(origin, target, sems.at[index, head]))
-    for copy in copies:
-        copy.start()
     away = (1 - core) * HEADS
     for head in range(HEADS):
         cols = slice(head * HD, (head + 1) * HD)
+        out_ref[core * HEADS + head, :BLK, :HD] = k_ref[source, cols]
+        out_ref[core * HEADS + head, :BLK, HD:] = v_ref[source, cols]
+        out_ref[core * HEADS + head, BLK : 2 * BLK, :HD] = q_ref[source, cols]
+        out_ref[core * HEADS + head, BLK : 2 * BLK, HD:] = g_ref[source, cols]
         out_ref[away + head, :BLK, :HD] = r_ref[:BLK, cols]
         out_ref[away + head, :BLK, HD:] = r_ref[BLK : 2 * BLK, cols]
         out_ref[away + head, BLK : 2 * BLK, :HD] = r_ref[2 * BLK : 3 * BLK, cols]
@@ -107,8 +101,6 @@
     for head in range(HEADS):
         out_ref[core * HEADS + head, 2 * BLK :, :] = table
         out_ref[away + head, 2 * BLK :, :] = far_table
-    for copy in copies:
-        copy.wait()
 
 
 def combine_kernel(own_ref, r_ref, out_ref):
@@ -118,41 +110,38 @@
         out_ref[shard, BLK:, :] = own_ref[shard, BLK:, :]
 
 
-def place(source, lead, block, outs, sems):
-    copies = []
+def place(source, lead, block, outs, held, sems):
     half = BLK // 2
+    rows = pl.ds(pl.multiple_of(block * BLK, BLK), BLK)
+    copies = [
+        pltpu.make_async_copy(held.at[index], out.at[rows, :], sems.at[index])
+        for index, out in enumerate(outs)
+    ]
     for head in range(HEADS):
-        cols = pl.ds(head * HD, HD)
-        for index, (low, lane, out, row, size) in enumerate(
-            (
-                (0, 0, 1, 0, BLK),
-                (0, HD, 2, 0, BLK),
-                (BLK, 0, 0, 0, half),
-                (BLK, HD, 0, half, half),
-            )
-        ):
-            rows = pl.ds(pl.multiple_of(block * BLK + row, half), size)
-            copies.append(
-                pltpu.make_async_copy(
-                    source.at[lead + head, pl.ds(low, size), pl.ds(lane, HD)],
-                    outs[out].at[rows, cols],
-                    sems.at[index, head],
-                )
-            )
-    for copy in copies:
-        copy.start()
+        cols = slice(head * HD, (head + 1) * HD)
+        held[1, :, cols] = source[lead + head, :BLK, :HD]
+    copies[1].start()
+    for head in range(HEADS):
+        cols = slice(head * HD, (head + 1) * HD)
+        held[2, :, cols] = source[lead + head, :BLK, HD:]
+    copies[2].start()
+    for head in range(HEADS):
+        cols = slice(head * HD, (head + 1) * HD)
+        held[0, :half, cols] = source[lead + head, BLK:, :HD]
+        held[0, half:, cols] = source[lead + head, BLK:, HD:]
+    copies[0].start()
     for copy in copies:
         copy.wait()
 
 
-def own_kernel(own_ref, dq_ref, dk_ref, dv_ref, sems):
+def own_kernel(own_ref, dq_ref, dk_ref, dv_ref, held, sems):
     core = lax.rem(lax.axis_index("pat"), 2)
-    place(own_ref, core * HEADS, core, (dq_ref, dk_ref, dv_ref), sems)
-
-
-def foreign_kernel(r_ref, dq_in, dk_in, dv_in, dq_ref, dk_ref, dv_ref, sems):
+    place(own_ref, core * HEADS, core, (dq_ref, dk_ref, dv_ref), held, sems)
+
+
+def foreign_kernel(r_ref, dq_in, dk_in, dv_in, dq_ref, dk_ref, dv_ref, held, sems):
     core = lax.rem(lax.axis_index("pat"), 2)
-    place(r_ref, 0, 1 - core, (dq_ref, dk_ref, dv_ref), sems)
+    place(r_ref, 0, 1 - core, (dq_ref, dk_ref, dv_ref), held, sems)
 
 
 GROUP = 5
@@ -384,10 +373,10 @@
     sent = pl.pallas_call(
         pack_kernel,
         out_shape=bf16(SHARDS, IN_ROWS, 2 * HD),
-        in_specs=[ANY, ANY, SMEM, VMEM] + [ANY] * 4,
+        in_specs=[ANY, ANY, SMEM] + [VMEM] * 5,
         out_specs=VMEM,
         scratch_shapes=table_scratch
-        + [pltpu.SemaphoreType.DMA((2,)), pltpu.SemaphoreType.DMA((4, HEADS))],
+        + [pltpu.SemaphoreType.DMA((2,))],
         compiler_params=kernel_params(16),
         name="pack",
     )(*tables, far_count, arrived, *arrays)
@@ -413,7 +402,10 @@
         out_shape=(bf16(ROWS, width),) * 3,
         in_specs=[VMEM],
         out_specs=(ANY,) * 3,
-        scratch_shapes=[pltpu.SemaphoreType.DMA((4, HEADS))],
+        scratch_shapes=[
+            pltpu.VMEM((3, BLK, HEADS * HD), jnp.bfloat16),
+            pltpu.SemaphoreType.DMA((3,)),
+        ],
         compiler_params=kernel_params(16),
         cost_estimate=pl.CostEstimate(flops=0, bytes_accessed=3 << 20, transcendentals=0),
         name="own",
@@ -423,7 +415,10 @@
         out_shape=(bf16(ROWS, width),) * 3,
         in_specs=[VMEM, ANY, ANY, ANY],
         out_specs=(ANY,) * 3,
-        scratch_shapes=[pltpu.SemaphoreType.DMA((4, HEADS))],
+        scratch_shapes=[
+            pltpu.VMEM((3, BLK, HEADS * HD), jnp.bfloat16),
+            pltpu.SemaphoreType.DMA((3,)),
+        ],
         input_output_aliases={1: 0, 2: 1, 3: 2},
         compiler_params=kernel_params(16),
         name="foreign",

time: 93.1 us -> 92.7 us (level)
  no operation moved by 1% of the time
where the time goes in v9:
time: 92.7 us; the launch traced here: 92.5 us
  blocking collectives  57.7 us (62%)
  Pallas kernels  17.9 us (19%)
  starting transfers between devices  7.72 us (8%)
  waiting for transfers between devices  7.61 us (8%)
  between operations  1.4 us (2%)
    all_to_all x1, blocking collectives, body(): lax.all_to_all(sent, 'seq', split_axis=0, concat_axis=0, tiled=True)  33.2 us
    all_to_all x1, blocking collectives, body(): lax.all_to_all(combined, 'seq', split_axis=0, concat_axis=0, tiled=True)  24.5 us
    pallas_call x1, Pallas kernels, attention(): pl.pallas_call(attention_kernel, out_shape=(bf16(SHARDS, OUT_ROWS, 2 * HD...  12.7 us
    ppermute x1, starting transfers between devices, body(): arrived = lax.ppermute(away, 'pat', pairs)  3.33 us
    ppermute x1, waiting for transfers between devices, body(): partial = lax.ppermute(partial, 'pat', pairs)  2.5 us
    ppermute x1, waiting for transfers between devices, body(): other = lax.ppermute(received[:, :BLK, :], 'pat', pairs)  2.29 us
    pallas_call x1, Pallas kernels, body(): pl.pallas_call(split_kernel, out_shape=bf16(4 * BLK + META, width), in_sp...  2.26 us
    ppermute x1, starting transfers between devices, body(): foreign = lax.ppermute(foreign, 'pat', pairs)  2.18 us
  transfers between devices with their start and end apart: 4, of which 4 were waited for; matrix products, arithmetic and copies ran while one was open for 0% of the time, Pallas kernels for 1%

profile of v9, /device:TPU:1, one launch (start us, length us, event | category | flops | bytes accessed | tf_op | source)
XLA Modules:
  0.0 92.5 jit_solution(17478054598503389671)
XLA Ops:
  0.6 0.0 copy-start.4
  0.6 0.0 copy-start.5
  0.7 0.0 copy-start
  0.7 0.0 copy-start.1
  0.7 0.0 copy-start.2
  0.7 0.0 copy-start.3
  0.7 2.3 %split.1 = bf16[528,1024]{1,0:T(8,128)(2,1)} custom-call(s32[1,15]{1,0:T(1,128)} %pick_hbm.3, s32[2]{0:T(128)} %ids_hbm.3, bf16[256,1024]{1,0:T(8,128)(2,1)} %k_ref.3, bf16[256,1024]{1,0:T(8,128)(2,1)} %v_ref.3, bf16[256,1024]{1,0:T(8,128)(2,1)} %q_ref.3, bf16[256,1024]{1,0:T(8,128)(2,1)} %g_ref.3), custom_call_target="tpu_custom_call" | custom-call | tf_op jit(solution)/shard_map/split/pallas_call | solution.py:357
  3.0 3.3 %collective-permute-start = (bf16[528,1024]{1,0:T(8,128)(2,1)}, bf16[528,1024]{1,0:T(8,128)(2,1)S(1)}, u32[]{:S(2)}, u32[]{:S(2)}) collective-permute-start(bf16[528,1024]{1,0:T(8,128)(2,1)} %split.1), channel_id=1, source_target_pairs={{0,16},{16,0},{32,48},{48,32},{64,80},{80,64},{96,112},{112,96},{1... | collective-permute-start | bytes 3244040 | tf_op jit(solution)/shard_map/ppermute | solution.py:372
  6.9 1.9 %collective-permute-done.r_ref = bf16[528,1024]{1,0:T(8,128)(2,1)S(1)} collective-permute-done((bf16[528,1024]{1,0:T(8,128)(2,1)}, bf16[528,1024]{1,0:T(8,128)(2,1)S(1)}, u32[]{:S(2)}, u32[]{:S(2)}) %collective-permute-start) | collective-permute-done | bytes 1081376 | tf_op jit(solution)/shard_map/ppermute | solution.py:372
  8.9 0.8 pack.1
  9.6 33.2 %all_to_all.10.x_ref = bf16[16,264,256]{2,1,0:T(8,128)(2,1)S(1)} all-to-all(bf16[16,264,256]{2,1,0:T(8,128)(2,1)S(1)} %pack.1), channel_id=1, replica_groups=mesh['pat'=16,'seq'=16] {'seq'}, dimensions={0} | all-to-all | bytes 4325376 | tf_op jit(solution)/shard_map/all_to_all | solution.py:383
  42.8 0.1 slice.4
  42.9 1.8 %collective-permute-start.1 = (bf16[16,128,256]{2,1,0:T(8,128)(2,1)S(1)}, bf16[16,128,256]{2,1,0:T(8,128)(2,1)S(1)}, u32[]{:S(2)}, u32[]{:S(2)}) collective-permute-start(bf16[16,128,256]{2,1,0:T(8,128)(2,1)S(1)} %slice.4), channel_id=1, source_target_pairs={{0,16},{16,0},{32,48},{48,32},{64,80},{80,64},{96,112},{112,96},{1... | collective-permute-start | bytes 3145736 | tf_op jit(solution)/shard_map/ppermute | solution.py:384
  44.7 2.3 %collective-permute-done.1.r_ref = bf16[16,128,256]{2,1,0:T(8,128)(2,1)S(1)} collective-permute-done((bf16[16,128,256]{2,1,0:T(8,128)(2,1)S(1)}, bf16[16,128,256]{2,1,0:T(8,128)(2,1)S(1)}, u32[]{:S(2)}, u32[]{:S(2)}) %collective-permute-start.1) | collective-permute-done | bytes 1048608 | tf_op jit(solution)/shard_map/ppermute | solution.py:384
  47.0 12.7 %attention.1 = (bf16[16,192,256]{2,1,0:T(8,128)(2,1)S(1)}, bf16[16,128,256]{2,1,0:T(8,128)(2,1)}) custom-call(bf16[16,264,256]{2,1,0:T(8,128)(2,1)S(1)} %all_to_all.10.x_ref, bf16[16,128,256]{2,1,0:T(8,128)(2,1)S(1)} %collective-permute-done.1.r_ref), custom_call_target="tpu_custom_call" | custom-call | tf_op jit(solution)/shard_map/attention/pallas_call | solution.py:320
  59.7 0.5 collective-permute-start.2
  60.1 2.5 %collective-permute-done.2.r_ref = bf16[16,128,256]{2,1,0:T(8,128)(2,1)S(1)} collective-permute-done((bf16[16,128,256]{2,1,0:T(8,128)(2,1)}, bf16[16,128,256]{2,1,0:T(8,128)(2,1)S(1)}, u32[]{:S(2)}, u32[]{:S(2)}) %collective-permute-start.2) | collective-permute-done | bytes 1048608 | tf_op jit(solution)/shard_map/ppermute | solution.py:386
  62.6 0.2 combine.1
  62.9 24.5 %all_to_all.11.own_ref = bf16[16,192,256]{2,1,0:T(8,128)(2,1)S(1)} all-to-all(bf16[16,192,256]{2,1,0:T(8,128)(2,1)S(1)} %combine.1), channel_id=1, replica_groups=mesh['pat'=16,'seq'=16] {'seq'}, dimensions={0} | all-to-all | bytes 3145728 | tf_op jit(solution)/shard_map/all_to_all | solution.py:397
  87.4 0.1 constant_dynamic-slice_fusion
  87.5 2.2 %collective-permute-start.3 = (bf16[8,192,256]{2,1,0:T(8,128)(2,1)S(1)}, bf16[8,192,256]{2,1,0:T(8,128)(2,1)S(1)}, u32[]{:S(2)}, u32[]{:S(2)}) collective-permute-start(bf16[8,192,256]{2,1,0:T(8,128)(2,1)S(1)} %constant_dynamic-slice_fusion), channel_id=1, source_target_pairs={{0,16},{16,0},{32,48},{48,32},{64,80},{80,64},{96,112},{112,96},{1... | collective-permute-start | bytes 2359304 | tf_op jit(solution)/shard_map/ppermute | solution.py:399
  89.6 1.0 %own.1 = (bf16[256,1024]{1,0:T(8,128)(2,1)}, bf16[256,1024]{1,0:T(8,128)(2,1)}, bf16[256,1024]{1,0:T(8,128)(2,1)}) custom-call(bf16[16,192,256]{2,1,0:T(8,128)(2,1)S(1)} %all_to_all.11.own_ref), custom_call_target="tpu_custom_call" | custom-call | bytes 3145728 | tf_op jit(solution)/shard_map/own/pallas_call | solution.py:400
  90.6 0.9 %collective-permute-done.3.r_ref = bf16[8,192,256]{2,1,0:T(8,128)(2,1)S(1)} collective-permute-done((bf16[8,192,256]{2,1,0:T(8,128)(2,1)S(1)}, bf16[8,192,256]{2,1,0:T(8,128)(2,1)S(1)}, u32[]{:S(2)}, u32[]{:S(2)}) %collective-permute-start.3) | collective-permute-done | bytes 786464 | tf_op jit(solution)/shard_map/ppermute | solution.py:399
  91.6 1.0 %foreign.1 = (bf16[256,1024]{1,0:T(8,128)(2,1)}, bf16[256,1024]{1,0:T(8,128)(2,1)}, bf16[256,1024]{1,0:T(8,128)(2,1)}) custom-call(bf16[8,192,256]{2,1,0:T(8,128)(2,1)S(1)} %collective-permute-done.3.r_ref, bf16[256,1024]{1,0:T(8,128)(2,1)} %get-tuple-element.14.dq_in, ...), custom_call_target="tpu_custom_call", output_to_operand_aliasing={{0}: (1, {}), {1}: (2, {}), {2}: (3, {})} | custom-call | tf_op jit(solution)/shard_map/foreign/pallas_call | solution.py:413
  (6 shorter events, 0.0 us)
Async XLA Ops:
  0.6 8.2 %copy-start.4 = (s32[1,15]{1,0:T(1,128)S(1)}, s32[1,15]{1,0:T(1,128)}, u32[]{:S(2)}) copy-start(s32[1,15]{1,0:T(1,128)} %pick_hbm.3) | copy-start | bytes 184
  0.6 8.2 %copy-start.5 = (s32[2]{0:T(128)S(1)}, s32[2]{0:T(128)}, u32[]{:S(2)}) copy-start(s32[2]{0:T(128)} %ids_hbm.3) | copy-start | bytes 28
  0.7 8.2 %copy-start = (bf16[256,1024]{1,0:T(8,128)(2,1)S(1)}, bf16[256,1024]{1,0:T(8,128)(2,1)}, u32[]{:S(2)}) copy-start(bf16[256,1024]{1,0:T(8,128)(2,1)} %k_ref.3) | copy-start | bytes 1572868
  0.7 8.2 %copy-start.1 = (bf16[256,1024]{1,0:T(8,128)(2,1)S(1)}, bf16[256,1024]{1,0:T(8,128)(2,1)}, u32[]{:S(2)}) copy-start(bf16[256,1024]{1,0:T(8,128)(2,1)} %v_ref.3) | copy-start | bytes 1572868
  0.7 8.2 %copy-start.2 = (bf16[256,1024]{1,0:T(8,128)(2,1)S(1)}, bf16[256,1024]{1,0:T(8,128)(2,1)}, u32[]{:S(2)}) copy-start(bf16[256,1024]{1,0:T(8,128)(2,1)} %q_ref.3) | copy-start | bytes 1572868
  0.7 8.2 %copy-start.3 = (bf16[256,1024]{1,0:T(8,128)(2,1)S(1)}, bf16[256,1024]{1,0:T(8,128)(2,1)}, u32[]{:S(2)}) copy-start(bf16[256,1024]{1,0:T(8,128)(2,1)} %g_ref.3) | copy-start | bytes 1572868
  3.0 5.9 %collective-permute-start = (bf16[528,1024]{1,0:T(8,128)(2,1)}, bf16[528,1024]{1,0:T(8,128)(2,1)S(1)}, u32[]{:S(2)}, u32[]{:S(2)}) collective-permute-start(bf16[528,1024]{1,0:T(8,128)(2,1)} %split.1), channel_id=1, source_target_pairs={{0,16},{16,0},{32,48},{48,32},{64,80},{80,64},{96,112},{112,96},{1... | collective-permute-start | bytes 3244040 | tf_op jit(solution)/shard_map/ppermute | solution.py:372
  42.9 4.0 %collective-permute-start.1 = (bf16[16,128,256]{2,1,0:T(8,128)(2,1)S(1)}, bf16[16,128,256]{2,1,0:T(8,128)(2,1)S(1)}, u32[]{:S(2)}, u32[]{:S(2)}) collective-permute-start(bf16[16,128,256]{2,1,0:T(8,128)(2,1)S(1)} %slice.4), channel_id=1, source_target_pairs={{0,16},{16,0},{32,48},{48,32},{64,80},{80,64},{96,112},{112,96},{1... | collective-permute-start | bytes 3145736 | tf_op jit(solution)/shard_map/ppermute | solution.py:384
  59.7 3.0 %collective-permute-start.2 = (bf16[16,128,256]{2,1,0:T(8,128)(2,1)}, bf16[16,128,256]{2,1,0:T(8,128)(2,1)S(1)}, u32[]{:S(2)}, u32[]{:S(2)}) collective-permute-start(bf16[16,128,256]{2,1,0:T(8,128)(2,1)} %get-tuple-element.11), channel_id=1, source_target_pairs={{0,16},{16,0},{32,48},{48,32},{64,80},{80,64},{96,112},{112,96},{1... | collective-permute-start | bytes 3145736 | tf_op jit(solution)/shard_map/ppermute | solution.py:386
  87.5 4.1 %collective-permute-start.3 = (bf16[8,192,256]{2,1,0:T(8,128)(2,1)S(1)}, bf16[8,192,256]{2,1,0:T(8,128)(2,1)S(1)}, u32[]{:S(2)}, u32[]{:S(2)}) collective-permute-start(bf16[8,192,256]{2,1,0:T(8,128)(2,1)S(1)} %constant_dynamic-slice_fusion), channel_id=1, source_target_pairs={{0,16},{16,0},{32,48},{48,32},{64,80},{80,64},{96,112},{112,96},{1... | collective-permute-start | bytes 2359304 | tf_op jit(solution)/shard_map/ppermute | solution.py:399

commit v10 on v9

--- a/solution.py
+++ b/solution.py
@@ -15,7 +15,7 @@
 LIGHT = 4
 ROWS = 2 * BLK
 META = 16
-TAIL = 8
+TAIL = 16
 IN_ROWS = 2 * BLK + TAIL
 OUT_ROWS = BLK + BLK // 2
 SCALE = HD**-0.5

time: 92.7 us -> 93.4 us (level)
  no operation moved by 1% of the time
where the time goes in v10:
time: 93.4 us; the launch traced here: 93.2 us
  blocking collectives  58.3 us (62%)
  Pallas kernels  17.9 us (19%)
  starting transfers between devices  7.79 us (8%)
  waiting for transfers between devices  7.61 us (8%)
  between operations  1.4 us (1%)
    all_to_all x1, blocking collectives, body(): lax.all_to_all(sent, 'seq', split_axis=0, concat_axis=0, tiled=True)  33.6 us
    all_to_all x1, blocking collectives, body(): lax.all_to_all(combined, 'seq', split_axis=0, concat_axis=0, tiled=True)  24.7 us
    pallas_call x1, Pallas kernels, attention(): pl.pallas_call(attention_kernel, out_shape=(bf16(SHARDS, OUT_ROWS, 2 * HD...  12.7 us
    ppermute x1, starting transfers between devices, body(): arrived = lax.ppermute(away, 'pat', pairs)  3.33 us
    ppermute x1, waiting for transfers between devices, body(): partial = lax.ppermute(partial, 'pat', pairs)  2.5 us
    ppermute x1, waiting for transfers between devices, body(): other = lax.ppermute(received[:, :BLK, :], 'pat', pairs)  2.29 us
    pallas_call x1, Pallas kernels, body(): pl.pallas_call(split_kernel, out_shape=bf16(4 * BLK + META, width), in_sp...  2.26 us
    ppermute x1, starting transfers between devices, body(): foreign = lax.ppermute(foreign, 'pat', pairs)  2.18 us
  transfers between devices with their start and end apart: 4, of which 4 were waited for; matrix products, arithmetic and copies ran while one was open for 0% of the time, Pallas kernels for 1%

profile of v10, /device:TPU:1, one launch (start us, length us, event | category | flops | bytes accessed | tf_op | source)
XLA Modules:
  0.0 93.2 jit_solution(14448511815653932701)
XLA Ops:
  0.6 0.0 copy-start.4
  0.6 0.0 copy-start.5
  0.7 0.0 copy-start
  0.7 0.0 copy-start.1
  0.7 0.0 copy-start.2
  0.7 0.0 copy-start.3
  0.7 2.3 %split.1 = bf16[528,1024]{1,0:T(8,128)(2,1)} custom-call(s32[1,15]{1,0:T(1,128)} %pick_hbm.3, s32[2]{0:T(128)} %ids_hbm.3, bf16[256,1024]{1,0:T(8,128)(2,1)} %k_ref.3, bf16[256,1024]{1,0:T(8,128)(2,1)} %v_ref.3, bf16[256,1024]{1,0:T(8,128)(2,1)} %q_ref.3, bf16[256,1024]{1,0:T(8,128)(2,1)} %g_ref.3), custom_call_target="tpu_custom_call" | custom-call | tf_op jit(solution)/shard_map/split/pallas_call | solution.py:357
  3.0 3.3 %collective-permute-start = (bf16[528,1024]{1,0:T(8,128)(2,1)}, bf16[528,1024]{1,0:T(8,128)(2,1)S(1)}, u32[]{:S(2)}, u32[]{:S(2)}) collective-permute-start(bf16[528,1024]{1,0:T(8,128)(2,1)} %split.1), channel_id=1, source_target_pairs={{0,16},{16,0},{32,48},{48,32},{64,80},{80,64},{96,112},{112,96},{1... | collective-permute-start | bytes 3244040 | tf_op jit(solution)/shard_map/ppermute | solution.py:372
  6.9 1.9 %collective-permute-done.r_ref = bf16[528,1024]{1,0:T(8,128)(2,1)S(1)} collective-permute-done((bf16[528,1024]{1,0:T(8,128)(2,1)}, bf16[528,1024]{1,0:T(8,128)(2,1)S(1)}, u32[]{:S(2)}, u32[]{:S(2)}) %collective-permute-start) | collective-permute-done | bytes 1081376 | tf_op jit(solution)/shard_map/ppermute | solution.py:372
  8.9 0.8 pack.1
  9.6 33.6 %all_to_all.10.x_ref = bf16[16,272,256]{2,1,0:T(8,128)(2,1)S(1)} all-to-all(bf16[16,272,256]{2,1,0:T(8,128)(2,1)S(1)} %pack.1), channel_id=1, replica_groups=mesh['pat'=16,'seq'=16] {'seq'}, dimensions={0} | all-to-all | bytes 4456448 | tf_op jit(solution)/shard_map/all_to_all | solution.py:383
  43.3 0.1 slice.4
  43.4 1.8 %collective-permute-start.1 = (bf16[16,128,256]{2,1,0:T(8,128)(2,1)S(1)}, bf16[16,128,256]{2,1,0:T(8,128)(2,1)S(1)}, u32[]{:S(2)}, u32[]{:S(2)}) collective-permute-start(bf16[16,128,256]{2,1,0:T(8,128)(2,1)S(1)} %slice.4), channel_id=1, source_target_pairs={{0,16},{16,0},{32,48},{48,32},{64,80},{80,64},{96,112},{112,96},{1... | collective-permute-start | bytes 3145736 | tf_op jit(solution)/shard_map/ppermute | solution.py:384
  45.2 2.3 %collective-permute-done.1.r_ref = bf16[16,128,256]{2,1,0:T(8,128)(2,1)S(1)} collective-permute-done((bf16[16,128,256]{2,1,0:T(8,128)(2,1)S(1)}, bf16[16,128,256]{2,1,0:T(8,128)(2,1)S(1)}, u32[]{:S(2)}, u32[]{:S(2)}) %collective-permute-start.1) | collective-permute-done | bytes 1048608 | tf_op jit(solution)/shard_map/ppermute | solution.py:384
  47.5 12.7 %attention.1 = (bf16[16,192,256]{2,1,0:T(8,128)(2,1)S(1)}, bf16[16,128,256]{2,1,0:T(8,128)(2,1)}) custom-call(bf16[16,272,256]{2,1,0:T(8,128)(2,1)S(1)} %all_to_all.10.x_ref, bf16[16,128,256]{2,1,0:T(8,128)(2,1)S(1)} %collective-permute-done.1.r_ref), custom_call_target="tpu_custom_call" | custom-call | tf_op jit(solution)/shard_map/attention/pallas_call | solution.py:320
  60.2 0.5 collective-permute-start.2
  60.7 2.5 %collective-permute-done.2.r_ref = bf16[16,128,256]{2,1,0:T(8,128)(2,1)S(1)} collective-permute-done((bf16[16,128,256]{2,1,0:T(8,128)(2,1)}, bf16[16,128,256]{2,1,0:T(8,128)(2,1)S(1)}, u32[]{:S(2)}, u32[]{:S(2)}) %collective-permute-start.2) | collective-permute-done | bytes 1048608 | tf_op jit(solution)/shard_map/ppermute | solution.py:386
  63.2 0.2 combine.1
  63.4 24.7 %all_to_all.11.own_ref = bf16[16,192,256]{2,1,0:T(8,128)(2,1)S(1)} all-to-all(bf16[16,192,256]{2,1,0:T(8,128)(2,1)S(1)} %combine.1), channel_id=1, replica_groups=mesh['pat'=16,'seq'=16] {'seq'}, dimensions={0} | all-to-all | bytes 3145728 | tf_op jit(solution)/shard_map/all_to_all | solution.py:397
  88.1 0.1 constant_dynamic-slice_fusion
  88.2 2.2 %collective-permute-start.3 = (bf16[8,192,256]{2,1,0:T(8,128)(2,1)S(1)}, bf16[8,192,256]{2,1,0:T(8,128)(2,1)S(1)}, u32[]{:S(2)}, u32[]{:S(2)}) collective-permute-start(bf16[8,192,256]{2,1,0:T(8,128)(2,1)S(1)} %constant_dynamic-slice_fusion), channel_id=1, source_target_pairs={{0,16},{16,0},{32,48},{48,32},{64,80},{80,64},{96,112},{112,96},{1... | collective-permute-start | bytes 2359304 | tf_op jit(solution)/shard_map/ppermute | solution.py:399
  90.3 1.0 %own.1 = (bf16[256,1024]{1,0:T(8,128)(2,1)}, bf16[256,1024]{1,0:T(8,128)(2,1)}, bf16[256,1024]{1,0:T(8,128)(2,1)}) custom-call(bf16[16,192,256]{2,1,0:T(8,128)(2,1)S(1)} %all_to_all.11.own_ref), custom_call_target="tpu_custom_call" | custom-call | bytes 3145728 | tf_op jit(solution)/shard_map/own/pallas_call | solution.py:400
  91.3 0.9 %collective-permute-done.3.r_ref = bf16[8,192,256]{2,1,0:T(8,128)(2,1)S(1)} collective-permute-done((bf16[8,192,256]{2,1,0:T(8,128)(2,1)S(1)}, bf16[8,192,256]{2,1,0:T(8,128)(2,1)S(1)}, u32[]{:S(2)}, u32[]{:S(2)}) %collective-permute-start.3) | collective-permute-done | bytes 786464 | tf_op jit(solution)/shard_map/ppermute | solution.py:399
  92.3 1.0 %foreign.1 = (bf16[256,1024]{1,0:T(8,128)(2,1)}, bf16[256,1024]{1,0:T(8,128)(2,1)}, bf16[256,1024]{1,0:T(8,128)(2,1)}) custom-call(bf16[8,192,256]{2,1,0:T(8,128)(2,1)S(1)} %collective-permute-done.3.r_ref, bf16[256,1024]{1,0:T(8,128)(2,1)} %get-tuple-element.14.dq_in, ...), custom_call_target="tpu_custom_call", output_to_operand_aliasing={{0}: (1, {}), {1}: (2, {}), {2}: (3, {})} | custom-call | tf_op jit(solution)/shard_map/foreign/pallas_call | solution.py:413
  (6 shorter events, 0.0 us)
Async XLA Ops:
  0.6 8.2 %copy-start.4 = (s32[1,15]{1,0:T(1,128)S(1)}, s32[1,15]{1,0:T(1,128)}, u32[]{:S(2)}) copy-start(s32[1,15]{1,0:T(1,128)} %pick_hbm.3) | copy-start | bytes 184
  0.6 8.2 %copy-start.5 = (s32[2]{0:T(128)S(1)}, s32[2]{0:T(128)}, u32[]{:S(2)}) copy-start(s32[2]{0:T(128)} %ids_hbm.3) | copy-start | bytes 28
  0.7 8.2 %copy-start = (bf16[256,1024]{1,0:T(8,128)(2,1)S(1)}, bf16[256,1024]{1,0:T(8,128)(2,1)}, u32[]{:S(2)}) copy-start(bf16[256,1024]{1,0:T(8,128)(2,1)} %k_ref.3) | copy-start | bytes 1572868
  0.7 8.2 %copy-start.1 = (bf16[256,1024]{1,0:T(8,128)(2,1)S(1)}, bf16[256,1024]{1,0:T(8,128)(2,1)}, u32[]{:S(2)}) copy-start(bf16[256,1024]{1,0:T(8,128)(2,1)} %v_ref.3) | copy-start | bytes 1572868
  0.7 8.2 %copy-start.2 = (bf16[256,1024]{1,0:T(8,128)(2,1)S(1)}, bf16[256,1024]{1,0:T(8,128)(2,1)}, u32[]{:S(2)}) copy-start(bf16[256,1024]{1,0:T(8,128)(2,1)} %q_ref.3) | copy-start | bytes 1572868
  0.7 8.2 %copy-start.3 = (bf16[256,1024]{1,0:T(8,128)(2,1)S(1)}, bf16[256,1024]{1,0:T(8,128)(2,1)}, u32[]{:S(2)}) copy-start(bf16[256,1024]{1,0:T(8,128)(2,1)} %g_ref.3) | copy-start | bytes 1572868
  3.0 5.9 %collective-permute-start = (bf16[528,1024]{1,0:T(8,128)(2,1)}, bf16[528,1024]{1,0:T(8,128)(2,1)S(1)}, u32[]{:S(2)}, u32[]{:S(2)}) collective-permute-start(bf16[528,1024]{1,0:T(8,128)(2,1)} %split.1), channel_id=1, source_target_pairs={{0,16},{16,0},{32,48},{48,32},{64,80},{80,64},{96,112},{112,96},{1... | collective-permute-start | bytes 3244040 | tf_op jit(solution)/shard_map/ppermute | solution.py:372
  43.4 4.1 %collective-permute-start.1 = (bf16[16,128,256]{2,1,0:T(8,128)(2,1)S(1)}, bf16[16,128,256]{2,1,0:T(8,128)(2,1)S(1)}, u32[]{:S(2)}, u32[]{:S(2)}) collective-permute-start(bf16[16,128,256]{2,1,0:T(8,128)(2,1)S(1)} %slice.4), channel_id=1, source_target_pairs={{0,16},{16,0},{32,48},{48,32},{64,80},{80,64},{96,112},{112,96},{1... | collective-permute-start | bytes 3145736 | tf_op jit(solution)/shard_map/ppermute | solution.py:384
  60.2 3.0 %collective-permute-start.2 = (bf16[16,128,256]{2,1,0:T(8,128)(2,1)}, bf16[16,128,256]{2,1,0:T(8,128)(2,1)S(1)}, u32[]{:S(2)}, u32[]{:S(2)}) collective-permute-start(bf16[16,128,256]{2,1,0:T(8,128)(2,1)} %get-tuple-element.11), channel_id=1, source_target_pairs={{0,16},{16,0},{32,48},{48,32},{64,80},{80,64},{96,112},{112,96},{1... | collective-permute-start | bytes 3145736 | tf_op jit(solution)/shard_map/ppermute | solution.py:386
  88.2 4.1 %collective-permute-start.3 = (bf16[8,192,256]{2,1,0:T(8,128)(2,1)S(1)}, bf16[8,192,256]{2,1,0:T(8,128)(2,1)S(1)}, u32[]{:S(2)}, u32[]{:S(2)}) collective-permute-start(bf16[8,192,256]{2,1,0:T(8,128)(2,1)S(1)} %constant_dynamic-slice_fusion), channel_id=1, source_target_pairs={{0,16},{16,0},{32,48},{48,32},{64,80},{80,64},{96,112},{112,96},{1... | collective-permute-start | bytes 2359304 | tf_op jit(solution)/shard_map/ppermute | solution.py:399
